TPU v7x, 256 devices: a whole 4x4x8 slice. The times are simulated.
256 devices in a mesh: half: 2 (over z_lo), row: 8 (over z_hi, core), col: 16 (over y, x).
Axes of the slice: x: 4, y: 4, z: 8 (z_hi: 4, z_lo: 2; z = z_hi * 2 + z_lo), core: 2. Of those that a mesh axis runs over, the one named last changes fastest.
Arguments:
- root_factor: bfloat16 [3, 16, 128, 3, 16, 128], P(None, ('half', 'row'), None, None, 'col')
- root_pivots: float32 [3, 16, 128], P(None, ('half', 'row')), may hold values from -2 to 2
- child_factor: bfloat16 [2, 4, 8, 128, 2, 16, 128], P('half', None, 'row', None, None, 'col')
- child_pivots: float32 [2, 4, 8, 128], P('half', None, 'row'), may hold values from -2 to 2
- child_block: bfloat16 [2, 6, 8, 64, 2, 16, 128], P('half', None, 'row', None, None, 'col'), may hold values from -0.109375 to 0.109375
- child_rows: int32 [2, 3072], P('half'), may hold values from 0 to 6143, as said below
Outputs:
- root_inverse: float32 [6, 8, 128, 3, 16, 128], P(None, 'row', None, None, 'col')
- child_offdiag: float32 [2, 6, 8, 64, 2, 16, 128], P('half', None, 'row', None, None, 'col')
- child_inverse: float32 [2, 4, 8, 128, 2, 16, 128], P('half', None, 'row', None, None, 'col')
Inputs may be any that keep to these rules, and one draw needn't show every extreme that they name: root_factor read as a 6144 x 6144 matrix and each child_factor[c] read as a 4096 x 4096 matrix are unit lower triangular (ones on the diagonal, zeros above it). Entry i of child_rows[c] lies in root rows 128 * k to 128 * k + 127 for k = i // 64; every such block contributes its first and its last row; entries of one child are distinct and ascending.
All inputs are finite; a program needn't handle non-finite values.
Results may differ from a plain program's by a relative error of at most 0.0041.
Values may be sent and summed in bfloat16 or wider, within the bound.
No kernel may reach another device: no remote copies, remote signals or barrier semaphores. Data moves between devices by JAX's collectives and lax.ppermute only.
A program may use at most 128 MiB of HBM per device.

v0:
```python
import jax
import jax.numpy as jnp
from jax import lax
from jax.sharding import PartitionSpec as P


def transpose_product(left, right):
    return lax.dot_general(
        left, right, (((0,), (0,)), ((), ())), preferred_element_type=jnp.float32
    )


def deal_rows(panel, groups, block_size):
    height = panel.shape[0]
    width = panel.shape[1]
    outer = width // (block_size * groups)
    return (
        panel.reshape(height, outer, groups, block_size)
        .transpose(0, 2, 1, 3)
        .reshape(height, width)
    )


def per_device(root_factor, root_pivots, child_factor, child_pivots, child_block, child_rows):
    n_row = lax.axis_size("row")
    row_index = lax.axis_index("row")
    block_size = root_factor.shape[2]
    own_rows = root_factor.shape[0] * block_size
    own_cols = root_factor.shape[3] * block_size
    factor_here = root_factor.reshape(own_rows, own_cols)
    scaled_root = (root_pivots.reshape(own_rows)[:, None] * factor_here.astype(jnp.float32)).astype(
        jnp.bfloat16
    )
    gathered = lax.all_gather(root_factor, "col", axis=4, tiled=True)
    panel = gathered.reshape(own_rows, -1)
    ordered = deal_rows(panel, n_row, block_size)
    half_sum = lax.psum_scatter(
        transpose_product(ordered, scaled_root), "row", scatter_dimension=0, tiled=True
    )
    root_inverse = lax.psum(half_sum, "half")
    root_low = root_inverse.astype(jnp.bfloat16)
    reach_rows = child_block.shape[3]
    all_rows = child_rows[0]
    reached = all_rows.shape[0]
    by_row = all_rows.reshape(reached // (reach_rows * n_row), n_row, reach_rows)
    mine_rows = lax.dynamic_index_in_dim(by_row, row_index, 1, keepdims=False).reshape(-1)
    rows_here = mine_rows // (block_size * n_row) * block_size + mine_rows % block_size
    picked = jnp.take(root_low, rows_here, axis=0)
    picked_rows = picked.shape[0]
    shaped = picked.reshape(picked_rows, own_cols // block_size, 1, block_size)
    wide = lax.all_gather(shaped, "col", axis=2, tiled=True).reshape(picked_rows, -1)
    restricted = jnp.take(wide, all_rows, axis=1)
    block_groups = child_block.shape[1]
    block_cols = child_block.shape[4] * child_block.shape[6]
    restricted_blocks = restricted.reshape(picked_rows, block_groups, n_row, reach_rows)
    start_total = jnp.zeros((picked_rows, block_cols), jnp.float32)
    piece = lax.all_gather(child_block, "row", axis=2, tiled=True)
    count = piece.shape[2]
    right = piece.reshape(block_groups, count, reach_rows, block_cols)
    offdiag = start_total - lax.dot_general(
        restricted_blocks,
        right,
        (((1, 2, 3), (0, 1, 2)), ((), ())),
        preferred_element_type=jnp.float32,
    )
    offdiag_low = offdiag.astype(jnp.bfloat16)
    child_rows_here = child_factor.shape[1] * block_size
    child_cols_here = child_factor.shape[4] * block_size
    lower_here = child_factor.reshape(child_rows_here, child_cols_here)
    scaled_child = (
        child_pivots.reshape(child_rows_here)[:, None] * lower_here.astype(jnp.float32)
    ).astype(jnp.bfloat16)
    factor_gathered, block_gathered = (
        lax.all_gather(child_factor, "col", axis=5, tiled=True),
        lax.all_gather(child_block, "col", axis=5, tiled=True),
    )
    factor_panel = deal_rows(factor_gathered.reshape(child_rows_here, -1), n_row, block_size)
    block_panel = deal_rows(block_gathered.reshape(picked_rows, -1), n_row, block_size)
    own = transpose_product(factor_panel, scaled_child)
    coupled = transpose_product(block_panel, offdiag_low)
    child_inverse = lax.psum_scatter(own - coupled, "row", scatter_dimension=0, tiled=True)
    root_out = root_inverse.reshape(
        root_inverse.shape[0] // block_size, 1, block_size, own_cols // block_size, 1, block_size
    )
    return (root_out, offdiag.reshape(child_block.shape), child_inverse.reshape(child_factor.shape))


def solution(mesh):
    return jax.shard_map(
        per_device,
        mesh=mesh,
        in_specs=(
            P(None, ("half", "row"), None, None, "col", None),
            P(None, ("half", "row"), None),
            P("half", None, "row", None, None, "col", None),
            P("half", None, "row", None),
            P("half", None, "row", None, None, "col", None),
            P("half", None),
        ),
        out_specs=(
            P(None, "row", None, None, "col", None),
            P("half", None, "row", None, None, "col", None),
            P("half", None, "row", None, None, "col", None),
        ),
        check_vma=False,
    )
```

profile of v0, /device:TPU:1, one launch (start us, length us, event | category | flops | bytes accessed | tf_op | source)
XLA Modules:
  0.0 564.2 jit_solution(4853052067851650158)
XLA Ops:
  7.2 0.7 all-gather.6.cloned.1.call-update
  7.9 0.7 copy.57
  8.6 1.1 multiply_convert_fusion
  9.7 0.3 copy.27
  10.0 63.3 %all-gather.6.cloned.1.call-done = bf16[3,1,128,3,16,128]{5,2,3,1,0,4:T(8,128)(2,1)} async-done(((bf16[3,1,128,3,1,128]{5,2,3,1,0,4:T(8,128)(2,1)}), bf16[3,1,128,3,16,128]{5,2,3,1,0,4:T(8,128)(2,1)}) %all-gather.6.cloned.1.call-update) | async-done | bytes 4718608 | tf_op jit(solution)/shard_map/all_gather | solution.py:34
  73.3 7.5 %copy.29 = bf16[3,1,128,3,16,128]{5,4,3,2,0,1:T(8,128)(2,1)} copy(bf16[3,1,128,3,16,128]{5,2,3,1,0,4:T(8,128)(2,1)} %all-gather.6.cloned.1.call-done) | data formatting | bytes 9437184 | tf_op jit(solution)/shard_map/all_gather | solution.py:34
  80.8 7.1 %copy.30 = bf16[384,8,6,128]{0,3,2,1:T(8,128)(2,1)} copy(bf16[384,8,6,128]{3,1,2,0:T(8,128)(2,1)} %bitcast.61) | data formatting | bytes 9437184 | tf_op jit(solution)/shard_map/transpose | solution.py:19
  87.9 8.7 %convolution_bitcast_fusion = f32[6144,384]{0,1:T(8,128)} fusion(bf16[384,6144]{0,1:T(8,128)(2,1)} %bitcast.60, bf16[48,8,3,128]{3,2,1,0:T(4,128)(2,1)S(1)} %bitcast.67), kind=kOutput, calls=%fused_computation.2 | convolution fusion | flops 1811939328 | bytes 14450688 | tf_op jit(solution)/shard_map/dot_general | solution.py:8
  96.6 104.7 %reduce-scatter.3.cloned.1.call-done = f32[768,384]{0,1:T(8,128)} async-done(((f32[6144,384]{0,1:T(8,128)}), f32[768,384]{0,1:T(8,128)}) %reduce-scatter.3.cloned.1.call-update) | async-done | bytes 1179664 | tf_op jit(solution)/shard_map/reduce_scatter | solution.py:37
  201.4 0.5 all-gather.10.cloned.1.call-update
  202.0 0.7 copy.38
  202.8 0.7 copy.35
  203.6 0.5 broadcast.258
  204.1 0.7 reduce.8
  204.9 0.1 reshape.262
  205.0 0.1 reshape.261
  205.1 53.6 %all-reduce.2.cloned.1.call-done = f32[768,384]{0,1:T(8,128)} async-done(((f32[768,384]{0,1:T(8,128)}), f32[768,384]{0,1:T(8,128)}) %all-reduce.2.cloned.1.call-update) | async-done | bytes 1179664 | tf_op jit(solution)/shard_map/psum | solution.py:40
  258.8 1.3 convert_element_type.29
  260.1 0.3 copy.31
  260.4 2.1 gather_fusion
  262.6 0.2 copy.32
  262.8 0.9 copy.33
  263.7 0.2 reduce-scatter.5.cloned.1.call-start
  264.0 0.1 broadcast_in_dim.26
  264.1 0.7 multiply_convert_fusion.1
  264.8 29.5 %all-gather.10.cloned.1.call-done = bf16[1,6,8,64,2,1,128]{6,4,5,3,2,1,0:T(2,128)(2,1)} async-done(((bf16[1,6,1,64,2,1,128]{6,4,5,3,2,1,0:T(2,128)(2,1)}), bf16[1,6,8,64,2,1,128]{6,4,5,3,2,1,0:T(2,128)(2,1)}) %all-gather.10.cloned.1.call-update) | async-done | bytes 1572880 | tf_op jit(solution)/shard_map/all_gather | solution.py:57
  294.3 3.8 reshape.264
  298.1 50.1 %all-gather.14.cloned.1.call-done = bf16[1,6,1,64,2,16,128]{6,3,4,2,1,0,5:T(8,128)(2,1)} async-done(((bf16[1,6,1,64,2,1,128]{6,3,4,2,1,0,5:T(8,128)(2,1)}), bf16[1,6,1,64,2,16,128]{6,3,4,2,1,0,5:T(8,128)(2,1)}) %all-gather.14.cloned.1.call-update) | async-done | bytes 3145744 | tf_op jit(solution)/shard_map/all_gather | solution.py:75
  348.2 3.9 copy.39
  352.1 3.5 copy.40
  355.6 51.6 %all-gather.12.cloned.1.call-done = bf16[1,4,1,128,2,16,128]{6,3,4,2,1,0,5:T(8,128)(2,1)} async-done(((bf16[1,4,1,128,2,1,128]{6,3,4,2,1,0,5:T(8,128)(2,1)}), bf16[1,4,1,128,2,16,128]{6,3,4,2,1,0,5:T(8,128)(2,1)}) %all-gather.12.cloned.1.call-update) | async-done | bytes 4194320 | tf_op jit(solution)/shard_map/all_gather | solution.py:74
  407.2 6.9 %copy.36 = bf16[1,4,1,128,2,16,128]{6,5,4,3,1,2,0:T(8,128)(2,1)} copy(bf16[1,4,1,128,2,16,128]{6,3,4,2,1,0,5:T(8,128)(2,1)} %all-gather.12.cloned.1.call-done) | data formatting | bytes 8388608 | tf_op jit(solution)/shard_map/all_gather | solution.py:74
  414.1 7.6 %copy.37 = bf16[512,8,4,128]{0,3,2,1:T(8,128)(2,1)} copy(bf16[512,8,4,128]{3,1,2,0:T(8,128)(2,1)} %bitcast.63) | data formatting | bytes 8388608 | tf_op jit(solution)/shard_map/transpose | solution.py:19
  421.7 5.8 %fusion.4 = f32[256,4096]{1,0:T(8,128)} fusion(bf16[512,4096]{0,1:T(8,128)(2,1)} %bitcast.62, bf16[64,8,2,128]{3,2,1,0:T(2,128)(2,1)S(1)} %bitcast.70), kind=kOutput, calls=%fused_computation.13 | convolution fusion | flops 1073741824 | bytes 8650752 | tf_op jit(solution)/shard_map/dot_general | solution.py:8
  427.5 41.9 %all-gather.8.cloned.1.call-done = bf16[384,3,16,128]{3,0,1,2:T(8,128)(2,1)} async-done(((bf16[384,3,1,128]{3,0,1,2:T(8,128)(2,1)}), bf16[384,3,16,128]{3,0,1,2:T(8,128)(2,1)}) %all-gather.8.cloned.1.call-update) | async-done | bytes 4718608 | tf_op jit(solution)/shard_map/all_gather | solution.py:51
  469.3 6.7 %copy.34 = bf16[384,3,16,128]{0,3,2,1:T(8,128)(2,1)} copy(bf16[384,3,16,128]{3,0,1,2:T(8,128)(2,1)} %all-gather.8.cloned.1.call-done) | data formatting | bytes 9437184 | tf_op jit(solution)/shard_map/all_gather | solution.py:51
  476.1 13.6 %gather_fusion.1 = bf16[3072,384]{1,0:T(8,128)(2,1)S(1)} fusion(bf16[384,6144]{0,1:T(8,128)(2,1)} %bitcast.59, s32[3072]{0:T(1024)S(1)} %broadcast_clamp_fusion), kind=kCustom, calls=%fused_computation.1 | custom fusion | bytes 4730880 | tf_op jit(solution)/shard_map/jit(_take)/gather | solution.py:52
  489.7 1.8 broadcast_select_fusion
  491.5 0.8 fusion.1
  492.4 1.5 copy-done
  493.8 3.2 fusion
  497.1 1.2 copy-done.3
  498.3 0.2 reshape.260
  498.5 1.9 copy.41
  500.4 0.9 reshape.265
  501.4 53.7 %reduce-scatter.5.cloned.1.call-done = f32[512,256]{0,1:T(8,128)} async-done(((f32[4096,256]{0,1:T(8,128)}), f32[512,256]{0,1:T(8,128)}) %reduce-scatter.5.cloned.1.call-update) | async-done | bytes 524304 | tf_op jit(solution)/shard_map/reduce_scatter | solution.py:81
  555.1 1.2 reshape.268
  556.3 1.0 copy.43
  (36 shorter events, 0.6 us)
Async XLA Ops:
  7.2 66.1 %all-gather.6.cloned.1.call-start = ((), (), s32[]{:S(2)}) async-start(), calls=%async_computation.2 | async-start | bytes 5013504 | tf_op jit(solution)/shard_map/all_gather | solution.py:34
  7.9 193.4 %reduce-scatter.3.cloned.1.call-start = ((), (), s32[]{:S(2)}) async-start(), calls=%async_computation.3 | async-start | bytes 10616832 | tf_op jit(solution)/shard_map/reduce_scatter | solution.py:37
  96.5 105.5 %copy-start.5 = (bf16[1,6,1,64,2,1,128]{6,4,5,3,2,1,0:T(2,128)(2,1)S(1)}, bf16[1,6,1,64,2,1,128]{6,4,5,3,2,1,0:T(2,128)(2,1)}, u32[]{:S(2)}) copy-start(bf16[1,6,1,64,2,1,128]{6,4,5,3,2,1,0:T(2,128)(2,1)} %param.10) | copy-start | bytes 589828
  96.5 106.3 %copy-start.4 = (bf16[1,4,1,128,2,1,128]{6,4,5,3,2,1,0:T(2,128)(2,1)S(1)}, bf16[1,4,1,128,2,1,128]{6,4,5,3,2,1,0:T(2,128)(2,1)}, u32[]{:S(2)}) copy-start(bf16[1,4,1,128,2,1,128]{6,4,5,3,2,1,0:T(2,128)(2,1)} %param.8) | copy-start | bytes 786436
  96.5 107.6 %copy-start.6 = (s32[1,3072]{1,0:T(1,128)S(1)}, s32[1,3072]{1,0:T(1,128)}, u32[]{:S(2)}) copy-start(s32[1,3072]{1,0:T(1,128)} %param.11) | copy-start | bytes 36868
  96.5 162.2 %all-reduce.2.cloned.1.call-start = ((), (), s32[]{:S(2)}) async-start(), calls=%async_computation.4 | async-start | bytes 2359296 | tf_op jit(solution)/shard_map/psum | solution.py:40
  201.4 92.9 %all-gather.10.cloned.1.call-start = ((), (), s32[]{:S(2)}) async-start(), calls=%async_computation.6 | async-start | bytes 1769472 | tf_op jit(solution)/shard_map/all_gather | solution.py:57
  201.9 146.2 %all-gather.14.cloned.1.call-start = ((), (), s32[]{:S(2)}) async-start(), calls=%async_computation.8 | async-start | bytes 3342336 | tf_op jit(solution)/shard_map/all_gather | solution.py:75
  202.7 204.4 %all-gather.12.cloned.1.call-start = ((), (), s32[]{:S(2)}) async-start(), calls=%async_computation.7 | async-start | bytes 4456448 | tf_op jit(solution)/shard_map/all_gather | solution.py:74
  203.6 265.8 %all-gather.8.cloned.1.call-start = ((), (), s32[]{:S(2)}) async-start(), calls=%async_computation.5 | async-start | bytes 5013504 | tf_op jit(solution)/shard_map/all_gather | solution.py:51
  260.1 4.0 copy-start.7
  263.7 291.3 %reduce-scatter.5.cloned.1.call-start = ((), (), s32[]{:S(2)}) async-start(), calls=%async_computation.9 | async-start | bytes 4718592 | tf_op jit(solution)/shard_map/reduce_scatter | solution.py:81
  489.7 1.9 copy-start.2
  489.7 2.7 copy-start.1
  491.5 2.3 copy-start
  497.1 1.3 copy-start.3
Sparse Core Ops, SparseCore 0:
  10.4 62.8 all-gather.5
  96.7 104.6 reduce-scatter.2
  203.9 54.7 all-reduce.1
  260.6 33.6 all-gather.9
  297.5 50.6 all-gather.13
  351.3 55.8 all-gather.11
  410.5 58.8 all-gather.7
  497.2 57.8 reduce-scatter.4
where the time goes:
time: 566 us; the launch traced here: 564 us
  waiting for transfers between devices  450 us (80%)
  local copies, waits for them, and re-layouts  75.4 us (13%)
  matrix products  18.5 us (3%)
  between operations  14.3 us (3%)
  other arithmetic  5.77 us (1%)
    reduce_scatter x1, waiting for transfers between devices, per_device(): lax.psum_scatter(transpose_product(ordered, scaled_root), 'row', scatter_...  105 us
    all_gather x1, waiting for transfers between devices, per_device(): gathered = lax.all_gather(root_factor, 'col', axis=4, tiled=True)  63.3 us
    reduce_scatter x1, waiting for transfers between devices, per_device(): lax.psum_scatter(own - coupled, 'row', scatter_dimension=0, tiled=True)  53.7 us
    psum x1, waiting for transfers between devices, per_device(): root_inverse = lax.psum(half_sum, 'half')  53.6 us
    all_gather x1, waiting for transfers between devices, per_device(): lax.all_gather(child_factor, 'col', axis=5, tiled=True)  51.6 us
    all_gather x1, waiting for transfers between devices, per_device(): lax.all_gather(child_block, 'col', axis=5, tiled=True)  50.1 us
    all_gather x1, waiting for transfers between devices, per_device(): lax.all_gather(shaped, 'col', axis=2, tiled=True).reshape(picked_rows, -1)  41.9 us
    all_gather x1, waiting for transfers between devices, per_device(): piece = lax.all_gather(child_block, 'row', axis=2, tiled=True)  29.5 us
  transfers between devices with their start and end apart: 8, of which 8 were waited for; matrix products, arithmetic and copies ran while one was open for 8% of the time, Pallas kernels for 0%

commit v1 on v0

v1 whole, which is shorter than its diff:
```python
import functools

import jax
import jax.numpy as jnp
from jax import lax
from jax.experimental import pallas as pl
from jax.experimental.pallas import tpu as pltpu
from jax.sharding import PartitionSpec as P

AXES = ("half", "row", "col")
N_HALF, N_ROW, N_COL = 2, 8, 16
SIDE = 4
BLK = 128
REACH = 64
VMEM_LIMIT = 48 * 1024 * 1024


def permute(array, target):
    pairs = []
    for half in range(N_HALF):
        for row in range(N_ROW):
            for col in range(N_COL):
                to_half, to_row, to_col = target(half, row, col)
                pairs.append(
                    (
                        (half * N_ROW + row) * N_COL + col,
                        (to_half * N_ROW + to_row) * N_COL + to_col,
                    )
                )
    return lax.ppermute(array, AXES, pairs)


def along_x(step):
    return lambda h, r, q: (h, r, q // SIDE * SIDE + (q + step) % SIDE)


def along_y(step):
    return lambda h, r, q: (h, r, (q + SIDE * step) % N_COL)


def along_z(step):
    return lambda h, r, q: (h, (r + 2 * step) % N_ROW, q)


def other_core(h, r, q):
    return (h, r ^ 1, q)


def other_half(h, r, q):
    return (1 - h, r, q)


def transposed_place(h, r, q):
    return (h, q % N_ROW, q // N_ROW * N_ROW + (r ^ (q % N_ROW)))


def ring_gather(own, along, split):
    before = permute(own, along(1))
    after = permute(own, along(-1))
    if split:
        cut = own.shape[0] // 2
        across = jnp.concatenate(
            [permute(before[:cut], along(1)), permute(after[cut:], along(-1))], 0
        )
    else:
        across = permute(before, along(1))
    return jnp.concatenate([own, after, across, before], 0)


def plane_gather(first, second):
    one = ring_gather(first, along_x, False)
    two = ring_gather(second, along_y, False)
    one = ring_gather(one, along_y, True)
    two = ring_gather(two, along_x, True)
    return one.reshape(N_COL, *first.shape), two.reshape(N_COL, *second.shape)


def dot(left, right):
    return jnp.dot(left, right, preferred_element_type=jnp.float32)


def dot_nt(left, right):
    return lax.dot_general(left, right, (((1,), (1,)), ((), ())), preferred_element_type=jnp.float32)


def cat(parts, axis):
    return jnp.concatenate(parts, axis)


def root_kernel(slot_one, slot_two, one_ref, two_ref, right_ref, out_ref, acc):
    acc[...] = jnp.zeros_like(acc)

    def step(r, carry):
        right = [right_ref[r, pl.ds(BLK * i, BLK), :] for i in range(6)]
        right_0 = right[0]
        right_1 = cat(right[1:3], 1)
        right_2 = cat(right[3:6], 1)
        for side in range(2):
            one = slot_one[side * N_ROW + r]
            two = slot_two[side * N_ROW + r]
            acc[side] += dot(two_ref[two], right_2)
            acc[side, : 2 * BLK, : 2 * BLK] += dot(one_ref[one, BLK:, :], right_1)
            acc[side, :BLK, :BLK] += dot(one_ref[one, :BLK, :], right_0)
        return carry

    lax.fori_loop(0, N_ROW, step, 0)
    for outer in range(3):
        for side in range(2):
            out_ref[pl.ds((2 * outer + side) * BLK, BLK), :] = acc[
                side, pl.ds(outer * BLK, BLK), :
            ].astype(out_ref.dtype)


def pick_kernel(mine_ref, other_ref, row_ref, col_ref, root_ref, picked_ref):
    total = mine_ref[...].astype(jnp.float32) + other_ref[...].astype(jnp.float32)
    root_ref[...] = total
    low = total.astype(jnp.bfloat16)
    lanes = lax.broadcasted_iota(jnp.int32, (REACH, BLK), 1)

    def chooser(ref, i):
        return jnp.where(ref[pl.ds(i * REACH, REACH), :] == lanes, 1.0, 0.0).astype(jnp.bfloat16)

    rows = cat(
        [dot(chooser(row_ref, i), low[i * BLK : (i + 1) * BLK, :]).astype(jnp.bfloat16) for i in range(6)], 0
    )
    for i in range(3):
        picked_ref[pl.ds(i * REACH, REACH), :] = dot_nt(
            chooser(col_ref, i), rows[:, i * BLK : (i + 1) * BLK]
        ).astype(jnp.bfloat16)


def offdiag_kernel(slot_one, slot_two, one_ref, two_ref, block_ref, out_ref, low_ref, acc):
    acc[...] = jnp.zeros_like(acc)

    def step(r, carry):
        left = cat([block_ref[r, pl.ds(256 * i, 256), :] for i in range(3)], 1)
        right = cat(
            [
                one_ref[slot_one[r]],
                two_ref[slot_two[r]],
                one_ref[slot_one[N_ROW + r]],
                two_ref[slot_two[N_ROW + r]],
            ],
            0,
        )
        acc[...] += dot(left, right)
        return carry

    lax.fori_loop(0, N_ROW, step, 0)
    total = -acc[...]
    low_ref[...] = total.astype(low_ref.dtype)
    out_ref[...] = total.T


def own_kernel(slots, left_ref, right_ref, out_ref, acc):
    acc[...] = jnp.zeros_like(acc)

    def step(r, carry):
        right = [right_ref[r, pl.ds(BLK * i, BLK), :] for i in range(6)]
        right_0 = cat(right[0:2], 0)
        right_1 = cat([cat(right[2:4], 1), cat(right[4:6], 1)], 0)
        for side in range(2):
            slot = slots[side * N_ROW + r]
            left_0 = cat([left_ref[slot, :BLK, :], left_ref[slot, BLK : 2 * BLK, :]], 1)
            left_1 = cat([left_ref[slot, 2 * BLK : 4 * BLK, :], left_ref[slot, 4 * BLK : 6 * BLK, :]], 1)
            acc[side] += dot(left_1, right_1)
            acc[side, :BLK, :BLK] += dot(left_0, right_0)
        return carry

    lax.fori_loop(0, N_ROW, step, 0)
    out_ref[...] = acc[...]


def child_kernel(slots, part_slots, own_ref, left_ref, right_ref, out_ref, acc):
    acc[...] = own_ref[...]

    def step(r, carry):
        right = right_ref[part_slots[r]]
        for side in range(2):
            slot = slots[side * N_ROW + r]
            left = cat([left_ref[slot, pl.ds(256 * i, 256), :] for i in range(3)], 1)
            acc[side] -= dot_nt(left, right)
        return carry

    lax.fori_loop(0, N_ROW, step, 0)
    for outer in range(2):
        for side in range(2):
            out_ref[pl.ds((2 * outer + side) * BLK, BLK), :] = acc[side, pl.ds(outer * BLK, BLK), :]


def call(kernel, scalars, arrays, outs, scratch=(), blocks=None):
    vmem = pl.BlockSpec(memory_space=pltpu.VMEM)
    smem = pl.BlockSpec(memory_space=pltpu.SMEM)
    return pl.pallas_call(
        kernel,
        in_specs=[smem] * len(scalars) + [vmem] * len(arrays),
        out_specs=[vmem] * len(outs),
        out_shape=[jax.ShapeDtypeStruct(*o) for o in outs],
        scratch_shapes=list(scratch),
        compiler_params=pltpu.CompilerParams(vmem_limit_bytes=VMEM_LIMIT),
    )(*scalars, *arrays)


def stack_blocks(array, pairs):
    return jnp.concatenate([array[a, :, b, :] for a, b in pairs], 0)


def per_device(root_factor, root_pivots, child_factor, child_pivots, child_block, child_rows):
    row = lax.axis_index("row")
    col = lax.axis_index("col")
    bf16 = jnp.bfloat16
    root = root_factor.reshape(3, BLK, 3, BLK)
    scaled_root = (root_pivots.reshape(3, BLK, 1, 1) * root.astype(jnp.float32)).astype(bf16)
    root_pairs = [(0, 0), (1, 0), (1, 1), (2, 0), (2, 1), (2, 2)]
    root_turned = stack_blocks(root.transpose(0, 3, 2, 1), root_pairs)
    root_scaled = stack_blocks(scaled_root, root_pairs)

    child = child_factor.reshape(4, BLK, 2, BLK)
    scaled_child = (child_pivots.reshape(4, BLK, 1, 1) * child.astype(jnp.float32)).astype(bf16)
    child_pairs = [(0, 0), (1, 0), (2, 0), (2, 1), (3, 0), (3, 1)]
    child_turned = stack_blocks(child.transpose(0, 3, 2, 1), child_pairs)
    child_scaled = stack_blocks(scaled_child, child_pairs)
    block = child_block.reshape(6 * REACH, 2 * BLK)
    block_turned = block.T.reshape(2 * BLK, 3, BLK).transpose(1, 0, 2).reshape(768, BLK)
    block_sorted = block.reshape(3, 2, REACH, 2 * BLK).transpose(1, 0, 2, 3).reshape(6 * REACH, 2 * BLK)
    block_sorted = block_sorted.T.reshape(2 * BLK, 3, BLK).transpose(1, 0, 2).reshape(768, BLK)

    root_right = lax.all_gather(root_scaled, "row", axis=0, tiled=False)
    root_here = permute(root_turned, transposed_place)
    child_here = permute(jnp.concatenate([child_turned, block_turned], 0), transposed_place)
    child_left = lax.all_gather(child_here, "col", axis=0, tiled=False)
    child_right = lax.all_gather(jnp.concatenate([child_scaled, block_sorted], 0), "row", axis=0, tiled=False)

    root_one, root_two = plane_gather(root_here[:384], root_here[384:])

    side = jnp.arange(2, dtype=jnp.int32)[:, None]
    classes = jnp.arange(N_ROW, dtype=jnp.int32)[None, :]
    source = side * N_ROW + (classes ^ row)
    my_x, my_y = col % SIDE, col // SIDE

    def plane_slots(place):
        dx = (place % SIDE - my_x) % SIDE
        dy = (place // SIDE - my_y) % SIDE
        return (dy * SIDE + dx).reshape(-1), (dx * SIDE + dy).reshape(-1)

    root_slots = plane_slots(source)
    (partial,) = call(
        root_kernel,
        root_slots,
        (root_one, root_two, root_right),
        [((768, 384), bf16)],
        [pltpu.VMEM((2, 384, 384), jnp.float32)],
    )
    other = permute(partial, other_half)
    rows = child_rows[0].reshape(48, REACH) % BLK
    row_picks = lax.dynamic_index_in_dim(rows.reshape(6, N_ROW, REACH), row, 1, keepdims=False)
    col_picks = lax.dynamic_index_in_dim(rows.reshape(3, N_COL, REACH), col, 1, keepdims=False)
    root_inverse, picked = call(
        pick_kernel,
        (),
        (partial, other, row_picks.reshape(-1, 1), col_picks.reshape(-1, 1)),
        [((768, 384), jnp.float32), ((192, 384), bf16)],
    )
    restricted_one, restricted_two = plane_gather(picked[:96], picked[96:])
    offdiag_slots = plane_slots(side * N_ROW + classes)
    offdiag, offdiag_low = call(
        offdiag_kernel,
        offdiag_slots,
        (restricted_one, restricted_two, child_right[:, 768:]),
        [((384, 256), jnp.float32), ((256, 384), bf16)],
        [pltpu.VMEM((256, 384), jnp.float32)],
    )
    slots = source.reshape(-1)
    (own,) = call(
        own_kernel,
        (slots,),
        (child_left[:, :768], child_right[:, :768]),
        [((2, 256, 256), jnp.float32)],
        [pltpu.VMEM((2, 256, 256), jnp.float32)],
    )
    line = ring_gather(offdiag_low, along_z, True)
    beside = permute(line, other_core)
    parts = jnp.concatenate([line, beside], 0).reshape(N_ROW, 256, 384)
    r = classes[0]
    part_slots = ((r ^ row) & 1) * SIDE + (r // 2 - row // 2) % SIDE
    (child_inverse,) = call(
        child_kernel,
        (slots, part_slots),
        (own, child_left[:, 768:], parts),
        [((512, 256), jnp.float32)],
        [pltpu.VMEM((2, 256, 256), jnp.float32)],
    )
    return (
        root_inverse.reshape(6, 1, BLK, 3, 1, BLK),
        offdiag.reshape(child_block.shape),
        child_inverse.reshape(child_factor.shape),
    )


def solution(mesh):
    return jax.shard_map(
        per_device,
        mesh=mesh,
        in_specs=(
            P(None, ("half", "row"), None, None, "col", None),
            P(None, ("half", "row"), None),
            P("half", None, "row", None, None, "col", None),
            P("half", None, "row", None),
            P("half", None, "row", None, None, "col", None),
            P("half", None),
        ),
        out_specs=(
            P(None, "row", None, None, "col", None),
            P("half", None, "row", None, None, "col", None),
            P("half", None, "row", None, None, "col", None),
        ),
        check_vma=False,
    )
```

time: 566 us -> 247 us (0.44)
  waiting for transfers between devices: 450 us -> 65.5 us
  starting transfers between devices: 0.5 us -> 110 us
  local copies, waits for them, and re-layouts: 75.4 us -> 37.2 us
  matrix products: 18.5 us -> 0 us
  Pallas kernels: 0 us -> 15.1 us
    all_gather x5 -> x3, waiting for transfers between devices: 236 us -> 0.06 us  [the longest x1 0.02 us: per_device(): child_left = lax.all_gather(child_here, 'col', axis=0, tiled=False)]
    reduce_scatter x2 -> x0, waiting for transfers between devices: 158 us -> none  [the longest x1 105 us: per_device(): lax.psum_scatter(transpose_product(ordered, scaled_root), 'row', scatter_...]
    ppermute x0 -> x36, starting transfers between devices: none -> 110 us  [permute(): return lax.ppermute(array, AXES, pairs)]
    ppermute x0 -> x36, waiting for transfers between devices: none -> 65.3 us  [permute(): return lax.ppermute(array, AXES, pairs)]
    psum x1 -> x0, waiting for transfers between devices: 53.6 us -> none  [per_device(): root_inverse = lax.psum(half_sum, 'half')]
    all_gather x4 -> x0, local copies, waits for them, and re-layouts: 25.1 us -> none  [the longest x1 7.5 us: per_device(): gathered = lax.all_gather(root_factor, 'col', axis=4, tiled=True)]
    dot_general x4 -> x0, matrix products: 18.5 us -> none  [the longest x3 17.7 us: transpose_product(): lax.dot_general(left, right, (((0,), (0,)), ((), ())), preferred_element_...]
    transpose x3 -> x2, local copies, waits for them, and re-layouts: 18.1 us -> 0.18 us  [the longest x1 0.16 us: per_device(): block_sorted.T.reshape(2 * BLK, 3, BLK).transpose(1, 0, 2).reshape(768, BLK)]
  transfers between devices with their start and end apart: 8 -> 39, of which waited for: 8 -> 16; matrix products, arithmetic and copies ran while one was open for 8% -> 12% of each run, Pallas kernels for 0% -> 4%
where the time goes in v1:
time: 247 us; the launch traced here: 246 us
  starting transfers between devices  110 us (45%)
  waiting for transfers between devices  65.5 us (27%)
  local copies, waits for them, and re-layouts  37.2 us (15%)
  Pallas kernels  15.1 us (6%)
  between operations  14.6 us (6%)
  other arithmetic  3.53 us (1%)
    ppermute x36, starting transfers between devices, permute(): return lax.ppermute(array, AXES, pairs)  110 us
    ppermute x36, waiting for transfers between devices, permute(): return lax.ppermute(array, AXES, pairs)  65.3 us
    pallas_call x5, Pallas kernels, call(): pl.pallas_call(kernel, in_specs=[smem] * len(scalars) + [vmem] * len(arra...  15.1 us
    unnamed x80, local copies, waits for them, and re-layouts  14.5 us
    concatenate x7, local copies, waits for them, and re-layouts, ring_gather(): return jnp.concatenate([own, after, across, before], 0)  5.5 us
  transfers between devices with their start and end apart: 39, of which 16 were waited for; matrix products, arithmetic and copies ran while one was open for 12% of the time, Pallas kernels for 4%

profile of v1, /device:TPU:1, one launch (start us, length us, event | category | flops | bytes accessed | tf_op | source)
XLA Modules:
  0.0 246.4 jit_solution(15873919142183871805)
XLA Ops:
  7.9 1.1 multiply_convert_fusion
  9.9 1.1 reshape_reshape.3
  13.4 4.5 %collective-permute-start.30 = (bf16[1536,128]{1,0:T(8,128)(2,1)S(1)}, bf16[1536,128]{1,0:T(8,128)(2,1)S(1)}, u32[]{:S(2)}, u32[]{:S(2)}) collective-permute-start(bf16[1536,128]{1,0:T(8,128)(2,1)S(1)} %constant_dynamic-update-slice_fusion.51), channel_id=1, source_target_pairs={{0,0},{1,17},{2,34},{3,51},{4,68},{5,85},{6,102},{7,119},{8,8},{9,... | collective-permute-start | bytes 1179656 | tf_op jit(solution)/shard_map/ppermute | solution.py:30
  17.9 4.7 %collective-permute-done.30 = bf16[1536,128]{1,0:T(8,128)(2,1)S(1)} collective-permute-done((bf16[1536,128]{1,0:T(8,128)(2,1)S(1)}, bf16[1536,128]{1,0:T(8,128)(2,1)S(1)}, u32[]{:S(2)}, u32[]{:S(2)}) %collective-permute-start.30) | collective-permute-done | bytes 393248 | tf_op jit(solution)/shard_map/ppermute | solution.py:30
  23.5 4.7 %collective-permute-start = (bf16[768,128]{0,1:T(8,128)(2,1)S(1)}, bf16[768,128]{0,1:T(8,128)(2,1)S(1)}, u32[]{:S(2)}, u32[]{:S(2)}) collective-permute-start(bf16[768,128]{0,1:T(8,128)(2,1)S(1)} %constant_dynamic-update-slice_fusion), channel_id=1, source_target_pairs={{0,0},{1,17},{2,34},{3,51},{4,68},{5,85},{6,102},{7,119},{8,8},{9,... | collective-permute-start | bytes 589832 | tf_op jit(solution)/shard_map/ppermute | solution.py:30
  30.4 2.2 collective-permute-done
  33.3 49.8 %collective-permute-start.1 = (bf16[384,128]{0,1:T(8,128)(2,1)S(1)}, bf16[384,128]{0,1:T(8,128)(2,1)S(1)}, u32[]{:S(2)}, u32[]{:S(2)}) collective-permute-start(bf16[384,128]{0,1:T(8,128)(2,1)S(1)} %get-tuple-element.45), channel_id=1, source_target_pairs={{0,3},{1,0},{2,1},{3,2},{4,7},{5,4},{6,5},{7,6},{8,11},{9,8},{10,9... | collective-permute-start | bytes 294920 | tf_op jit(solution)/shard_map/ppermute | solution.py:30
  83.9 1.9 collective-permute-start.8
  85.8 2.0 collective-permute-done.2
  89.3 4.3 %collective-permute-done.3 = bf16[384,128]{0,1:T(8,128)(2,1)S(1)} collective-permute-done((bf16[384,128]{0,1:T(8,128)(2,1)S(1)}, bf16[384,128]{0,1:T(8,128)(2,1)S(1)}, u32[]{:S(2)}, u32[]{:S(2)}) %collective-permute-start.3) | collective-permute-done | bytes 98336 | tf_op jit(solution)/shard_map/ppermute | solution.py:30
  93.6 2.9 %collective-permute-start.4 = (bf16[1536,128]{0,1:T(8,128)(2,1)S(1)}, bf16[1536,128]{0,1:T(8,128)(2,1)S(1)}, u32[]{:S(2)}, u32[]{:S(2)}) collective-permute-start(bf16[1536,128]{0,1:T(8,128)(2,1)S(1)} %pad_maximum_fusion), channel_id=1, source_target_pairs={{0,12},{1,13},{2,14},{3,15},{4,0},{5,1},{6,2},{7,3},{8,4},{9,5},{1... | collective-permute-start | bytes 1179656 | tf_op jit(solution)/shard_map/ppermute | solution.py:30
  96.6 1.5 collective-permute-start.12
  99.5 8.5 %collective-permute-done.5 = bf16[1536,128]{0,1:T(8,128)(2,1)S(1)} collective-permute-done((bf16[1536,128]{0,1:T(8,128)(2,1)S(1)}, bf16[1536,128]{0,1:T(8,128)(2,1)S(1)}, u32[]{:S(2)}, u32[]{:S(2)}) %collective-permute-start.5) | collective-permute-done | bytes 393248 | tf_op jit(solution)/shard_map/ppermute | solution.py:30
  108.2 2.7 %collective-permute-start.7 = (bf16[768,128]{0,1:T(8,128)(2,1)S(1)}, bf16[768,128]{0,1:T(8,128)(2,1)S(1)}, u32[]{:S(2)}, u32[]{:S(2)}) collective-permute-start(bf16[768,128]{0,1:T(8,128)(2,1)S(1)} %slice.176), channel_id=1, source_target_pairs={{0,12},{1,13},{2,14},{3,15},{4,0},{5,1},{6,2},{7,3},{8,4},{9,5},{1... | collective-permute-start | bytes 589832 | tf_op jit(solution)/shard_map/ppermute | solution.py:30
  112.3 2.7 %collective-permute-start.14 = (bf16[768,128]{0,1:T(8,128)(2,1)}, bf16[768,128]{0,1:T(8,128)(2,1)}, u32[]{:S(2)}, u32[]{:S(2)}) collective-permute-start(bf16[768,128]{0,1:T(8,128)(2,1)} %slice.179), channel_id=1, source_target_pairs={{0,3},{1,0},{2,1},{3,2},{4,7},{5,4},{6,5},{7,6},{8,11},{9,8},{10,9... | collective-permute-start | bytes 589832 | tf_op jit(solution)/shard_map/ppermute | solution.py:30
  118.3 1.6 constant_dynamic-update-slice_fusion.15
  119.9 1.8 constant_dynamic-update-slice_fusion.14
  121.7 1.9 copy.50
  123.7 1.4 copy-done
  125.1 4.6 %shard_map.85.mine_ref = bf16[768,384]{1,0:T(8,128)(2,1)} custom-call(s32[16]{0:T(128)S(1)} %multiply_add_fusion.3.slot_one, s32[16]{0:T(128)S(1)} %get-tuple-element.23.slot_two, bf16[16,384,128]{2,1,0:T(8,128)(2,1)S(1)} %bitcast.136, bf16[16,384,128]{2,1,0:T(8,128)(2,1)S(1)} %bitcast.137, bf16[8,768,128]{2,1,0:T(8,128)(2,1)S(1)} %bitcast.139), custom_call_target="tpu_custom_call" | custom-call | tf_op jit(solution)/shard_map/pallas_call | solution.py:194
  131.5 9.6 %collective-permute-done.15.other_ref = bf16[768,384]{1,0:T(8,128)(2,1)S(1)} collective-permute-done((bf16[768,384]{1,0:T(8,128)(2,1)}, bf16[768,384]{1,0:T(8,128)(2,1)S(1)}, u32[]{:S(2)}, u32[]{:S(2)}) %collective-permute-start.15) | collective-permute-done | bytes 589856 | tf_op jit(solution)/shard_map/ppermute | solution.py:30
  141.1 1.6 shard_map.86
  142.7 2.4 collective-permute-start.16
  145.2 2.7 %collective-permute-start.23 = (bf16[96,384]{1,0:T(8,128)(2,1)S(1)}, bf16[96,384]{1,0:T(8,128)(2,1)S(1)}, u32[]{:S(2)}, u32[]{:S(2)}) collective-permute-start(bf16[96,384]{1,0:T(8,128)(2,1)S(1)} %get-tuple-element.46), channel_id=1, source_target_pairs={{0,12},{1,13},{2,14},{3,15},{4,0},{5,1},{6,2},{7,3},{8,4},{9,5},{1... | collective-permute-start | bytes 221192 | tf_op jit(solution)/shard_map/ppermute | solution.py:30
  147.8 1.7 collective-permute-done.17
  149.6 4.3 %collective-permute-done.18 = bf16[96,384]{1,0:T(8,128)(2,1)S(1)} collective-permute-done((bf16[96,384]{1,0:T(8,128)(2,1)S(1)}, bf16[96,384]{1,0:T(8,128)(2,1)S(1)}, u32[]{:S(2)}, u32[]{:S(2)}) %collective-permute-start.18) | collective-permute-done | bytes 73760 | tf_op jit(solution)/shard_map/ppermute | solution.py:30
  155.6 1.2 collective-permute-start.26
  157.2 11.6 %collective-permute-done.20 = bf16[384,384]{1,0:T(8,128)(2,1)S(1)} collective-permute-done((bf16[384,384]{1,0:T(8,128)(2,1)S(1)}, bf16[384,384]{1,0:T(8,128)(2,1)S(1)}, u32[]{:S(2)}, u32[]{:S(2)}) %collective-permute-start.20) | collective-permute-done | bytes 294944 | tf_op jit(solution)/shard_map/ppermute | solution.py:30
  169.0 2.9 %collective-permute-start.22 = (bf16[192,384]{1,0:T(8,128)(2,1)S(1)}, bf16[192,384]{1,0:T(8,128)(2,1)S(1)}, u32[]{:S(2)}, u32[]{:S(2)}) collective-permute-start(bf16[192,384]{1,0:T(8,128)(2,1)S(1)} %slice.187), channel_id=1, source_target_pairs={{0,12},{1,13},{2,14},{3,15},{4,0},{5,1},{6,2},{7,3},{8,4},{9,5},{1... | collective-permute-start | bytes 442376 | tf_op jit(solution)/shard_map/ppermute | solution.py:30
  172.1 2.7 %collective-permute-start.29 = (bf16[192,384]{1,0:T(8,128)(2,1)S(1)}, bf16[192,384]{1,0:T(8,128)(2,1)S(1)}, u32[]{:S(2)}, u32[]{:S(2)}) collective-permute-start(bf16[192,384]{1,0:T(8,128)(2,1)S(1)} %slice.189), channel_id=1, source_target_pairs={{0,3},{1,0},{2,1},{3,2},{4,7},{5,4},{6,5},{7,6},{8,11},{9,8},{10,9... | collective-permute-start | bytes 442376 | tf_op jit(solution)/shard_map/ppermute | solution.py:30
  174.9 4.3 %collective-permute-done.21 = bf16[192,384]{1,0:T(8,128)(2,1)S(1)} collective-permute-done((bf16[192,384]{1,0:T(8,128)(2,1)S(1)}, bf16[192,384]{1,0:T(8,128)(2,1)S(1)}, u32[]{:S(2)}, u32[]{:S(2)}) %collective-permute-start.21) | collective-permute-done | bytes 147488 | tf_op jit(solution)/shard_map/ppermute | solution.py:30
  179.3 3.0 %collective-permute-done.28 = bf16[192,384]{1,0:T(8,128)(2,1)S(1)} collective-permute-done((bf16[192,384]{1,0:T(8,128)(2,1)S(1)}, bf16[192,384]{1,0:T(8,128)(2,1)S(1)}, u32[]{:S(2)}, u32[]{:S(2)}) %collective-permute-start.28) | collective-permute-done | bytes 147488 | tf_op jit(solution)/shard_map/ppermute | solution.py:30
  183.6 2.3 fusion.10
  185.9 2.9 %shard_map.87 = (f32[384,256]{1,0:T(8,128)S(1)}, bf16[256,384]{1,0:T(8,128)(2,1)S(1)}) custom-call(s32[16]{0:T(128)S(1)} %multiply_add_fusion.1.slot_one, s32[16]{0:T(128)S(1)} %get-tuple-element.20.slot_two, bf16[16,96,384]{2,1,0:T(8,128)(2,1)S(1)} %bitcast.141, bf16[16,96,384]{2,1,0:T(8,128)(2,1)S(1)} %bitcast.140, ...), custom_call_target="tpu_custom_call" | custom-call | tf_op jit(solution)/shard_map/pallas_call | solution.py:194
  188.8 12.8 %collective-permute-start.32 = (bf16[256,384]{1,0:T(8,128)(2,1)S(1)}, bf16[256,384]{1,0:T(8,128)(2,1)S(1)}, u32[]{:S(2)}, u32[]{:S(2)}) collective-permute-start(bf16[256,384]{1,0:T(8,128)(2,1)S(1)} %get-tuple-element.10), channel_id=1, source_target_pairs={{0,32},{1,33},{2,34},{3,35},{4,36},{5,37},{6,38},{7,39},{8,40},{9,... | collective-permute-start | bytes 589832 | tf_op jit(solution)/shard_map/ppermute | solution.py:30
  202.3 1.9 collective-permute-done.32
  204.2 2.9 %collective-permute-start.33 = (bf16[128,384]{1,0:T(8,128)(2,1)S(1)}, bf16[128,384]{1,0:T(8,128)(2,1)S(1)}, u32[]{:S(2)}, u32[]{:S(2)}) collective-permute-start(bf16[128,384]{1,0:T(8,128)(2,1)S(1)} %slice.206), channel_id=1, source_target_pairs={{0,32},{1,33},{2,34},{3,35},{4,36},{5,37},{6,38},{7,39},{8,40},{9,... | collective-permute-start | bytes 294920 | tf_op jit(solution)/shard_map/ppermute | solution.py:30
  207.2 1.5 collective-permute-done.31
  208.6 1.2 collective-permute-start.34
  210.5 1.9 collective-permute-done.33
  213.1 3.0 %collective-permute-done.34 = bf16[128,384]{1,0:T(8,128)(2,1)S(1)} collective-permute-done((bf16[128,384]{1,0:T(8,128)(2,1)S(1)}, bf16[128,384]{1,0:T(8,128)(2,1)S(1)}, u32[]{:S(2)}, u32[]{:S(2)}) %collective-permute-start.34) | collective-permute-done | bytes 98336 | tf_op jit(solution)/shard_map/ppermute | solution.py:30
  217.5 6.4 %collective-permute-start.35 = (bf16[1024,384]{1,0:T(8,128)(2,1)}, bf16[1024,384]{1,0:T(8,128)(2,1)}, u32[]{:S(2)}, u32[]{:S(2)}) collective-permute-start(bf16[1024,384]{1,0:T(8,128)(2,1)} %get-tuple-element.36), channel_id=1, source_target_pairs={{0,16},{1,17},{2,18},{3,19},{4,20},{5,21},{6,22},{7,23},{8,24},{9,... | collective-permute-start | bytes 2359304 | tf_op jit(solution)/shard_map/ppermute | solution.py:30
  223.9 3.3 %reshape.121 = f32[6,1,128,3,1,128]{5,4,3,2,1,0:T(1,128)} reshape(f32[768,384]{1,0:T(8,128)} %copy-done.3) | data formatting | bytes 2359296 | tf_op jit(solution)/shard_map/reshape | solution.py:294
  228.1 1.3 constant_dynamic-update-slice_fusion.63
  229.4 3.4 %fusion.9 = (bf16[16,768,128]{2,1,0:T(8,128)(2,1)S(1)}, bf16[16,768,128]{2,1,0:T(8,128)(2,1)S(1)}) fusion(bf16[16,1536,128]{2,1,0:T(8,128)(2,1)} %bitcast.142), kind=kLoop, calls=%fused_computation.152 | loop fusion | bytes 12582912 | tf_op jit(solution)/shard_map/slice | solution.py:289
  232.8 2.7 %shard_map.88.own_ref = f32[2,256,256]{2,1,0:T(8,128)S(1)} custom-call(s32[16]{0:T(128)S(1)} %add.142.slots, bf16[16,768,128]{2,1,0:T(8,128)(2,1)S(1)} %get-tuple-element.27.left_ref, bf16[8,768,128]{2,1,0:T(8,128)(2,1)S(1)} %get-tuple-element.28.right_ref), custom_call_target="tpu_custom_call" | custom-call | tf_op jit(solution)/shard_map/pallas_call | solution.py:194
  235.5 3.3 %shard_map.89 = f32[512,256]{1,0:T(8,128)S(1)} custom-call(s32[16]{0:T(128)S(1)} %add.142.slots, s32[8]{0:T(128)S(1)} %fusion.part_slots, f32[2,256,256]{2,1,0:T(8,128)S(1)} %shard_map.88.own_ref, bf16[16,768,128]{2,1,0:T(8,128)(2,1)S(1)} %get-tuple-element.26.left_ref, bf16[8,256,384]{2,1,0:T(8,128)(2,1)S(1)} %bitcast.138), custom_call_target="tpu_custom_call" | custom-call | tf_op jit(solution)/shard_map/pallas_call | solution.py:194
  238.8 1.1 reshape.114
  (185 shorter events, 26.0 us)
Async XLA Ops:
  7.2 4.0 %copy-start.12 = (f32[1,4,1,128]{3,2,1,0:T(1,128)S(1)}, f32[1,4,1,128]{3,2,1,0:T(1,128)}, u32[]{:S(2)}) copy-start(f32[1,4,1,128]{3,2,1,0:T(1,128)} %param.9) | copy-start | bytes 6148
  7.2 4.0 %copy-start.4 = (bf16[1,4,1,128,2,1,128]{6,4,5,3,2,1,0:T(2,128)(2,1)S(1)}, bf16[1,4,1,128,2,1,128]{6,4,5,3,2,1,0:T(2,128)(2,1)}, u32[]{:S(2)}) copy-start(bf16[1,4,1,128,2,1,128]{6,4,5,3,2,1,0:T(2,128)(2,1)} %param.8) | copy-start | bytes 786436
  7.2 116.5 %all-gather.7.cloned.1.call-start = ((), (), s32[]{:S(2)}) async-start(), calls=%async_computation | async-start | bytes 1769472 | tf_op jit(solution)/shard_map/all_gather | solution.py:228
  9.8 173.7 %all-gather.9.cloned.1.call-start = ((), (), s32[]{:S(2)}) async-start(), calls=%async_computation.1 | async-start | bytes 3538944 | tf_op jit(solution)/shard_map/all_gather | solution.py:232
  11.1 2.0 copy-start.7
  12.2 11.2 %copy-start.6 = (bf16[3,1,128,3,1,128]{5,2,4,3,1,0:T(8,128)(2,1)S(1)}, bf16[3,1,128,3,1,128]{5,2,4,3,1,0:T(8,128)(2,1)}, u32[]{:S(2)}) copy-start(bf16[3,1,128,3,1,128]{5,2,4,3,1,0:T(8,128)(2,1)} %param.6) | copy-start | bytes 884740
  12.2 217.2 %all-gather.11.cloned.1.call-start = ((), (), s32[]{:S(2)}) async-start(), calls=%async_computation.2 | async-start | bytes 6684672 | tf_op jit(solution)/shard_map/all_gather | solution.py:231
  12.3 16.6 %copy-start.11 = (s32[1,3072]{1,0:T(1,128)S(1)}, s32[1,3072]{1,0:T(1,128)}, u32[]{:S(2)}) copy-start(s32[1,3072]{1,0:T(1,128)} %param.11) | copy-start | bytes 36868
  13.4 9.2 %collective-permute-start.30 = (bf16[1536,128]{1,0:T(8,128)(2,1)S(1)}, bf16[1536,128]{1,0:T(8,128)(2,1)S(1)}, u32[]{:S(2)}, u32[]{:S(2)}) collective-permute-start(bf16[1536,128]{1,0:T(8,128)(2,1)S(1)} %constant_dynamic-update-slice_fusion.51), channel_id=1, source_target_pairs={{0,0},{1,17},{2,34},{3,51},{4,68},{5,85},{6,102},{7,119},{8,8},{9,... | collective-permute-start | bytes 1179656 | tf_op jit(solution)/shard_map/ppermute | solution.py:30
  23.5 9.1 %collective-permute-start = (bf16[768,128]{0,1:T(8,128)(2,1)S(1)}, bf16[768,128]{0,1:T(8,128)(2,1)S(1)}, u32[]{:S(2)}, u32[]{:S(2)}) collective-permute-start(bf16[768,128]{0,1:T(8,128)(2,1)S(1)} %constant_dynamic-update-slice_fusion), channel_id=1, source_target_pairs={{0,0},{1,17},{2,34},{3,51},{4,68},{5,85},{6,102},{7,119},{8,8},{9,... | collective-permute-start | bytes 589832 | tf_op jit(solution)/shard_map/ppermute | solution.py:30
  33.3 55.2 %collective-permute-start.1 = (bf16[384,128]{0,1:T(8,128)(2,1)S(1)}, bf16[384,128]{0,1:T(8,128)(2,1)S(1)}, u32[]{:S(2)}, u32[]{:S(2)}) collective-permute-start(bf16[384,128]{0,1:T(8,128)(2,1)S(1)} %get-tuple-element.45), channel_id=1, source_target_pairs={{0,3},{1,0},{2,1},{3,2},{4,7},{5,4},{6,5},{7,6},{8,11},{9,8},{10,9... | collective-permute-start | bytes 294920 | tf_op jit(solution)/shard_map/ppermute | solution.py:30
  83.1 4.7 %collective-permute-start.2 = (bf16[384,128]{0,1:T(8,128)(2,1)S(1)}, bf16[384,128]{0,1:T(8,128)(2,1)S(1)}, u32[]{:S(2)}, u32[]{:S(2)}) collective-permute-start(bf16[384,128]{0,1:T(8,128)(2,1)S(1)} %get-tuple-element.45), channel_id=1, source_target_pairs={{0,1},{1,2},{2,3},{3,0},{4,5},{5,6},{6,7},{7,4},{8,9},{9,10},{10,1... | collective-permute-start | bytes 294920 | tf_op jit(solution)/shard_map/ppermute | solution.py:30
  83.1 4.7 %collective-permute-start.9 = (bf16[384,128]{0,1:T(8,128)(2,1)S(1)}, bf16[384,128]{0,1:T(8,128)(2,1)S(1)}, u32[]{:S(2)}, u32[]{:S(2)}) collective-permute-start(bf16[384,128]{0,1:T(8,128)(2,1)S(1)} %get-tuple-element.42), channel_id=1, source_target_pairs={{0,4},{1,5},{2,6},{3,7},{4,8},{5,9},{6,10},{7,11},{8,12},{9,13},{1... | collective-permute-start | bytes 294920 | tf_op jit(solution)/shard_map/ppermute | solution.py:30
  83.9 4.7 %collective-permute-start.8 = (bf16[384,128]{0,1:T(8,128)(2,1)S(1)}, bf16[384,128]{0,1:T(8,128)(2,1)S(1)}, u32[]{:S(2)}, u32[]{:S(2)}) collective-permute-start(bf16[384,128]{0,1:T(8,128)(2,1)S(1)} %get-tuple-element.42), channel_id=1, source_target_pairs={{0,12},{1,13},{2,14},{3,15},{4,0},{5,1},{6,2},{7,3},{8,4},{9,5},{1... | collective-permute-start | bytes 294920 | tf_op jit(solution)/shard_map/ppermute | solution.py:30
  87.8 5.7 %collective-permute-start.3 = (bf16[384,128]{0,1:T(8,128)(2,1)S(1)}, bf16[384,128]{0,1:T(8,128)(2,1)S(1)}, u32[]{:S(2)}, u32[]{:S(2)}) collective-permute-start(bf16[384,128]{0,1:T(8,128)(2,1)S(1)} %collective-permute-done.2), channel_id=1, source_target_pairs={{0,1},{1,2},{2,3},{3,0},{4,5},{5,6},{6,7},{7,4},{8,9},{9,10},{10,1... | collective-permute-start | bytes 294920 | tf_op jit(solution)/shard_map/ppermute | solution.py:30
  87.8 8.7 %collective-permute-start.10 = (bf16[384,128]{0,1:T(8,128)(2,1)S(1)}, bf16[384,128]{0,1:T(8,128)(2,1)S(1)}, u32[]{:S(2)}, u32[]{:S(2)}) collective-permute-start(bf16[384,128]{0,1:T(8,128)(2,1)S(1)} %collective-permute-done.9), channel_id=1, source_target_pairs={{0,4},{1,5},{2,6},{3,7},{4,8},{5,9},{6,10},{7,11},{8,12},{9,13},{1... | collective-permute-start | bytes 294920 | tf_op jit(solution)/shard_map/ppermute | solution.py:30
  93.6 14.6 %collective-permute-start.4 = (bf16[1536,128]{0,1:T(8,128)(2,1)S(1)}, bf16[1536,128]{0,1:T(8,128)(2,1)S(1)}, u32[]{:S(2)}, u32[]{:S(2)}) collective-permute-start(bf16[1536,128]{0,1:T(8,128)(2,1)S(1)} %pad_maximum_fusion), channel_id=1, source_target_pairs={{0,12},{1,13},{2,14},{3,15},{4,0},{5,1},{6,2},{7,3},{8,4},{9,5},{1... | collective-permute-start | bytes 1179656 | tf_op jit(solution)/shard_map/ppermute | solution.py:30
  96.5 11.5 %collective-permute-start.5 = (bf16[1536,128]{0,1:T(8,128)(2,1)S(1)}, bf16[1536,128]{0,1:T(8,128)(2,1)S(1)}, u32[]{:S(2)}, u32[]{:S(2)}) collective-permute-start(bf16[1536,128]{0,1:T(8,128)(2,1)S(1)} %pad_maximum_fusion), channel_id=1, source_target_pairs={{0,4},{1,5},{2,6},{3,7},{4,8},{5,9},{6,10},{7,11},{8,12},{9,13},{1... | collective-permute-start | bytes 1179656 | tf_op jit(solution)/shard_map/ppermute | solution.py:30
  96.5 15.1 %collective-permute-start.11 = (bf16[1536,128]{0,1:T(8,128)(2,1)S(1)}, bf16[1536,128]{0,1:T(8,128)(2,1)S(1)}, u32[]{:S(2)}, u32[]{:S(2)}) collective-permute-start(bf16[1536,128]{0,1:T(8,128)(2,1)S(1)} %pad_maximum_fusion.1), channel_id=1, source_target_pairs={{0,3},{1,0},{2,1},{3,2},{4,7},{5,4},{6,5},{7,6},{8,11},{9,8},{10,9... | collective-permute-start | bytes 1179656 | tf_op jit(solution)/shard_map/ppermute | solution.py:30
  96.6 14.2 %collective-permute-start.12 = (bf16[1536,128]{0,1:T(8,128)(2,1)S(1)}, bf16[1536,128]{0,1:T(8,128)(2,1)S(1)}, u32[]{:S(2)}, u32[]{:S(2)}) collective-permute-start(bf16[1536,128]{0,1:T(8,128)(2,1)S(1)} %pad_maximum_fusion.1), channel_id=1, source_target_pairs={{0,1},{1,2},{2,3},{3,0},{4,5},{5,6},{6,7},{7,4},{8,9},{9,10},{10,1... | collective-permute-start | bytes 1179656 | tf_op jit(solution)/shard_map/ppermute | solution.py:30
  108.0 7.8 %collective-permute-start.6 = (bf16[768,128]{0,1:T(8,128)(2,1)S(1)}, bf16[768,128]{0,1:T(8,128)(2,1)S(1)}, u32[]{:S(2)}, u32[]{:S(2)}) collective-permute-start(bf16[768,128]{0,1:T(8,128)(2,1)S(1)} %slice.175), channel_id=1, source_target_pairs={{0,4},{1,5},{2,6},{3,7},{4,8},{5,9},{6,10},{7,11},{8,12},{9,13},{1... | collective-permute-start | bytes 589832 | tf_op jit(solution)/shard_map/ppermute | solution.py:30
  108.2 7.7 %collective-permute-start.7 = (bf16[768,128]{0,1:T(8,128)(2,1)S(1)}, bf16[768,128]{0,1:T(8,128)(2,1)S(1)}, u32[]{:S(2)}, u32[]{:S(2)}) collective-permute-start(bf16[768,128]{0,1:T(8,128)(2,1)S(1)} %slice.176), channel_id=1, source_target_pairs={{0,12},{1,13},{2,14},{3,15},{4,0},{5,1},{6,2},{7,3},{8,4},{9,5},{1... | collective-permute-start | bytes 589832 | tf_op jit(solution)/shard_map/ppermute | solution.py:30
  110.9 1.4 copy-start.5
  111.6 5.9 %collective-permute-start.13 = (bf16[768,128]{0,1:T(8,128)(2,1)}, bf16[768,128]{0,1:T(8,128)(2,1)S(1)}, u32[]{:S(2)}, u32[]{:S(2)}) collective-permute-start(bf16[768,128]{0,1:T(8,128)(2,1)} %slice.178), channel_id=1, source_target_pairs={{0,1},{1,2},{2,3},{3,0},{4,5},{5,6},{6,7},{7,4},{8,9},{9,10},{10,1... | collective-permute-start | bytes 589832 | tf_op jit(solution)/shard_map/ppermute | solution.py:30
  112.3 6.0 %collective-permute-start.14 = (bf16[768,128]{0,1:T(8,128)(2,1)}, bf16[768,128]{0,1:T(8,128)(2,1)}, u32[]{:S(2)}, u32[]{:S(2)}) collective-permute-start(bf16[768,128]{0,1:T(8,128)(2,1)} %slice.179), channel_id=1, source_target_pairs={{0,3},{1,0},{2,1},{3,2},{4,7},{5,4},{6,5},{7,6},{8,11},{9,8},{10,9... | collective-permute-start | bytes 589832 | tf_op jit(solution)/shard_map/ppermute | solution.py:30
  123.7 1.4 copy-start
  129.7 11.4 %collective-permute-start.15 = (bf16[768,384]{1,0:T(8,128)(2,1)}, bf16[768,384]{1,0:T(8,128)(2,1)S(1)}, u32[]{:S(2)}, u32[]{:S(2)}) collective-permute-start(bf16[768,384]{1,0:T(8,128)(2,1)} %shard_map.85.mine_ref), channel_id=1, source_target_pairs={{0,128},{1,129},{2,130},{3,131},{4,132},{5,133},{6,134},{7,135},{8... | collective-permute-start | bytes 1769480 | tf_op jit(solution)/shard_map/ppermute | solution.py:30
  142.7 39.8 %copy-start.3 = (f32[768,384]{1,0:T(8,128)}, f32[768,384]{1,0:T(8,128)S(1)}, u32[]{:S(2)}) copy-start(f32[768,384]{1,0:T(8,128)S(1)} %get-tuple-element.7) | copy-start | bytes 3538948
  142.7 6.9 %collective-permute-start.16 = (bf16[96,384]{1,0:T(8,128)(2,1)S(1)}, bf16[96,384]{1,0:T(8,128)(2,1)S(1)}, u32[]{:S(2)}, u32[]{:S(2)}) collective-permute-start(bf16[96,384]{1,0:T(8,128)(2,1)S(1)} %get-tuple-element.49), channel_id=1, source_target_pairs={{0,3},{1,0},{2,1},{3,2},{4,7},{5,4},{6,5},{7,6},{8,11},{9,8},{10,9... | collective-permute-start | bytes 221192 | tf_op jit(solution)/shard_map/ppermute | solution.py:30
  145.2 4.4 %collective-permute-start.17 = (bf16[96,384]{1,0:T(8,128)(2,1)S(1)}, bf16[96,384]{1,0:T(8,128)(2,1)S(1)}, u32[]{:S(2)}, u32[]{:S(2)}) collective-permute-start(bf16[96,384]{1,0:T(8,128)(2,1)S(1)} %get-tuple-element.49), channel_id=1, source_target_pairs={{0,1},{1,2},{2,3},{3,0},{4,5},{5,6},{6,7},{7,4},{8,9},{9,10},{10,1... | collective-permute-start | bytes 221192 | tf_op jit(solution)/shard_map/ppermute | solution.py:30
  145.2 4.4 %collective-permute-start.24 = (bf16[96,384]{1,0:T(8,128)(2,1)S(1)}, bf16[96,384]{1,0:T(8,128)(2,1)S(1)}, u32[]{:S(2)}, u32[]{:S(2)}) collective-permute-start(bf16[96,384]{1,0:T(8,128)(2,1)S(1)} %get-tuple-element.46), channel_id=1, source_target_pairs={{0,4},{1,5},{2,6},{3,7},{4,8},{5,9},{6,10},{7,11},{8,12},{9,13},{1... | collective-permute-start | bytes 221192 | tf_op jit(solution)/shard_map/ppermute | solution.py:30
  145.2 4.5 %collective-permute-start.23 = (bf16[96,384]{1,0:T(8,128)(2,1)S(1)}, bf16[96,384]{1,0:T(8,128)(2,1)S(1)}, u32[]{:S(2)}, u32[]{:S(2)}) collective-permute-start(bf16[96,384]{1,0:T(8,128)(2,1)S(1)} %get-tuple-element.46), channel_id=1, source_target_pairs={{0,12},{1,13},{2,14},{3,15},{4,0},{5,1},{6,2},{7,3},{8,4},{9,5},{1... | collective-permute-start | bytes 221192 | tf_op jit(solution)/shard_map/ppermute | solution.py:30
  149.6 4.4 %collective-permute-start.18 = (bf16[96,384]{1,0:T(8,128)(2,1)S(1)}, bf16[96,384]{1,0:T(8,128)(2,1)S(1)}, u32[]{:S(2)}, u32[]{:S(2)}) collective-permute-start(bf16[96,384]{1,0:T(8,128)(2,1)S(1)} %collective-permute-done.17), channel_id=1, source_target_pairs={{0,1},{1,2},{2,3},{3,0},{4,5},{5,6},{6,7},{7,4},{8,9},{9,10},{10,1... | collective-permute-start | bytes 221192 | tf_op jit(solution)/shard_map/ppermute | solution.py:30
  149.6 6.0 %collective-permute-start.25 = (bf16[96,384]{1,0:T(8,128)(2,1)S(1)}, bf16[96,384]{1,0:T(8,128)(2,1)S(1)}, u32[]{:S(2)}, u32[]{:S(2)}) collective-permute-start(bf16[96,384]{1,0:T(8,128)(2,1)S(1)} %collective-permute-done.24), channel_id=1, source_target_pairs={{0,4},{1,5},{2,6},{3,7},{4,8},{5,9},{6,10},{7,11},{8,12},{9,13},{1... | collective-permute-start | bytes 221192 | tf_op jit(solution)/shard_map/ppermute | solution.py:30
  154.0 14.9 %collective-permute-start.19 = (bf16[384,384]{1,0:T(8,128)(2,1)S(1)}, bf16[384,384]{1,0:T(8,128)(2,1)S(1)}, u32[]{:S(2)}, u32[]{:S(2)}) collective-permute-start(bf16[384,384]{1,0:T(8,128)(2,1)S(1)} %pad_maximum_fusion.2), channel_id=1, source_target_pairs={{0,12},{1,13},{2,14},{3,15},{4,0},{5,1},{6,2},{7,3},{8,4},{9,5},{1... | collective-permute-start | bytes 884744 | tf_op jit(solution)/shard_map/ppermute | solution.py:30
  154.6 14.2 %collective-permute-start.20 = (bf16[384,384]{1,0:T(8,128)(2,1)S(1)}, bf16[384,384]{1,0:T(8,128)(2,1)S(1)}, u32[]{:S(2)}, u32[]{:S(2)}) collective-permute-start(bf16[384,384]{1,0:T(8,128)(2,1)S(1)} %pad_maximum_fusion.2), channel_id=1, source_target_pairs={{0,4},{1,5},{2,6},{3,7},{4,8},{5,9},{6,10},{7,11},{8,12},{9,13},{1... | collective-permute-start | bytes 884744 | tf_op jit(solution)/shard_map/ppermute | solution.py:30
  155.6 16.4 %collective-permute-start.26 = (bf16[384,384]{1,0:T(8,128)(2,1)S(1)}, bf16[384,384]{1,0:T(8,128)(2,1)S(1)}, u32[]{:S(2)}, u32[]{:S(2)}) collective-permute-start(bf16[384,384]{1,0:T(8,128)(2,1)S(1)} %pad_maximum_fusion.3), channel_id=1, source_target_pairs={{0,3},{1,0},{2,1},{3,2},{4,7},{5,4},{6,5},{7,6},{8,11},{9,8},{10,9... | collective-permute-start | bytes 884744 | tf_op jit(solution)/shard_map/ppermute | solution.py:30
  156.8 15.1 %collective-permute-start.27 = (bf16[384,384]{1,0:T(8,128)(2,1)S(1)}, bf16[384,384]{1,0:T(8,128)(2,1)S(1)}, u32[]{:S(2)}, u32[]{:S(2)}) collective-permute-start(bf16[384,384]{1,0:T(8,128)(2,1)S(1)} %pad_maximum_fusion.3), channel_id=1, source_target_pairs={{0,1},{1,2},{2,3},{3,0},{4,5},{5,6},{6,7},{7,4},{8,9},{9,10},{10,1... | collective-permute-start | bytes 884744 | tf_op jit(solution)/shard_map/ppermute | solution.py:30
  168.8 10.4 %collective-permute-start.21 = (bf16[192,384]{1,0:T(8,128)(2,1)S(1)}, bf16[192,384]{1,0:T(8,128)(2,1)S(1)}, u32[]{:S(2)}, u32[]{:S(2)}) collective-permute-start(bf16[192,384]{1,0:T(8,128)(2,1)S(1)} %slice.186), channel_id=1, source_target_pairs={{0,4},{1,5},{2,6},{3,7},{4,8},{5,9},{6,10},{7,11},{8,12},{9,13},{1... | collective-permute-start | bytes 442376 | tf_op jit(solution)/shard_map/ppermute | solution.py:30
  169.0 10.3 %collective-permute-start.22 = (bf16[192,384]{1,0:T(8,128)(2,1)S(1)}, bf16[192,384]{1,0:T(8,128)(2,1)S(1)}, u32[]{:S(2)}, u32[]{:S(2)}) collective-permute-start(bf16[192,384]{1,0:T(8,128)(2,1)S(1)} %slice.187), channel_id=1, source_target_pairs={{0,12},{1,13},{2,14},{3,15},{4,0},{5,1},{6,2},{7,3},{8,4},{9,5},{1... | collective-permute-start | bytes 442376 | tf_op jit(solution)/shard_map/ppermute | solution.py:30
  171.9 10.4 %collective-permute-start.28 = (bf16[192,384]{1,0:T(8,128)(2,1)S(1)}, bf16[192,384]{1,0:T(8,128)(2,1)S(1)}, u32[]{:S(2)}, u32[]{:S(2)}) collective-permute-start(bf16[192,384]{1,0:T(8,128)(2,1)S(1)} %slice.188), channel_id=1, source_target_pairs={{0,1},{1,2},{2,3},{3,0},{4,5},{5,6},{6,7},{7,4},{8,9},{9,10},{10,1... | collective-permute-start | bytes 442376 | tf_op jit(solution)/shard_map/ppermute | solution.py:30
  172.1 10.3 %collective-permute-start.29 = (bf16[192,384]{1,0:T(8,128)(2,1)S(1)}, bf16[192,384]{1,0:T(8,128)(2,1)S(1)}, u32[]{:S(2)}, u32[]{:S(2)}) collective-permute-start(bf16[192,384]{1,0:T(8,128)(2,1)S(1)} %slice.189), channel_id=1, source_target_pairs={{0,3},{1,0},{2,1},{3,2},{4,7},{5,4},{6,5},{7,6},{8,11},{9,8},{10,9... | collective-permute-start | bytes 442376 | tf_op jit(solution)/shard_map/ppermute | solution.py:30
  183.6 2.3 copy-start.2
  188.8 15.4 %collective-permute-start.32 = (bf16[256,384]{1,0:T(8,128)(2,1)S(1)}, bf16[256,384]{1,0:T(8,128)(2,1)S(1)}, u32[]{:S(2)}, u32[]{:S(2)}) collective-permute-start(bf16[256,384]{1,0:T(8,128)(2,1)S(1)} %get-tuple-element.10), channel_id=1, source_target_pairs={{0,32},{1,33},{2,34},{3,35},{4,36},{5,37},{6,38},{7,39},{8,40},{9,... | collective-permute-start | bytes 589832 | tf_op jit(solution)/shard_map/ppermute | solution.py:30
  201.5 7.1 %collective-permute-start.31 = (bf16[256,384]{1,0:T(8,128)(2,1)S(1)}, bf16[256,384]{1,0:T(8,128)(2,1)S(1)}, u32[]{:S(2)}, u32[]{:S(2)}) collective-permute-start(bf16[256,384]{1,0:T(8,128)(2,1)S(1)} %get-tuple-element.10), channel_id=1, source_target_pairs={{0,96},{1,97},{2,98},{3,99},{4,100},{5,101},{6,102},{7,103},{8,104... | collective-permute-start | bytes 589832 | tf_op jit(solution)/shard_map/ppermute | solution.py:30
  204.2 8.2 %collective-permute-start.33 = (bf16[128,384]{1,0:T(8,128)(2,1)S(1)}, bf16[128,384]{1,0:T(8,128)(2,1)S(1)}, u32[]{:S(2)}, u32[]{:S(2)}) collective-permute-start(bf16[128,384]{1,0:T(8,128)(2,1)S(1)} %slice.206), channel_id=1, source_target_pairs={{0,32},{1,33},{2,34},{3,35},{4,36},{5,37},{6,38},{7,39},{8,40},{9,... | collective-permute-start | bytes 294920 | tf_op jit(solution)/shard_map/ppermute | solution.py:30
  208.6 7.5 %collective-permute-start.34 = (bf16[128,384]{1,0:T(8,128)(2,1)S(1)}, bf16[128,384]{1,0:T(8,128)(2,1)S(1)}, u32[]{:S(2)}, u32[]{:S(2)}) collective-permute-start(bf16[128,384]{1,0:T(8,128)(2,1)S(1)} %slice.207), channel_id=1, source_target_pairs={{0,96},{1,97},{2,98},{3,99},{4,100},{5,101},{6,102},{7,103},{8,104... | collective-permute-start | bytes 294920 | tf_op jit(solution)/shard_map/ppermute | solution.py:30
  217.5 10.6 %collective-permute-start.35 = (bf16[1024,384]{1,0:T(8,128)(2,1)}, bf16[1024,384]{1,0:T(8,128)(2,1)}, u32[]{:S(2)}, u32[]{:S(2)}) collective-permute-start(bf16[1024,384]{1,0:T(8,128)(2,1)} %get-tuple-element.36), channel_id=1, source_target_pairs={{0,16},{1,17},{2,18},{3,19},{4,20},{5,21},{6,22},{7,23},{8,24},{9,... | collective-permute-start | bytes 2359304 | tf_op jit(solution)/shard_map/ppermute | solution.py:30
  (4 other events, 3.2 us)
Sparse Core Ops, SparseCore 0:
  10.0 56.3 all-gather.6
  68.8 48.0 all-gather.8
  119.3 74.9 all-gather.10

commit v2 on v1

--- a/solution.py
+++ b/solution.py
@@ -54,25 +54,19 @@
     return (h, q % N_ROW, q // N_ROW * N_ROW + (r ^ (q % N_ROW)))
 
 
-def ring_gather(own, along, split):
+def ring_parts(own, along, split):
     before = permute(own, along(1))
     after = permute(own, along(-1))
-    if split:
-        cut = own.shape[0] // 2
-        across = jnp.concatenate(
-            [permute(before[:cut], along(1)), permute(after[cut:], along(-1))], 0
-        )
-    else:
-        across = permute(before, along(1))
-    return jnp.concatenate([own, after, across, before], 0)
+    if not split:
+        return [own, after, permute(before, along(1)), before]
+    cut = own.shape[0] // 2
+    return [own, after, permute(before[:cut], along(1)), permute(after[cut:], along(-1)), before]
 
 
 def plane_gather(first, second):
-    one = ring_gather(first, along_x, False)
-    two = ring_gather(second, along_y, False)
-    one = ring_gather(one, along_y, True)
-    two = ring_gather(two, along_x, True)
-    return one.reshape(N_COL, *first.shape), two.reshape(N_COL, *second.shape)
+    one = jnp.stack(ring_parts(first, along_x, False))
+    two = jnp.stack(ring_parts(second, along_y, False))
+    return ring_parts(one, along_y, True), ring_parts(two, along_x, True)
 
 
 def dot(left, right):
@@ -87,7 +81,26 @@
     return jnp.concatenate(parts, axis)
 
 
-def root_kernel(slot_one, slot_two, one_ref, two_ref, right_ref, out_ref, acc):
+def load(pairs, sems):
+    copies = [pltpu.make_async_copy(src, dst, sems.at[i]) for i, (src, dst) in enumerate(pairs)]
+    for copy in copies:
+        copy.start()
+    for copy in copies:
+        copy.wait()
+
+
+def spread(parts, held):
+    at = 0
+    pairs = []
+    for part in parts:
+        pairs.append((part, held.at[pl.ds(at, part.shape[0])]))
+        at += part.shape[0]
+    return pairs
+
+
+def root_kernel(slot_one, slot_two, *refs):
+    parts, (right_in, out_ref, one_ref, two_ref, right_ref, acc, sems) = refs[:10], refs[10:]
+    load(spread(parts[:5], one_ref) + spread(parts[5:], two_ref) + [(right_in, right_ref)], sems)
     acc[...] = jnp.zeros_like(acc)
 
     def step(r, carry):
@@ -129,7 +142,10 @@
         ).astype(jnp.bfloat16)
 
 
-def offdiag_kernel(slot_one, slot_two, one_ref, two_ref, block_ref, out_ref, low_ref, acc):
+def offdiag_kernel(slot_one, slot_two, *refs):
+    parts, (right_in, out_ref, low_ref, one_ref, two_ref, block_ref, acc, sems) = refs[:10], refs[10:]
+    block_in = right_in.at[:, pl.ds(768, 768), :]
+    load(spread(parts[:5], one_ref) + spread(parts[5:], two_ref) + [(block_in, block_ref)], sems)
     acc[...] = jnp.zeros_like(acc)
 
     def step(r, carry):
@@ -152,7 +168,9 @@
     out_ref[...] = total.T
 
 
-def own_kernel(slots, left_ref, right_ref, out_ref, acc):
+def own_kernel(slots, left_in, right_in, out_ref, left_ref, right_ref, acc, sems):
+    first = pl.ds(0, 768)
+    load([(left_in.at[:, first, :], left_ref), (right_in.at[:, first, :], right_ref)], sems)
     acc[...] = jnp.zeros_like(acc)
 
     def step(r, carry):
@@ -171,8 +189,14 @@
     out_ref[...] = acc[...]
 
 
-def child_kernel(slots, part_slots, own_ref, left_ref, right_ref, out_ref, acc):
-    acc[...] = own_ref[...]
+def child_kernel(slots, part_slots, *refs):
+    parts, (own_in, left_in, out_ref, left_ref, right_ref, acc, sems) = refs[:10], refs[10:]
+    pairs = [(left_in.at[:, pl.ds(768, 768), :], left_ref), (own_in, acc)]
+    at = 0
+    for part in parts:
+        pairs.append((part, right_ref.at[at // 256, pl.ds(at % 256, part.shape[0]), :]))
+        at += part.shape[0]
+    load(pairs, sems)
 
     def step(r, carry):
         right = right_ref[part_slots[r]]
@@ -188,12 +212,12 @@
             out_ref[pl.ds((2 * outer + side) * BLK, BLK), :] = acc[side, pl.ds(outer * BLK, BLK), :]
 
 
-def call(kernel, scalars, arrays, outs, scratch=(), blocks=None):
+def call(kernel, scalars, arrays, outs, scratch, space=pl.ANY):
     vmem = pl.BlockSpec(memory_space=pltpu.VMEM)
     smem = pl.BlockSpec(memory_space=pltpu.SMEM)
     return pl.pallas_call(
         kernel,
-        in_specs=[smem] * len(scalars) + [vmem] * len(arrays),
+        in_specs=[smem] * len(scalars) + [pl.BlockSpec(memory_space=space)] * len(arrays),
         out_specs=[vmem] * len(outs),
         out_shape=[jax.ShapeDtypeStruct(*o) for o in outs],
         scratch_shapes=list(scratch),
@@ -227,11 +251,14 @@
 
     root_right = lax.all_gather(root_scaled, "row", axis=0, tiled=False)
     root_here = permute(root_turned, transposed_place)
-    child_here = permute(jnp.concatenate([child_turned, block_turned], 0), transposed_place)
+    child_stack = jnp.concatenate([child_turned, block_turned], 0)
+    root_here, child_stack = lax.optimization_barrier((root_here, child_stack))
+    child_here = permute(child_stack, transposed_place)
+    child_right = lax.all_gather(jnp.concatenate([child_scaled, block_sorted], 0), "row", axis=0, tiled=False)
+
+    root_parts = plane_gather(root_here[:384], root_here[384:])
+    child_here, root_parts = lax.optimization_barrier((child_here, root_parts))
     child_left = lax.all_gather(child_here, "col", axis=0, tiled=False)
-    child_right = lax.all_gather(jnp.concatenate([child_scaled, block_sorted], 0), "row", axis=0, tiled=False)
-
-    root_one, root_two = plane_gather(root_here[:384], root_here[384:])
 
     side = jnp.arange(2, dtype=jnp.int32)[:, None]
     classes = jnp.arange(N_ROW, dtype=jnp.int32)[None, :]
@@ -247,9 +274,15 @@
     (partial,) = call(
         root_kernel,
         root_slots,
-        (root_one, root_two, root_right),
+        (*root_parts[0], *root_parts[1], root_right),
         [((768, 384), bf16)],
-        [pltpu.VMEM((2, 384, 384), jnp.float32)],
+        [
+            pltpu.VMEM((N_COL, 384, BLK), bf16),
+            pltpu.VMEM((N_COL, 384, BLK), bf16),
+            pltpu.VMEM((N_ROW, 768, BLK), bf16),
+            pltpu.VMEM((2, 384, 384), jnp.float32),
+            pltpu.SemaphoreType.DMA((11,)),
+        ],
     )
     other = permute(partial, other_half)
     rows = child_rows[0].reshape(48, REACH) % BLK
@@ -260,35 +293,52 @@
         (),
         (partial, other, row_picks.reshape(-1, 1), col_picks.reshape(-1, 1)),
         [((768, 384), jnp.float32), ((192, 384), bf16)],
-    )
-    restricted_one, restricted_two = plane_gather(picked[:96], picked[96:])
+        (),
+        pltpu.VMEM,
+    )
+    picked_parts = plane_gather(picked[:96], picked[96:])
     offdiag_slots = plane_slots(side * N_ROW + classes)
     offdiag, offdiag_low = call(
         offdiag_kernel,
         offdiag_slots,
-        (restricted_one, restricted_two, child_right[:, 768:]),
+        (*picked_parts[0], *picked_parts[1], child_right),
         [((384, 256), jnp.float32), ((256, 384), bf16)],
-        [pltpu.VMEM((256, 384), jnp.float32)],
+        [
+            pltpu.VMEM((N_COL, 96, 384), bf16),
+            pltpu.VMEM((N_COL, 96, 384), bf16),
+            pltpu.VMEM((N_ROW, 768, BLK), bf16),
+            pltpu.VMEM((256, 384), jnp.float32),
+            pltpu.SemaphoreType.DMA((11,)),
+        ],
     )
     slots = source.reshape(-1)
     (own,) = call(
         own_kernel,
         (slots,),
-        (child_left[:, :768], child_right[:, :768]),
+        (child_left, child_right),
         [((2, 256, 256), jnp.float32)],
-        [pltpu.VMEM((2, 256, 256), jnp.float32)],
-    )
-    line = ring_gather(offdiag_low, along_z, True)
-    beside = permute(line, other_core)
-    parts = jnp.concatenate([line, beside], 0).reshape(N_ROW, 256, 384)
+        [
+            pltpu.VMEM((N_COL, 768, BLK), bf16),
+            pltpu.VMEM((N_ROW, 768, BLK), bf16),
+            pltpu.VMEM((2, 256, 256), jnp.float32),
+            pltpu.SemaphoreType.DMA((2,)),
+        ],
+    )
+    line = ring_parts(offdiag_low, along_z, True)
+    parts = line + [permute(part, other_core) for part in line]
     r = classes[0]
     part_slots = ((r ^ row) & 1) * SIDE + (r // 2 - row // 2) % SIDE
     (child_inverse,) = call(
         child_kernel,
         (slots, part_slots),
-        (own, child_left[:, 768:], parts),
+        (*parts, own, child_left),
         [((512, 256), jnp.float32)],
-        [pltpu.VMEM((2, 256, 256), jnp.float32)],
+        [
+            pltpu.VMEM((N_COL, 768, BLK), bf16),
+            pltpu.VMEM((N_ROW, 256, 384), bf16),
+            pltpu.VMEM((2, 256, 256), jnp.float32),
+            pltpu.SemaphoreType.DMA((12,)),
+        ],
     )
     return (
         root_inverse.reshape(6, 1, BLK, 3, 1, BLK),

time: 247 us -> 238 us (0.964)
  waiting for transfers between devices: 65.5 us -> 49 us
  starting transfers between devices: 110 us -> 118 us
  local copies, waits for them, and re-layouts: 37.2 us -> 30.5 us
  Pallas kernels: 15.1 us -> 21.6 us
    ppermute x36 -> x40, waiting for transfers between devices: 65.3 us -> 49 us  [permute(): return lax.ppermute(array, AXES, pairs)]
    ppermute x36 -> x40, starting transfers between devices: 110 us -> 118 us  [permute(): return lax.ppermute(array, AXES, pairs)]
    pallas_call x5, Pallas kernels: 15.1 us -> 21.6 us  [call(): pl.pallas_call(kernel, in_specs=[smem] * len(scalars) + [pl.BlockSpec(mem...]
    concatenate x9 -> x1, local copies, waits for them, and re-layouts: 6.82 us -> 0.69 us  [per_device(): child_stack = jnp.concatenate([child_turned, block_turned], 0)]
    slice x14 -> x10, local copies, waits for them, and re-layouts: 7.86 us -> 3.05 us  [the longest x5 1.56 us: ring_parts(): before[:cut]]
    unnamed x80 -> x75, local copies, waits for them, and re-layouts: 14.5 us -> 15.8 us
  transfers between devices with their start and end apart: 39 -> 43, of which waited for: 16 -> 12; matrix products, arithmetic and copies ran while one was open for 12% -> 9% of each run, Pallas kernels for 4% -> 7%
where the time goes in v2:
time: 238 us
  starting transfers between devices  118 us (50%)
  waiting for transfers between devices  49 us (21%)
  local copies, waits for them, and re-layouts  30.5 us (13%)
  Pallas kernels  21.6 us (9%)
  between operations  14.4 us (6%)
  other arithmetic  3.75 us (2%)
    ppermute x40, starting transfers between devices, permute(): return lax.ppermute(array, AXES, pairs)  118 us
    ppermute x40, waiting for transfers between devices, permute(): return lax.ppermute(array, AXES, pairs)  49 us
    pallas_call x5, Pallas kernels, call(): pl.pallas_call(kernel, in_specs=[smem] * len(scalars) + [pl.BlockSpec(mem...  21.6 us
    unnamed x75, local copies, waits for them, and re-layouts  15.8 us
  transfers between devices with their start and end apart: 43, of which 12 were waited for; matrix products, arithmetic and copies ran while one was open for 9% of the time, Pallas kernels for 7%

profile of v2, /device:TPU:1, one launch (start us, length us, event | category | flops | bytes accessed | tf_op | source)
XLA Modules:
  0.0 237.6 jit_solution(1762477693498048897)
XLA Ops:
  7.2 1.2 copy.49
  12.5 4.5 %collective-permute-start = (bf16[768,128]{1,0:T(8,128)(2,1)S(1)}, bf16[768,128]{1,0:T(8,128)(2,1)S(1)}, u32[]{:S(2)}, u32[]{:S(2)}) collective-permute-start(bf16[768,128]{1,0:T(8,128)(2,1)S(1)} %constant_dynamic-update-slice_fusion), channel_id=1, source_target_pairs={{0,0},{1,17},{2,34},{3,51},{4,68},{5,85},{6,102},{7,119},{8,8},{9,... | collective-permute-start | bytes 589832 | tf_op jit(solution)/shard_map/ppermute | solution.py:30
  21.8 9.2 %collective-permute-start.10 = (bf16[384,128]{1,0:T(8,128)(2,1)S(1)}, bf16[384,128]{1,0:T(8,128)(2,1)S(1)}, u32[]{:S(2)}, u32[]{:S(2)}) collective-permute-start(bf16[384,128]{1,0:T(8,128)(2,1)S(1)} %get-tuple-element.60), channel_id=1, source_target_pairs={{0,4},{1,5},{2,6},{3,7},{4,8},{5,9},{6,10},{7,11},{8,12},{9,13},{1... | collective-permute-start | bytes 294920 | tf_op jit(solution)/shard_map/ppermute | solution.py:30
  31.0 15.3 %collective-permute-start.2 = (bf16[384,128]{1,0:T(8,128)(2,1)S(1)}, bf16[384,128]{1,0:T(8,128)(2,1)S(1)}, u32[]{:S(2)}, u32[]{:S(2)}) collective-permute-start(bf16[384,128]{1,0:T(8,128)(2,1)S(1)} %get-tuple-element.61), channel_id=1, source_target_pairs={{0,3},{1,0},{2,1},{3,2},{4,7},{5,4},{6,5},{7,6},{8,11},{9,8},{10,9... | collective-permute-start | bytes 294920 | tf_op jit(solution)/shard_map/ppermute | solution.py:30
  46.2 2.5 %collective-permute-start.4 = (bf16[384,128]{1,0:T(8,128)(2,1)S(1)}, bf16[384,128]{1,0:T(8,128)(2,1)S(1)}, u32[]{:S(2)}, u32[]{:S(2)}) collective-permute-start(bf16[384,128]{1,0:T(8,128)(2,1)S(1)} %collective-permute-done.3), channel_id=1, source_target_pairs={{0,1},{1,2},{2,3},{3,0},{4,5},{5,6},{6,7},{7,4},{8,9},{9,10},{10,1... | collective-permute-start | bytes 294920 | tf_op jit(solution)/shard_map/ppermute | solution.py:30
  48.7 3.2 %collective-permute-start.9 = (bf16[384,128]{1,0:T(8,128)(2,1)S(1)}, bf16[384,128]{1,0:T(8,128)(2,1)S(1)}, u32[]{:S(2)}, u32[]{:S(2)}) collective-permute-start(bf16[384,128]{1,0:T(8,128)(2,1)S(1)} %get-tuple-element.60), channel_id=1, source_target_pairs={{0,12},{1,13},{2,14},{3,15},{4,0},{5,1},{6,2},{7,3},{8,4},{9,5},{1... | collective-permute-start | bytes 294920 | tf_op jit(solution)/shard_map/ppermute | solution.py:30
  52.1 2.7 %collective-permute-start.5 = (bf16[4,384,128]{2,1,0:T(8,128)(2,1)S(1)}, bf16[4,384,128]{2,1,0:T(8,128)(2,1)S(1)}, u32[]{:S(2)}, u32[]{:S(2)}) collective-permute-start(bf16[4,384,128]{2,1,0:T(8,128)(2,1)S(1)} %pad_maximum_fusion.refs_0_), channel_id=1, source_target_pairs={{0,12},{1,13},{2,14},{3,15},{4,0},{5,1},{6,2},{7,3},{8,4},{9,5},{1... | collective-permute-start | bytes 1179656 | tf_op jit(solution)/shard_map/ppermute | solution.py:30
  54.8 1.8 collective-permute-done.11
  56.7 2.4 %collective-permute-start.13 = (bf16[4,384,128]{2,1,0:T(8,128)(2,1)S(1)}, bf16[4,384,128]{2,1,0:T(8,128)(2,1)S(1)}, u32[]{:S(2)}, u32[]{:S(2)}) collective-permute-start(bf16[4,384,128]{2,1,0:T(8,128)(2,1)S(1)} %pad_maximum_fusion.1.refs_5_), channel_id=1, source_target_pairs={{0,1},{1,2},{2,3},{3,0},{4,5},{5,6},{6,7},{7,4},{8,9},{9,10},{10,1... | collective-permute-start | bytes 1179656 | tf_op jit(solution)/shard_map/ppermute | solution.py:30
  59.5 5.7 %collective-permute-start.1 = (bf16[1536,128]{1,0:T(8,128)(2,1)}, bf16[1536,128]{1,0:T(8,128)(2,1)S(1)}, u32[]{:S(2)}, u32[]{:S(2)}) collective-permute-start(bf16[1536,128]{1,0:T(8,128)(2,1)} %constant_dynamic-update-slice_fusion.6), channel_id=1, source_target_pairs={{0,0},{1,17},{2,34},{3,51},{4,68},{5,85},{6,102},{7,119},{8,8},{9,... | collective-permute-start | bytes 1179656 | tf_op jit(solution)/shard_map/ppermute | solution.py:30
  66.0 7.4 %collective-permute-start.7 = (bf16[2,384,128]{2,1,0:T(8,128)(2,1)}, bf16[2,384,128]{2,1,0:T(8,128)(2,1)S(1)}, u32[]{:S(2)}, u32[]{:S(2)}) collective-permute-start(bf16[2,384,128]{2,1,0:T(8,128)(2,1)} %slice.164), channel_id=1, source_target_pairs={{0,4},{1,5},{2,6},{3,7},{4,8},{5,9},{6,10},{7,11},{8,12},{9,13},{1... | collective-permute-start | bytes 589832 | tf_op jit(solution)/shard_map/ppermute | solution.py:30
  74.0 1.7 collective-permute-start.8
  77.3 2.7 %collective-permute-start.15 = (bf16[2,384,128]{2,1,0:T(8,128)(2,1)}, bf16[2,384,128]{2,1,0:T(8,128)(2,1)S(1)}, u32[]{:S(2)}, u32[]{:S(2)}) collective-permute-start(bf16[2,384,128]{2,1,0:T(8,128)(2,1)} %slice.167), channel_id=1, source_target_pairs={{0,3},{1,0},{2,1},{3,2},{4,7},{5,4},{6,5},{7,6},{8,11},{9,8},{10,9... | collective-permute-start | bytes 589832 | tf_op jit(solution)/shard_map/ppermute | solution.py:30
  79.9 1.1 collective-permute-done.1
  81.1 2.9 %collective-permute-done.14.refs_7_ = bf16[2,384,128]{2,1,0:T(8,128)(2,1)S(1)} collective-permute-done((bf16[2,384,128]{2,1,0:T(8,128)(2,1)}, bf16[2,384,128]{2,1,0:T(8,128)(2,1)S(1)}, u32[]{:S(2)}, u32[]{:S(2)}) %collective-permute-start.14) | collective-permute-done | bytes 196640 | tf_op jit(solution)/shard_map/ppermute | solution.py:30
  84.0 2.4 %collective-permute-done.15.refs_8_ = bf16[2,384,128]{2,1,0:T(8,128)(2,1)S(1)} collective-permute-done((bf16[2,384,128]{2,1,0:T(8,128)(2,1)}, bf16[2,384,128]{2,1,0:T(8,128)(2,1)S(1)}, u32[]{:S(2)}, u32[]{:S(2)}) %collective-permute-start.15) | collective-permute-done | bytes 196640 | tf_op jit(solution)/shard_map/ppermute | solution.py:30
  89.9 1.9 copy.52
  92.9 1.0 copy-done.6
  93.9 1.0 copy-done.8
  97.7 6.1 %shard_map.85.mine_ref = bf16[768,384]{1,0:T(8,128)(2,1)S(1)} custom-call(s32[16]{0:T(128)S(1)} %multiply_add_fusion.3.slot_one, s32[16]{0:T(128)S(1)} %get-tuple-element.49.slot_two, bf16[4,384,128]{2,1,0:T(8,128)(2,1)S(1)} %pad_maximum_fusion.refs_0_, bf16[4,384,128]{2,1,0:T(8,128)(2,1)S(1)} %collective-permute-done.5.refs_1_, ...), custom_call_target="tpu_custom_call" | custom-call | tf_op jit(solution)/shard_map/pallas_call | solution.py:218
  105.8 20.6 %collective-permute-done.16.other_ref = bf16[768,384]{1,0:T(8,128)(2,1)S(1)} collective-permute-done((bf16[768,384]{1,0:T(8,128)(2,1)S(1)}, bf16[768,384]{1,0:T(8,128)(2,1)S(1)}, u32[]{:S(2)}, u32[]{:S(2)}) %collective-permute-start.16) | collective-permute-done | bytes 589856 | tf_op jit(solution)/shard_map/ppermute | solution.py:30
  127.0 8.4 %collective-permute-start.25 = (bf16[96,384]{1,0:T(8,128)(2,1)S(1)}, bf16[96,384]{1,0:T(8,128)(2,1)S(1)}, u32[]{:S(2)}, u32[]{:S(2)}) collective-permute-start(bf16[96,384]{1,0:T(8,128)(2,1)S(1)} %get-tuple-element.64), channel_id=1, source_target_pairs={{0,4},{1,5},{2,6},{3,7},{4,8},{5,9},{6,10},{7,11},{8,12},{9,13},{1... | collective-permute-start | bytes 221192 | tf_op jit(solution)/shard_map/ppermute | solution.py:30
  135.4 12.2 %collective-permute-start.17 = (bf16[96,384]{1,0:T(8,128)(2,1)S(1)}, bf16[96,384]{1,0:T(8,128)(2,1)S(1)}, u32[]{:S(2)}, u32[]{:S(2)}) collective-permute-start(bf16[96,384]{1,0:T(8,128)(2,1)S(1)} %get-tuple-element.65), channel_id=1, source_target_pairs={{0,3},{1,0},{2,1},{3,2},{4,7},{5,4},{6,5},{7,6},{8,11},{9,8},{10,9... | collective-permute-start | bytes 221192 | tf_op jit(solution)/shard_map/ppermute | solution.py:30
  147.6 3.6 %collective-permute-start.19 = (bf16[96,384]{1,0:T(8,128)(2,1)S(1)}, bf16[96,384]{1,0:T(8,128)(2,1)S(1)}, u32[]{:S(2)}, u32[]{:S(2)}) collective-permute-start(bf16[96,384]{1,0:T(8,128)(2,1)S(1)} %collective-permute-done.18), channel_id=1, source_target_pairs={{0,1},{1,2},{2,3},{3,0},{4,5},{5,6},{6,7},{7,4},{8,9},{9,10},{10,1... | collective-permute-start | bytes 221192 | tf_op jit(solution)/shard_map/ppermute | solution.py:30
  151.3 2.6 %collective-permute-start.24 = (bf16[96,384]{1,0:T(8,128)(2,1)S(1)}, bf16[96,384]{1,0:T(8,128)(2,1)S(1)}, u32[]{:S(2)}, u32[]{:S(2)}) collective-permute-start(bf16[96,384]{1,0:T(8,128)(2,1)S(1)} %get-tuple-element.64), channel_id=1, source_target_pairs={{0,12},{1,13},{2,14},{3,15},{4,0},{5,1},{6,2},{7,3},{8,4},{9,5},{1... | collective-permute-start | bytes 221192 | tf_op jit(solution)/shard_map/ppermute | solution.py:30
  153.9 1.0 collective-permute-done.19
  155.0 2.0 collective-permute-start.20
  157.0 1.3 collective-permute-done.26
  158.3 2.4 %collective-permute-start.28 = (bf16[4,96,384]{2,1,0:T(8,128)(2,1)S(1)}, bf16[4,96,384]{2,1,0:T(8,128)(2,1)S(1)}, u32[]{:S(2)}, u32[]{:S(2)}) collective-permute-start(bf16[4,96,384]{2,1,0:T(8,128)(2,1)S(1)} %pad_maximum_fusion.3.refs_5_), channel_id=1, source_target_pairs={{0,1},{1,2},{2,3},{3,0},{4,5},{5,6},{6,7},{7,4},{8,9},{9,10},{10,1... | collective-permute-start | bytes 884744 | tf_op jit(solution)/shard_map/ppermute | solution.py:30
  161.2 3.4 %collective-permute-done.21.refs_4_ = bf16[4,96,384]{2,1,0:T(8,128)(2,1)S(1)} collective-permute-done((bf16[4,96,384]{2,1,0:T(8,128)(2,1)S(1)}, bf16[4,96,384]{2,1,0:T(8,128)(2,1)S(1)}, u32[]{:S(2)}, u32[]{:S(2)}) %collective-permute-start.21) | collective-permute-done | bytes 294944 | tf_op jit(solution)/shard_map/ppermute | solution.py:30
  164.7 2.7 %collective-permute-start.23 = (bf16[2,96,384]{2,1,0:T(8,128)(2,1)S(1)}, bf16[2,96,384]{2,1,0:T(8,128)(2,1)S(1)}, u32[]{:S(2)}, u32[]{:S(2)}) collective-permute-start(bf16[2,96,384]{2,1,0:T(8,128)(2,1)S(1)} %slice.175), channel_id=1, source_target_pairs={{0,12},{1,13},{2,14},{3,15},{4,0},{5,1},{6,2},{7,3},{8,4},{9,5},{1... | collective-permute-start | bytes 442376 | tf_op jit(solution)/shard_map/ppermute | solution.py:30
  167.5 2.8 %collective-permute-start.29 = (bf16[2,96,384]{2,1,0:T(8,128)(2,1)S(1)}, bf16[2,96,384]{2,1,0:T(8,128)(2,1)S(1)}, u32[]{:S(2)}, u32[]{:S(2)}) collective-permute-start(bf16[2,96,384]{2,1,0:T(8,128)(2,1)S(1)} %slice.176), channel_id=1, source_target_pairs={{0,1},{1,2},{2,3},{3,0},{4,5},{5,6},{6,7},{7,4},{8,9},{9,10},{10,1... | collective-permute-start | bytes 442376 | tf_op jit(solution)/shard_map/ppermute | solution.py:30
  170.5 3.6 %collective-permute-done.22.refs_2_ = bf16[2,96,384]{2,1,0:T(8,128)(2,1)S(1)} collective-permute-done((bf16[2,96,384]{2,1,0:T(8,128)(2,1)S(1)}, bf16[2,96,384]{2,1,0:T(8,128)(2,1)S(1)}, u32[]{:S(2)}, u32[]{:S(2)}) %collective-permute-start.22) | collective-permute-done | bytes 147488 | tf_op jit(solution)/shard_map/ppermute | solution.py:30
  174.2 3.9 %collective-permute-done.29.refs_7_ = bf16[2,96,384]{2,1,0:T(8,128)(2,1)S(1)} collective-permute-done((bf16[2,96,384]{2,1,0:T(8,128)(2,1)S(1)}, bf16[2,96,384]{2,1,0:T(8,128)(2,1)S(1)}, u32[]{:S(2)}, u32[]{:S(2)}) %collective-permute-start.29) | collective-permute-done | bytes 147488 | tf_op jit(solution)/shard_map/ppermute | solution.py:30
  178.1 1.4 collective-permute-done.30.refs_8_
  179.4 1.9 copy-done
  181.4 4.8 %shard_map.87 = (f32[384,256]{1,0:T(8,128)S(1)}, bf16[256,384]{1,0:T(8,128)(2,1)}) custom-call(s32[16]{0:T(128)S(1)} %multiply_add_fusion.1.slot_one, s32[16]{0:T(128)S(1)} %get-tuple-element.46.slot_two, bf16[4,96,384]{2,1,0:T(8,128)(2,1)S(1)} %pad_maximum_fusion.2.refs_0_, bf16[4,96,384]{2,1,0:T(8,128)(2,1)S(1)} %collective-permute-done.20.refs_1_, ...), custom_call_target="tpu_custom_call" | custom-call | tf_op jit(solution)/shard_map/pallas_call | solution.py:218
  186.2 1.2 collective-permute-start.32
  187.4 2.4 %collective-permute-start.31 = (bf16[256,384]{1,0:T(8,128)(2,1)}, bf16[256,384]{1,0:T(8,128)(2,1)S(1)}, u32[]{:S(2)}, u32[]{:S(2)}) collective-permute-start(bf16[256,384]{1,0:T(8,128)(2,1)} %get-tuple-element.35.refs_0_), channel_id=1, source_target_pairs={{0,96},{1,97},{2,98},{3,99},{4,100},{5,101},{6,102},{7,103},{8,104... | collective-permute-start | bytes 589832 | tf_op jit(solution)/shard_map/ppermute | solution.py:30
  189.8 5.4 %collective-permute-done.32.refs_4_ = bf16[256,384]{1,0:T(8,128)(2,1)S(1)} collective-permute-done((bf16[256,384]{1,0:T(8,128)(2,1)}, bf16[256,384]{1,0:T(8,128)(2,1)S(1)}, u32[]{:S(2)}, u32[]{:S(2)}) %collective-permute-start.32) | collective-permute-done | bytes 196640 | tf_op jit(solution)/shard_map/ppermute | solution.py:30
  195.6 3.4 %collective-permute-start.34 = (bf16[128,384]{1,0:T(8,128)(2,1)S(1)}, bf16[128,384]{1,0:T(8,128)(2,1)}, u32[]{:S(2)}, u32[]{:S(2)}) collective-permute-start(bf16[128,384]{1,0:T(8,128)(2,1)S(1)} %slice.185), channel_id=1, source_target_pairs={{0,96},{1,97},{2,98},{3,99},{4,100},{5,101},{6,102},{7,103},{8,104... | collective-permute-start | bytes 294920 | tf_op jit(solution)/shard_map/ppermute | solution.py:30
  199.0 12.7 %collective-permute-start.35 = (bf16[256,384]{1,0:T(8,128)(2,1)}, bf16[256,384]{1,0:T(8,128)(2,1)}, u32[]{:S(2)}, u32[]{:S(2)}) collective-permute-start(bf16[256,384]{1,0:T(8,128)(2,1)} %get-tuple-element.35.refs_0_), channel_id=1, source_target_pairs={{0,16},{1,17},{2,18},{3,19},{4,20},{5,21},{6,22},{7,23},{8,24},{9,... | collective-permute-start | bytes 589832 | tf_op jit(solution)/shard_map/ppermute | solution.py:30
  212.2 2.1 collective-permute-start.37
  214.4 3.4 %reshape.101 = f32[6,1,128,3,1,128]{5,4,3,2,1,0:T(1,128)} reshape(f32[768,384]{1,0:T(8,128)} %copy-done.2) | data formatting | bytes 2359296 | tf_op jit(solution)/shard_map/reshape | solution.py:344
  217.8 1.9 reshape.93
  219.7 4.6 %shard_map.88.refs_10_ = f32[2,256,256]{2,1,0:T(8,128)S(1)} custom-call(s32[16]{0:T(128)S(1)} %add.142.slots, bf16[16,1536,128]{2,1,0:T(8,128)(2,1)} %bitcast.152, bf16[8,1536,128]{2,1,0:T(8,128)(2,1)S(1)} %bitcast.150), custom_call_target="tpu_custom_call" | custom-call | tf_op jit(solution)/shard_map/pallas_call | solution.py:218
  224.4 5.6 %shard_map.89 = f32[512,256]{1,0:T(8,128)S(1)} custom-call(s32[16]{0:T(128)S(1)} %add.142.slots, s32[8]{0:T(128)S(1)} %fusion.part_slots, bf16[256,384]{1,0:T(8,128)(2,1)} %get-tuple-element.35.refs_0_, bf16[256,384]{1,0:T(8,128)(2,1)S(1)} %collective-permute-done.31.refs_1_, bf16[128,384]{1,0:T(8,128)(2,1)} %collective-permute-done.33.refs_2_, ...), custom_call_target="tpu_custom_call" | custom-call | tf_op jit(solution)/shard_map/pallas_call | solution.py:218
  230.0 1.1 reshape.94
  (179 shorter events, 23.8 us)
Async XLA Ops:
  7.2 82.7 %all-gather.7.cloned.1.call-start = ((), (), s32[]{:S(2)}) async-start(), calls=%async_computation | async-start | bytes 1769472 | tf_op jit(solution)/shard_map/all_gather | solution.py:252
  10.1 169.4 %all-gather.9.cloned.1.call-start = ((), (), s32[]{:S(2)}) async-start(), calls=%async_computation.1 | async-start | bytes 3538944 | tf_op jit(solution)/shard_map/all_gather | solution.py:257
  12.4 207.3 %all-gather.11.cloned.1.call-start = ((), (), s32[]{:S(2)}) async-start(), calls=%async_computation.2 | async-start | bytes 6684672 | tf_op jit(solution)/shard_map/all_gather | solution.py:261
  12.5 9.1 %collective-permute-start = (bf16[768,128]{1,0:T(8,128)(2,1)S(1)}, bf16[768,128]{1,0:T(8,128)(2,1)S(1)}, u32[]{:S(2)}, u32[]{:S(2)}) collective-permute-start(bf16[768,128]{1,0:T(8,128)(2,1)S(1)} %constant_dynamic-update-slice_fusion), channel_id=1, source_target_pairs={{0,0},{1,17},{2,34},{3,51},{4,68},{5,85},{6,102},{7,119},{8,8},{9,... | collective-permute-start | bytes 589832 | tf_op jit(solution)/shard_map/ppermute | solution.py:30
  21.7 24.6 %collective-permute-start.3 = (bf16[384,128]{1,0:T(8,128)(2,1)S(1)}, bf16[384,128]{1,0:T(8,128)(2,1)S(1)}, u32[]{:S(2)}, u32[]{:S(2)}) collective-permute-start(bf16[384,128]{1,0:T(8,128)(2,1)S(1)} %get-tuple-element.61), channel_id=1, source_target_pairs={{0,1},{1,2},{2,3},{3,0},{4,5},{5,6},{6,7},{7,4},{8,9},{9,10},{10,1... | collective-permute-start | bytes 294920 | tf_op jit(solution)/shard_map/ppermute | solution.py:30
  21.8 30.2 %collective-permute-start.10 = (bf16[384,128]{1,0:T(8,128)(2,1)S(1)}, bf16[384,128]{1,0:T(8,128)(2,1)S(1)}, u32[]{:S(2)}, u32[]{:S(2)}) collective-permute-start(bf16[384,128]{1,0:T(8,128)(2,1)S(1)} %get-tuple-element.60), channel_id=1, source_target_pairs={{0,4},{1,5},{2,6},{3,7},{4,8},{5,9},{6,10},{7,11},{8,12},{9,13},{1... | collective-permute-start | bytes 294920 | tf_op jit(solution)/shard_map/ppermute | solution.py:30
  31.0 21.0 %collective-permute-start.2 = (bf16[384,128]{1,0:T(8,128)(2,1)S(1)}, bf16[384,128]{1,0:T(8,128)(2,1)S(1)}, u32[]{:S(2)}, u32[]{:S(2)}) collective-permute-start(bf16[384,128]{1,0:T(8,128)(2,1)S(1)} %get-tuple-element.61), channel_id=1, source_target_pairs={{0,3},{1,0},{2,1},{3,2},{4,7},{5,4},{6,5},{7,6},{8,11},{9,8},{10,9... | collective-permute-start | bytes 294920 | tf_op jit(solution)/shard_map/ppermute | solution.py:30
  46.2 5.7 %collective-permute-start.4 = (bf16[384,128]{1,0:T(8,128)(2,1)S(1)}, bf16[384,128]{1,0:T(8,128)(2,1)S(1)}, u32[]{:S(2)}, u32[]{:S(2)}) collective-permute-start(bf16[384,128]{1,0:T(8,128)(2,1)S(1)} %collective-permute-done.3), channel_id=1, source_target_pairs={{0,1},{1,2},{2,3},{3,0},{4,5},{5,6},{6,7},{7,4},{8,9},{9,10},{10,1... | collective-permute-start | bytes 294920 | tf_op jit(solution)/shard_map/ppermute | solution.py:30
  48.7 6.1 %collective-permute-start.9 = (bf16[384,128]{1,0:T(8,128)(2,1)S(1)}, bf16[384,128]{1,0:T(8,128)(2,1)S(1)}, u32[]{:S(2)}, u32[]{:S(2)}) collective-permute-start(bf16[384,128]{1,0:T(8,128)(2,1)S(1)} %get-tuple-element.60), channel_id=1, source_target_pairs={{0,12},{1,13},{2,14},{3,15},{4,0},{5,1},{6,2},{7,3},{8,4},{9,5},{1... | collective-permute-start | bytes 294920 | tf_op jit(solution)/shard_map/ppermute | solution.py:30
  52.0 4.7 %collective-permute-start.11 = (bf16[384,128]{1,0:T(8,128)(2,1)S(1)}, bf16[384,128]{1,0:T(8,128)(2,1)S(1)}, u32[]{:S(2)}, u32[]{:S(2)}) collective-permute-start(bf16[384,128]{1,0:T(8,128)(2,1)S(1)} %collective-permute-done.10), channel_id=1, source_target_pairs={{0,4},{1,5},{2,6},{3,7},{4,8},{5,9},{6,10},{7,11},{8,12},{9,13},{1... | collective-permute-start | bytes 294920 | tf_op jit(solution)/shard_map/ppermute | solution.py:30
  52.1 35.8 %copy-start.21 = (s32[1,3072]{1,0:T(1,128)S(1)}, s32[1,3072]{1,0:T(1,128)}, u32[]{:S(2)}) copy-start(s32[1,3072]{1,0:T(1,128)} %param.11) | copy-start | bytes 36868
  52.1 21.3 %collective-permute-start.5 = (bf16[4,384,128]{2,1,0:T(8,128)(2,1)S(1)}, bf16[4,384,128]{2,1,0:T(8,128)(2,1)S(1)}, u32[]{:S(2)}, u32[]{:S(2)}) collective-permute-start(bf16[4,384,128]{2,1,0:T(8,128)(2,1)S(1)} %pad_maximum_fusion.refs_0_), channel_id=1, source_target_pairs={{0,12},{1,13},{2,14},{3,15},{4,0},{5,1},{6,2},{7,3},{8,4},{9,5},{1... | collective-permute-start | bytes 1179656 | tf_op jit(solution)/shard_map/ppermute | solution.py:30
  54.8 10.4 %collective-permute-start.6 = (bf16[4,384,128]{2,1,0:T(8,128)(2,1)S(1)}, bf16[4,384,128]{2,1,0:T(8,128)(2,1)S(1)}, u32[]{:S(2)}, u32[]{:S(2)}) collective-permute-start(bf16[4,384,128]{2,1,0:T(8,128)(2,1)S(1)} %pad_maximum_fusion.refs_0_), channel_id=1, source_target_pairs={{0,4},{1,5},{2,6},{3,7},{4,8},{5,9},{6,10},{7,11},{8,12},{9,13},{1... | collective-permute-start | bytes 1179656 | tf_op jit(solution)/shard_map/ppermute | solution.py:30
  56.7 19.1 %collective-permute-start.13 = (bf16[4,384,128]{2,1,0:T(8,128)(2,1)S(1)}, bf16[4,384,128]{2,1,0:T(8,128)(2,1)S(1)}, u32[]{:S(2)}, u32[]{:S(2)}) collective-permute-start(bf16[4,384,128]{2,1,0:T(8,128)(2,1)S(1)} %pad_maximum_fusion.1.refs_5_), channel_id=1, source_target_pairs={{0,1},{1,2},{2,3},{3,0},{4,5},{5,6},{6,7},{7,4},{8,9},{9,10},{10,1... | collective-permute-start | bytes 1179656 | tf_op jit(solution)/shard_map/ppermute | solution.py:30
  59.1 17.4 %collective-permute-start.12 = (bf16[4,384,128]{2,1,0:T(8,128)(2,1)S(1)}, bf16[4,384,128]{2,1,0:T(8,128)(2,1)S(1)}, u32[]{:S(2)}, u32[]{:S(2)}) collective-permute-start(bf16[4,384,128]{2,1,0:T(8,128)(2,1)S(1)} %pad_maximum_fusion.1.refs_5_), channel_id=1, source_target_pairs={{0,3},{1,0},{2,1},{3,2},{4,7},{5,4},{6,5},{7,6},{8,11},{9,8},{10,9... | collective-permute-start | bytes 1179656 | tf_op jit(solution)/shard_map/ppermute | solution.py:30
  59.5 21.6 %collective-permute-start.1 = (bf16[1536,128]{1,0:T(8,128)(2,1)}, bf16[1536,128]{1,0:T(8,128)(2,1)S(1)}, u32[]{:S(2)}, u32[]{:S(2)}) collective-permute-start(bf16[1536,128]{1,0:T(8,128)(2,1)} %constant_dynamic-update-slice_fusion.6), channel_id=1, source_target_pairs={{0,0},{1,17},{2,34},{3,51},{4,68},{5,85},{6,102},{7,119},{8,8},{9,... | collective-permute-start | bytes 1179656 | tf_op jit(solution)/shard_map/ppermute | solution.py:30
  65.2 26.7 %copy-start.3 = (bf16[4,384,128]{2,1,0:T(8,128)(2,1)}, bf16[4,384,128]{2,1,0:T(8,128)(2,1)S(1)}, u32[]{:S(2)}) copy-start(bf16[4,384,128]{2,1,0:T(8,128)(2,1)S(1)} %collective-permute-done.6.refs_4_) | copy-start | bytes 1179652
  66.0 15.1 %collective-permute-start.7 = (bf16[2,384,128]{2,1,0:T(8,128)(2,1)}, bf16[2,384,128]{2,1,0:T(8,128)(2,1)S(1)}, u32[]{:S(2)}, u32[]{:S(2)}) collective-permute-start(bf16[2,384,128]{2,1,0:T(8,128)(2,1)} %slice.164), channel_id=1, source_target_pairs={{0,4},{1,5},{2,6},{3,7},{4,8},{5,9},{6,10},{7,11},{8,12},{9,13},{1... | collective-permute-start | bytes 589832 | tf_op jit(solution)/shard_map/ppermute | solution.py:30
  74.0 7.1 %collective-permute-start.8 = (bf16[2,384,128]{2,1,0:T(8,128)(2,1)}, bf16[2,384,128]{2,1,0:T(8,128)(2,1)S(1)}, u32[]{:S(2)}, u32[]{:S(2)}) collective-permute-start(bf16[2,384,128]{2,1,0:T(8,128)(2,1)} %slice.165), channel_id=1, source_target_pairs={{0,12},{1,13},{2,14},{3,15},{4,0},{5,1},{6,2},{7,3},{8,4},{9,5},{1... | collective-permute-start | bytes 589832 | tf_op jit(solution)/shard_map/ppermute | solution.py:30
  76.5 7.5 %collective-permute-start.14 = (bf16[2,384,128]{2,1,0:T(8,128)(2,1)}, bf16[2,384,128]{2,1,0:T(8,128)(2,1)S(1)}, u32[]{:S(2)}, u32[]{:S(2)}) collective-permute-start(bf16[2,384,128]{2,1,0:T(8,128)(2,1)} %slice.166), channel_id=1, source_target_pairs={{0,1},{1,2},{2,3},{3,0},{4,5},{5,6},{6,7},{7,4},{8,9},{9,10},{10,1... | collective-permute-start | bytes 589832 | tf_op jit(solution)/shard_map/ppermute | solution.py:30
  77.3 9.1 %collective-permute-start.15 = (bf16[2,384,128]{2,1,0:T(8,128)(2,1)}, bf16[2,384,128]{2,1,0:T(8,128)(2,1)S(1)}, u32[]{:S(2)}, u32[]{:S(2)}) collective-permute-start(bf16[2,384,128]{2,1,0:T(8,128)(2,1)} %slice.167), channel_id=1, source_target_pairs={{0,3},{1,0},{2,1},{3,2},{4,7},{5,4},{6,5},{7,6},{8,11},{9,8},{10,9... | collective-permute-start | bytes 589832 | tf_op jit(solution)/shard_map/ppermute | solution.py:30
  103.8 22.6 %collective-permute-start.16 = (bf16[768,384]{1,0:T(8,128)(2,1)S(1)}, bf16[768,384]{1,0:T(8,128)(2,1)S(1)}, u32[]{:S(2)}, u32[]{:S(2)}) collective-permute-start(bf16[768,384]{1,0:T(8,128)(2,1)S(1)} %shard_map.85.mine_ref), channel_id=1, source_target_pairs={{0,128},{1,129},{2,130},{3,131},{4,132},{5,133},{6,134},{7,135},{8... | collective-permute-start | bytes 1769480 | tf_op jit(solution)/shard_map/ppermute | solution.py:30
  105.7 55.4 %copy-start.23 = (s32[2,8]{1,0:T(2,128)S(1)}, s32[2,8]{1,0:T(2,128)}, u32[]{:S(2)}) copy-start(s32[2,8]{1,0:T(2,128)} %get-tuple-element.66) | copy-start | bytes 196
  126.9 31.4 %copy-start.2 = (f32[768,384]{1,0:T(8,128)}, f32[768,384]{1,0:T(8,128)S(1)}, u32[]{:S(2)}) copy-start(f32[768,384]{1,0:T(8,128)S(1)} %get-tuple-element.32) | copy-start | bytes 3538948
  127.0 20.7 %collective-permute-start.18 = (bf16[96,384]{1,0:T(8,128)(2,1)S(1)}, bf16[96,384]{1,0:T(8,128)(2,1)S(1)}, u32[]{:S(2)}, u32[]{:S(2)}) collective-permute-start(bf16[96,384]{1,0:T(8,128)(2,1)S(1)} %get-tuple-element.65), channel_id=1, source_target_pairs={{0,1},{1,2},{2,3},{3,0},{4,5},{5,6},{6,7},{7,4},{8,9},{9,10},{10,1... | collective-permute-start | bytes 221192 | tf_op jit(solution)/shard_map/ppermute | solution.py:30
  127.0 26.8 %collective-permute-start.25 = (bf16[96,384]{1,0:T(8,128)(2,1)S(1)}, bf16[96,384]{1,0:T(8,128)(2,1)S(1)}, u32[]{:S(2)}, u32[]{:S(2)}) collective-permute-start(bf16[96,384]{1,0:T(8,128)(2,1)S(1)} %get-tuple-element.64), channel_id=1, source_target_pairs={{0,4},{1,5},{2,6},{3,7},{4,8},{5,9},{6,10},{7,11},{8,12},{9,13},{1... | collective-permute-start | bytes 221192 | tf_op jit(solution)/shard_map/ppermute | solution.py:30
  135.4 18.4 %collective-permute-start.17 = (bf16[96,384]{1,0:T(8,128)(2,1)S(1)}, bf16[96,384]{1,0:T(8,128)(2,1)S(1)}, u32[]{:S(2)}, u32[]{:S(2)}) collective-permute-start(bf16[96,384]{1,0:T(8,128)(2,1)S(1)} %get-tuple-element.65), channel_id=1, source_target_pairs={{0,3},{1,0},{2,1},{3,2},{4,7},{5,4},{6,5},{7,6},{8,11},{9,8},{10,9... | collective-permute-start | bytes 221192 | tf_op jit(solution)/shard_map/ppermute | solution.py:30
  147.6 7.3 %collective-permute-start.19 = (bf16[96,384]{1,0:T(8,128)(2,1)S(1)}, bf16[96,384]{1,0:T(8,128)(2,1)S(1)}, u32[]{:S(2)}, u32[]{:S(2)}) collective-permute-start(bf16[96,384]{1,0:T(8,128)(2,1)S(1)} %collective-permute-done.18), channel_id=1, source_target_pairs={{0,1},{1,2},{2,3},{3,0},{4,5},{5,6},{6,7},{7,4},{8,9},{9,10},{10,1... | collective-permute-start | bytes 221192 | tf_op jit(solution)/shard_map/ppermute | solution.py:30
  151.3 5.7 %collective-permute-start.24 = (bf16[96,384]{1,0:T(8,128)(2,1)S(1)}, bf16[96,384]{1,0:T(8,128)(2,1)S(1)}, u32[]{:S(2)}, u32[]{:S(2)}) collective-permute-start(bf16[96,384]{1,0:T(8,128)(2,1)S(1)} %get-tuple-element.64), channel_id=1, source_target_pairs={{0,12},{1,13},{2,14},{3,15},{4,0},{5,1},{6,2},{7,3},{8,4},{9,5},{1... | collective-permute-start | bytes 221192 | tf_op jit(solution)/shard_map/ppermute | solution.py:30
  153.9 4.4 %collective-permute-start.26 = (bf16[96,384]{1,0:T(8,128)(2,1)S(1)}, bf16[96,384]{1,0:T(8,128)(2,1)S(1)}, u32[]{:S(2)}, u32[]{:S(2)}) collective-permute-start(bf16[96,384]{1,0:T(8,128)(2,1)S(1)} %collective-permute-done.25), channel_id=1, source_target_pairs={{0,4},{1,5},{2,6},{3,7},{4,8},{5,9},{6,10},{7,11},{8,12},{9,13},{1... | collective-permute-start | bytes 221192 | tf_op jit(solution)/shard_map/ppermute | solution.py:30
  155.0 9.7 %collective-permute-start.20 = (bf16[4,96,384]{2,1,0:T(8,128)(2,1)S(1)}, bf16[4,96,384]{2,1,0:T(8,128)(2,1)S(1)}, u32[]{:S(2)}, u32[]{:S(2)}) collective-permute-start(bf16[4,96,384]{2,1,0:T(8,128)(2,1)S(1)} %pad_maximum_fusion.2.refs_0_), channel_id=1, source_target_pairs={{0,12},{1,13},{2,14},{3,15},{4,0},{5,1},{6,2},{7,3},{8,4},{9,5},{1... | collective-permute-start | bytes 884744 | tf_op jit(solution)/shard_map/ppermute | solution.py:30
  157.0 7.6 %collective-permute-start.21 = (bf16[4,96,384]{2,1,0:T(8,128)(2,1)S(1)}, bf16[4,96,384]{2,1,0:T(8,128)(2,1)S(1)}, u32[]{:S(2)}, u32[]{:S(2)}) collective-permute-start(bf16[4,96,384]{2,1,0:T(8,128)(2,1)S(1)} %pad_maximum_fusion.2.refs_0_), channel_id=1, source_target_pairs={{0,4},{1,5},{2,6},{3,7},{4,8},{5,9},{6,10},{7,11},{8,12},{9,13},{1... | collective-permute-start | bytes 884744 | tf_op jit(solution)/shard_map/ppermute | solution.py:30
  158.3 9.1 %collective-permute-start.28 = (bf16[4,96,384]{2,1,0:T(8,128)(2,1)S(1)}, bf16[4,96,384]{2,1,0:T(8,128)(2,1)S(1)}, u32[]{:S(2)}, u32[]{:S(2)}) collective-permute-start(bf16[4,96,384]{2,1,0:T(8,128)(2,1)S(1)} %pad_maximum_fusion.3.refs_5_), channel_id=1, source_target_pairs={{0,1},{1,2},{2,3},{3,0},{4,5},{5,6},{6,7},{7,4},{8,9},{9,10},{10,1... | collective-permute-start | bytes 884744 | tf_op jit(solution)/shard_map/ppermute | solution.py:30
  160.7 9.5 %collective-permute-start.27 = (bf16[4,96,384]{2,1,0:T(8,128)(2,1)S(1)}, bf16[4,96,384]{2,1,0:T(8,128)(2,1)S(1)}, u32[]{:S(2)}, u32[]{:S(2)}) collective-permute-start(bf16[4,96,384]{2,1,0:T(8,128)(2,1)S(1)} %pad_maximum_fusion.3.refs_5_), channel_id=1, source_target_pairs={{0,3},{1,0},{2,1},{3,2},{4,7},{5,4},{6,5},{7,6},{8,11},{9,8},{10,9... | collective-permute-start | bytes 884744 | tf_op jit(solution)/shard_map/ppermute | solution.py:30
  164.6 9.6 %collective-permute-start.22 = (bf16[2,96,384]{2,1,0:T(8,128)(2,1)S(1)}, bf16[2,96,384]{2,1,0:T(8,128)(2,1)S(1)}, u32[]{:S(2)}, u32[]{:S(2)}) collective-permute-start(bf16[2,96,384]{2,1,0:T(8,128)(2,1)S(1)} %slice.174), channel_id=1, source_target_pairs={{0,4},{1,5},{2,6},{3,7},{4,8},{5,9},{6,10},{7,11},{8,12},{9,13},{1... | collective-permute-start | bytes 442376 | tf_op jit(solution)/shard_map/ppermute | solution.py:30
  164.7 9.5 %collective-permute-start.23 = (bf16[2,96,384]{2,1,0:T(8,128)(2,1)S(1)}, bf16[2,96,384]{2,1,0:T(8,128)(2,1)S(1)}, u32[]{:S(2)}, u32[]{:S(2)}) collective-permute-start(bf16[2,96,384]{2,1,0:T(8,128)(2,1)S(1)} %slice.175), channel_id=1, source_target_pairs={{0,12},{1,13},{2,14},{3,15},{4,0},{5,1},{6,2},{7,3},{8,4},{9,5},{1... | collective-permute-start | bytes 442376 | tf_op jit(solution)/shard_map/ppermute | solution.py:30
  167.5 10.6 %collective-permute-start.29 = (bf16[2,96,384]{2,1,0:T(8,128)(2,1)S(1)}, bf16[2,96,384]{2,1,0:T(8,128)(2,1)S(1)}, u32[]{:S(2)}, u32[]{:S(2)}) collective-permute-start(bf16[2,96,384]{2,1,0:T(8,128)(2,1)S(1)} %slice.176), channel_id=1, source_target_pairs={{0,1},{1,2},{2,3},{3,0},{4,5},{5,6},{6,7},{7,4},{8,9},{9,10},{10,1... | collective-permute-start | bytes 442376 | tf_op jit(solution)/shard_map/ppermute | solution.py:30
  170.3 9.2 %collective-permute-start.30 = (bf16[2,96,384]{2,1,0:T(8,128)(2,1)S(1)}, bf16[2,96,384]{2,1,0:T(8,128)(2,1)S(1)}, u32[]{:S(2)}, u32[]{:S(2)}) collective-permute-start(bf16[2,96,384]{2,1,0:T(8,128)(2,1)S(1)} %slice.177), channel_id=1, source_target_pairs={{0,3},{1,0},{2,1},{3,2},{4,7},{5,4},{6,5},{7,6},{8,11},{9,8},{10,9... | collective-permute-start | bytes 442376 | tf_op jit(solution)/shard_map/ppermute | solution.py:30
  186.2 25.5 %copy-start.9 = (f32[384,256]{1,0:T(8,128)}, f32[384,256]{1,0:T(8,128)S(1)}, u32[]{:S(2)}) copy-start(f32[384,256]{1,0:T(8,128)S(1)} %get-tuple-element.34) | copy-start | bytes 1179652
  186.2 9.1 %collective-permute-start.32 = (bf16[256,384]{1,0:T(8,128)(2,1)}, bf16[256,384]{1,0:T(8,128)(2,1)S(1)}, u32[]{:S(2)}, u32[]{:S(2)}) collective-permute-start(bf16[256,384]{1,0:T(8,128)(2,1)} %get-tuple-element.35.refs_0_), channel_id=1, source_target_pairs={{0,32},{1,33},{2,34},{3,35},{4,36},{5,37},{6,38},{7,39},{8,40},{9,... | collective-permute-start | bytes 589832 | tf_op jit(solution)/shard_map/ppermute | solution.py:30
  187.4 8.2 %collective-permute-start.31 = (bf16[256,384]{1,0:T(8,128)(2,1)}, bf16[256,384]{1,0:T(8,128)(2,1)S(1)}, u32[]{:S(2)}, u32[]{:S(2)}) collective-permute-start(bf16[256,384]{1,0:T(8,128)(2,1)} %get-tuple-element.35.refs_0_), channel_id=1, source_target_pairs={{0,96},{1,97},{2,98},{3,99},{4,100},{5,101},{6,102},{7,103},{8,104... | collective-permute-start | bytes 589832 | tf_op jit(solution)/shard_map/ppermute | solution.py:30
  195.3 16.9 %collective-permute-start.33 = (bf16[128,384]{1,0:T(8,128)(2,1)S(1)}, bf16[128,384]{1,0:T(8,128)(2,1)}, u32[]{:S(2)}, u32[]{:S(2)}) collective-permute-start(bf16[128,384]{1,0:T(8,128)(2,1)S(1)} %slice.184), channel_id=1, source_target_pairs={{0,32},{1,33},{2,34},{3,35},{4,36},{5,37},{6,38},{7,39},{8,40},{9,... | collective-permute-start | bytes 294920 | tf_op jit(solution)/shard_map/ppermute | solution.py:30
  195.6 18.7 %collective-permute-start.34 = (bf16[128,384]{1,0:T(8,128)(2,1)S(1)}, bf16[128,384]{1,0:T(8,128)(2,1)}, u32[]{:S(2)}, u32[]{:S(2)}) collective-permute-start(bf16[128,384]{1,0:T(8,128)(2,1)S(1)} %slice.185), channel_id=1, source_target_pairs={{0,96},{1,97},{2,98},{3,99},{4,100},{5,101},{6,102},{7,103},{8,104... | collective-permute-start | bytes 294920 | tf_op jit(solution)/shard_map/ppermute | solution.py:30
  199.0 25.3 %collective-permute-start.35 = (bf16[256,384]{1,0:T(8,128)(2,1)}, bf16[256,384]{1,0:T(8,128)(2,1)}, u32[]{:S(2)}, u32[]{:S(2)}) collective-permute-start(bf16[256,384]{1,0:T(8,128)(2,1)} %get-tuple-element.35.refs_0_), channel_id=1, source_target_pairs={{0,16},{1,17},{2,18},{3,19},{4,20},{5,21},{6,22},{7,23},{8,24},{9,... | collective-permute-start | bytes 589832 | tf_op jit(solution)/shard_map/ppermute | solution.py:30
  211.7 12.6 %collective-permute-start.36 = (bf16[256,384]{1,0:T(8,128)(2,1)S(1)}, bf16[256,384]{1,0:T(8,128)(2,1)}, u32[]{:S(2)}, u32[]{:S(2)}) collective-permute-start(bf16[256,384]{1,0:T(8,128)(2,1)S(1)} %collective-permute-done.31.refs_1_), channel_id=1, source_target_pairs={{0,16},{1,17},{2,18},{3,19},{4,20},{5,21},{6,22},{7,23},{8,24},{9,... | collective-permute-start | bytes 589832 | tf_op jit(solution)/shard_map/ppermute | solution.py:30
  211.7 12.6 %collective-permute-start.39 = (bf16[256,384]{1,0:T(8,128)(2,1)S(1)}, bf16[256,384]{1,0:T(8,128)(2,1)}, u32[]{:S(2)}, u32[]{:S(2)}) collective-permute-start(bf16[256,384]{1,0:T(8,128)(2,1)S(1)} %collective-permute-done.32.refs_4_), channel_id=1, source_target_pairs={{0,16},{1,17},{2,18},{3,19},{4,20},{5,21},{6,22},{7,23},{8,24},{9,... | collective-permute-start | bytes 589832 | tf_op jit(solution)/shard_map/ppermute | solution.py:30
  212.2 12.1 %collective-permute-start.37 = (bf16[128,384]{1,0:T(8,128)(2,1)}, bf16[128,384]{1,0:T(8,128)(2,1)}, u32[]{:S(2)}, u32[]{:S(2)}) collective-permute-start(bf16[128,384]{1,0:T(8,128)(2,1)} %collective-permute-done.33.refs_2_), channel_id=1, source_target_pairs={{0,16},{1,17},{2,18},{3,19},{4,20},{5,21},{6,22},{7,23},{8,24},{9,... | collective-permute-start | bytes 294920 | tf_op jit(solution)/shard_map/ppermute | solution.py:30
  214.3 10.0 %collective-permute-start.38 = (bf16[128,384]{1,0:T(8,128)(2,1)}, bf16[128,384]{1,0:T(8,128)(2,1)}, u32[]{:S(2)}, u32[]{:S(2)}) collective-permute-start(bf16[128,384]{1,0:T(8,128)(2,1)} %collective-permute-done.34.refs_3_), channel_id=1, source_target_pairs={{0,16},{1,17},{2,18},{3,19},{4,20},{5,21},{6,22},{7,23},{8,24},{9,... | collective-permute-start | bytes 294920 | tf_op jit(solution)/shard_map/ppermute | solution.py:30
  (19 other events, 74.3 us)
Sparse Core Ops, SparseCore 0:
  10.2 37.6 all-gather.6
  49.7 71.4 all-gather.8
  123.6 75.9 all-gather.10

commit v3 on v2

--- a/solution.py
+++ b/solution.py
@@ -12,7 +12,7 @@
 SIDE = 4
 BLK = 128
 REACH = 64
-VMEM_LIMIT = 48 * 1024 * 1024
+VMEM_LIMIT = 60 * 1024 * 1024
 
 
 def permute(array, target):
@@ -50,8 +50,12 @@
     return (1 - h, r, q)
 
 
+def mixed(r, p):
+    return r ^ p ^ (r % 2 * SIDE)
+
+
 def transposed_place(h, r, q):
-    return (h, q % N_ROW, q // N_ROW * N_ROW + (r ^ (q % N_ROW)))
+    return (h, q % N_ROW, q // N_ROW * N_ROW + mixed(r, q % N_ROW))
 
 
 def ring_parts(own, along, split):
@@ -98,43 +102,14 @@
     return pairs
 
 
-def root_kernel(slot_one, slot_two, *refs):
-    parts, (right_in, out_ref, one_ref, two_ref, right_ref, acc, sems) = refs[:10], refs[10:]
-    load(spread(parts[:5], one_ref) + spread(parts[5:], two_ref) + [(right_in, right_ref)], sems)
-    acc[...] = jnp.zeros_like(acc)
-
-    def step(r, carry):
-        right = [right_ref[r, pl.ds(BLK * i, BLK), :] for i in range(6)]
-        right_0 = right[0]
-        right_1 = cat(right[1:3], 1)
-        right_2 = cat(right[3:6], 1)
-        for side in range(2):
-            one = slot_one[side * N_ROW + r]
-            two = slot_two[side * N_ROW + r]
-            acc[side] += dot(two_ref[two], right_2)
-            acc[side, : 2 * BLK, : 2 * BLK] += dot(one_ref[one, BLK:, :], right_1)
-            acc[side, :BLK, :BLK] += dot(one_ref[one, :BLK, :], right_0)
-        return carry
-
-    lax.fori_loop(0, N_ROW, step, 0)
-    for outer in range(3):
-        for side in range(2):
-            out_ref[pl.ds((2 * outer + side) * BLK, BLK), :] = acc[
-                side, pl.ds(outer * BLK, BLK), :
-            ].astype(out_ref.dtype)
-
-
-def pick_kernel(mine_ref, other_ref, row_ref, col_ref, root_ref, picked_ref):
-    total = mine_ref[...].astype(jnp.float32) + other_ref[...].astype(jnp.float32)
-    root_ref[...] = total
-    low = total.astype(jnp.bfloat16)
+def chooser(ref, i):
     lanes = lax.broadcasted_iota(jnp.int32, (REACH, BLK), 1)
-
-    def chooser(ref, i):
-        return jnp.where(ref[pl.ds(i * REACH, REACH), :] == lanes, 1.0, 0.0).astype(jnp.bfloat16)
-
+    return jnp.where(ref[pl.ds(i * REACH, REACH), :] == lanes, 1.0, 0.0).astype(jnp.bfloat16)
+
+
+def pick(low_ref, row_ref, col_ref, picked_ref):
     rows = cat(
-        [dot(chooser(row_ref, i), low[i * BLK : (i + 1) * BLK, :]).astype(jnp.bfloat16) for i in range(6)], 0
+        [dot(chooser(row_ref, i), low_ref[pl.ds(i * BLK, BLK), :]).astype(jnp.bfloat16) for i in range(6)], 0
     )
     for i in range(3):
         picked_ref[pl.ds(i * REACH, REACH), :] = dot_nt(
@@ -142,9 +117,50 @@
         ).astype(jnp.bfloat16)
 
 
+def root_kernel(slot_one, slot_two, *refs):
+    parts, right_in, picks = refs[:10], refs[10], refs[11:15]
+    out_ref, theirs_ref, mine_ref, one_ref, two_ref, right_ref, acc, sems = refs[15:]
+    right_in = right_in.at[:, pl.ds(0, 768), :]
+    load(spread(parts[:5], one_ref) + spread(parts[5:], two_ref) + [(right_in, right_ref)], sems)
+    acc[...] = jnp.zeros_like(acc)
+
+    def step(i, carry):
+        pair = (2 * i, 2 * i + 1)
+        right = [[right_ref[r, pl.ds(BLK * k, BLK), :] for k in range(6)] for r in pair]
+        right_0 = cat([right[0][0], right[1][0]], 0)
+        right_1 = cat([cat(right[k][1:3], 1) for k in range(2)], 0)
+        right_2 = cat([cat(right[k][3:6], 1) for k in range(2)], 0)
+        for side in range(2):
+            one = [slot_one[side * N_ROW + r] for r in pair]
+            two = [slot_two[side * N_ROW + r] for r in pair]
+            left_1 = cat([one_ref[one[k]] for k in range(2)], 1)
+            left_2 = cat([two_ref[two[k]] for k in range(2)], 1)
+            acc[side] += dot(left_2, right_2)
+            acc[side, : 2 * BLK, : 2 * BLK] += dot(left_1[BLK:], right_1)
+            acc[side, :BLK, :BLK] += dot(left_1[:BLK], right_0)
+        return carry
+
+    lax.fori_loop(0, N_ROW // 2, step, 0)
+    for outer in range(3):
+        for side in range(2):
+            out_ref[pl.ds((2 * outer + side) * BLK, BLK), :] = acc[
+                side, pl.ds(outer * BLK, BLK), :
+            ].astype(out_ref.dtype)
+    pick(out_ref, picks[0], picks[1], theirs_ref)
+    pick(out_ref, picks[2], picks[3], mine_ref)
+
+
+def sum_kernel(mine_ref, other_ref, out_ref):
+    for i in range(3):
+        lanes = pl.ds(i * BLK, BLK)
+        out_ref[pl.ds(i, 768, stride=3), :] = mine_ref[:, lanes].astype(jnp.float32) + other_ref[
+            :, lanes
+        ].astype(jnp.float32)
+
+
 def offdiag_kernel(slot_one, slot_two, *refs):
     parts, (right_in, out_ref, low_ref, one_ref, two_ref, block_ref, acc, sems) = refs[:10], refs[10:]
-    block_in = right_in.at[:, pl.ds(768, 768), :]
+    block_in = right_in.at[:, pl.ds(1536, 768), :]
     load(spread(parts[:5], one_ref) + spread(parts[5:], two_ref) + [(block_in, block_ref)], sems)
     acc[...] = jnp.zeros_like(acc)
 
@@ -165,12 +181,14 @@
     lax.fori_loop(0, N_ROW, step, 0)
     total = -acc[...]
     low_ref[...] = total.astype(low_ref.dtype)
-    out_ref[...] = total.T
+    for i in range(2):
+        out_ref[pl.ds(i, 384, stride=2), :] = total[i * BLK : (i + 1) * BLK, :].T
 
 
 def own_kernel(slots, left_in, right_in, out_ref, left_ref, right_ref, acc, sems):
-    first = pl.ds(0, 768)
-    load([(left_in.at[:, first, :], left_ref), (right_in.at[:, first, :], right_ref)], sems)
+    left_in = left_in.at[:, pl.ds(0, 768), :]
+    right_in = right_in.at[:, pl.ds(768, 768), :]
+    load([(left_in, left_ref), (right_in, right_ref)], sems)
     acc[...] = jnp.zeros_like(acc)
 
     def step(r, carry):
@@ -198,31 +216,37 @@
         at += part.shape[0]
     load(pairs, sems)
 
-    def step(r, carry):
-        right = right_ref[part_slots[r]]
-        for side in range(2):
-            slot = slots[side * N_ROW + r]
-            left = cat([left_ref[slot, pl.ds(256 * i, 256), :] for i in range(3)], 1)
+    def step(i, carry):
+        pair = (2 * i, 2 * i + 1)
+        right = cat([right_ref[part_slots[r]] for r in pair], 1)
+        for side in range(2):
+            held = [slots[side * N_ROW + r] for r in pair]
+            left = cat([left_ref[slot, pl.ds(256 * k, 256), :] for slot in held for k in range(3)], 1)
             acc[side] -= dot_nt(left, right)
         return carry
 
-    lax.fori_loop(0, N_ROW, step, 0)
+    lax.fori_loop(0, N_ROW // 2, step, 0)
     for outer in range(2):
         for side in range(2):
-            out_ref[pl.ds((2 * outer + side) * BLK, BLK), :] = acc[side, pl.ds(outer * BLK, BLK), :]
-
-
-def call(kernel, scalars, arrays, outs, scratch, space=pl.ANY):
+            for i in range(2):
+                first = (2 * outer + side) * 2 * BLK + i
+                out_ref[pl.ds(first, BLK, stride=2), :] = acc[
+                    side, pl.ds(outer * BLK, BLK), pl.ds(i * BLK, BLK)
+                ]
+
+
+def call(kernel, scalars, arrays, outs, scratch, blocks=()):
     vmem = pl.BlockSpec(memory_space=pltpu.VMEM)
     smem = pl.BlockSpec(memory_space=pltpu.SMEM)
+    anywhere = pl.BlockSpec(memory_space=pl.ANY)
     return pl.pallas_call(
         kernel,
-        in_specs=[smem] * len(scalars) + [pl.BlockSpec(memory_space=space)] * len(arrays),
+        in_specs=[smem] * len(scalars) + [anywhere] * len(arrays) + [vmem] * len(blocks),
         out_specs=[vmem] * len(outs),
         out_shape=[jax.ShapeDtypeStruct(*o) for o in outs],
         scratch_shapes=list(scratch),
         compiler_params=pltpu.CompilerParams(vmem_limit_bytes=VMEM_LIMIT),
-    )(*scalars, *arrays)
+    )(*scalars, *arrays, *blocks)
 
 
 def stack_blocks(array, pairs):
@@ -234,9 +258,9 @@
     col = lax.axis_index("col")
     bf16 = jnp.bfloat16
     root = root_factor.reshape(3, BLK, 3, BLK)
+    root_pairs = [(0, 0), (1, 0), (1, 1), (2, 0), (2, 1), (2, 2)]
+    root_here = permute(stack_blocks(root.transpose(0, 3, 2, 1), root_pairs), transposed_place)
     scaled_root = (root_pivots.reshape(3, BLK, 1, 1) * root.astype(jnp.float32)).astype(bf16)
-    root_pairs = [(0, 0), (1, 0), (1, 1), (2, 0), (2, 1), (2, 2)]
-    root_turned = stack_blocks(root.transpose(0, 3, 2, 1), root_pairs)
     root_scaled = stack_blocks(scaled_root, root_pairs)
 
     child = child_factor.reshape(4, BLK, 2, BLK)
@@ -248,21 +272,26 @@
     block_turned = block.T.reshape(2 * BLK, 3, BLK).transpose(1, 0, 2).reshape(768, BLK)
     block_sorted = block.reshape(3, 2, REACH, 2 * BLK).transpose(1, 0, 2, 3).reshape(6 * REACH, 2 * BLK)
     block_sorted = block_sorted.T.reshape(2 * BLK, 3, BLK).transpose(1, 0, 2).reshape(768, BLK)
-
-    root_right = lax.all_gather(root_scaled, "row", axis=0, tiled=False)
-    root_here = permute(root_turned, transposed_place)
+    right = lax.all_gather(
+        jnp.concatenate([root_scaled, child_scaled, block_sorted], 0), "row", axis=0, tiled=False
+    )
+
+    rows = child_rows[0].reshape(48, REACH) % BLK
+    row_picks = lax.dynamic_index_in_dim(rows.reshape(6, N_ROW, REACH), row, 1, keepdims=False)
+    col_picks = lax.dynamic_index_in_dim(rows.reshape(3, N_COL, REACH), col, 1, keepdims=False)
+    my_picks = jnp.concatenate([row_picks.reshape(-1), col_picks.reshape(-1)])[:, None]
+    other_picks = permute(my_picks, other_half)
+
     child_stack = jnp.concatenate([child_turned, block_turned], 0)
-    root_here, child_stack = lax.optimization_barrier((root_here, child_stack))
+    child_stack = lax.optimization_barrier((child_stack, root_here))[0]
     child_here = permute(child_stack, transposed_place)
-    child_right = lax.all_gather(jnp.concatenate([child_scaled, block_sorted], 0), "row", axis=0, tiled=False)
-
     root_parts = plane_gather(root_here[:384], root_here[384:])
-    child_here, root_parts = lax.optimization_barrier((child_here, root_parts))
+    child_here = lax.optimization_barrier((child_here, root_parts))[0]
     child_left = lax.all_gather(child_here, "col", axis=0, tiled=False)
 
     side = jnp.arange(2, dtype=jnp.int32)[:, None]
     classes = jnp.arange(N_ROW, dtype=jnp.int32)[None, :]
-    source = side * N_ROW + (classes ^ row)
+    source = side * N_ROW + mixed(classes, row)
     my_x, my_y = col % SIDE, col // SIDE
 
     def plane_slots(place):
@@ -271,11 +300,11 @@
         return (dy * SIDE + dx).reshape(-1), (dx * SIDE + dy).reshape(-1)
 
     root_slots = plane_slots(source)
-    (partial,) = call(
+    partial, theirs, mine = call(
         root_kernel,
         root_slots,
-        (*root_parts[0], *root_parts[1], root_right),
-        [((768, 384), bf16)],
+        (*root_parts[0], *root_parts[1], right),
+        [((768, 384), bf16), ((192, 384), bf16), ((192, 384), bf16)],
         [
             pltpu.VMEM((N_COL, 384, BLK), bf16),
             pltpu.VMEM((N_COL, 384, BLK), bf16),
@@ -283,26 +312,21 @@
             pltpu.VMEM((2, 384, 384), jnp.float32),
             pltpu.SemaphoreType.DMA((11,)),
         ],
-    )
-    other = permute(partial, other_half)
-    rows = child_rows[0].reshape(48, REACH) % BLK
-    row_picks = lax.dynamic_index_in_dim(rows.reshape(6, N_ROW, REACH), row, 1, keepdims=False)
-    col_picks = lax.dynamic_index_in_dim(rows.reshape(3, N_COL, REACH), col, 1, keepdims=False)
-    root_inverse, picked = call(
-        pick_kernel,
-        (),
-        (partial, other, row_picks.reshape(-1, 1), col_picks.reshape(-1, 1)),
-        [((768, 384), jnp.float32), ((192, 384), bf16)],
-        (),
-        pltpu.VMEM,
+        (other_picks[:384], other_picks[384:], my_picks[:384], my_picks[384:]),
+    )
+    theirs = permute(theirs, other_half)
+    picked = (mine.astype(jnp.float32) + theirs.astype(jnp.float32)).astype(bf16)
+    late = lax.optimization_barrier((partial, picked))[0]
+    (root_inverse,) = call(
+        sum_kernel, (), (), [((2304, BLK), jnp.float32)], (), (partial, permute(late, other_half))
     )
     picked_parts = plane_gather(picked[:96], picked[96:])
     offdiag_slots = plane_slots(side * N_ROW + classes)
     offdiag, offdiag_low = call(
         offdiag_kernel,
         offdiag_slots,
-        (*picked_parts[0], *picked_parts[1], child_right),
-        [((384, 256), jnp.float32), ((256, 384), bf16)],
+        (*picked_parts[0], *picked_parts[1], right),
+        [((768, BLK), jnp.float32), ((256, 384), bf16)],
         [
             pltpu.VMEM((N_COL, 96, 384), bf16),
             pltpu.VMEM((N_COL, 96, 384), bf16),
@@ -315,7 +339,7 @@
     (own,) = call(
         own_kernel,
         (slots,),
-        (child_left, child_right),
+        (child_left, right),
         [((2, 256, 256), jnp.float32)],
         [
             pltpu.VMEM((N_COL, 768, BLK), bf16),
@@ -332,7 +356,7 @@
         child_kernel,
         (slots, part_slots),
         (*parts, own, child_left),
-        [((512, 256), jnp.float32)],
+        [((1024, BLK), jnp.float32)],
         [
             pltpu.VMEM((N_COL, 768, BLK), bf16),
             pltpu.VMEM((N_ROW, 256, 384), bf16),

time: 238 us -> 222 us (0.933)
  local copies, waits for them, and re-layouts: 30.5 us -> 16.7 us
  starting transfers between devices: 118 us -> 112 us
  Pallas kernels: 21.6 us -> 27.2 us
  waiting for transfers between devices: 49 us -> 44.4 us
    reshape x5 -> x2, local copies, waits for them, and re-layouts: 6.72 us -> 0.16 us  [the longest x1 0.08 us: per_device(): col_picks.reshape(-1)]
    unnamed x75 -> x92, local copies, waits for them, and re-layouts: 15.8 us -> 9.38 us
    ppermute x40 -> x42, starting transfers between devices: 118 us -> 112 us  [permute(): return lax.ppermute(array, AXES, pairs)]
    pallas_call x5, Pallas kernels: 21.6 us -> 27.2 us  [call(): pl.pallas_call(kernel, in_specs=[smem] * len(scalars) + [anywhere] * len(...]
    ppermute x40 -> x42, waiting for transfers between devices: 49 us -> 44.3 us  [permute(): return lax.ppermute(array, AXES, pairs)]
    slice x0 -> x4, local copies, waits for them, and re-layouts: none -> 2.96 us  [the longest x1 0.86 us: per_device(): my_picks[:384]]
  transfers between devices with their start and end apart: 43 -> 44, of which waited for: 12 -> 17; matrix products, arithmetic and copies ran while one was open for 9% -> 7% of each run, Pallas kernels for 7% -> 10%
where the time goes in v3:
time: 222 us; the launch traced here: 221 us
  starting transfers between devices  112 us (50%)
  waiting for transfers between devices  44.4 us (20%)
  Pallas kernels  27.2 us (12%)
  local copies, waits for them, and re-layouts  16.7 us (8%)
  between operations  14.9 us (7%)
  other arithmetic  5.97 us (3%)
    ppermute x42, starting transfers between devices, permute(): return lax.ppermute(array, AXES, pairs)  112 us
    ppermute x42, waiting for transfers between devices, permute(): return lax.ppermute(array, AXES, pairs)  44.3 us
    pallas_call x5, Pallas kernels, call(): pl.pallas_call(kernel, in_specs=[smem] * len(scalars) + [anywhere] * len(...  27.2 us
    unnamed x92, local copies, waits for them, and re-layouts  9.38 us
  transfers between devices with their start and end apart: 44, of which 17 were waited for; matrix products, arithmetic and copies ran while one was open for 7% of the time, Pallas kernels for 10%

profile of v3, /device:TPU:1, one launch (start us, length us, event | category | flops | bytes accessed | tf_op | source)
XLA Modules:
  0.0 220.9 jit_solution(1680336819923589674)
XLA Ops:
  7.2 1.2 copy.59
  10.1 1.1 multiply_convert_fusion.1
  11.3 1.1 reshape_reshape.3
  13.6 5.5 %collective-permute-start = (bf16[768,128]{1,0:T(8,128)(2,1)S(1)}, bf16[768,128]{1,0:T(8,128)(2,1)S(1)}, u32[]{:S(2)}, u32[]{:S(2)}) collective-permute-start(bf16[768,128]{1,0:T(8,128)(2,1)S(1)} %constant_dynamic-update-slice_fusion), channel_id=1, source_target_pairs={{0,0},{1,17},{2,34},{3,51},{4,68},{5,85},{6,102},{7,119},{8,8},{9,... | collective-permute-start | bytes 589832 | tf_op jit(solution)/shard_map/ppermute | solution.py:30
  21.5 7.1 %collective-permute-done = bf16[768,128]{1,0:T(8,128)(2,1)S(1)} collective-permute-done((bf16[768,128]{1,0:T(8,128)(2,1)S(1)}, bf16[768,128]{1,0:T(8,128)(2,1)S(1)}, u32[]{:S(2)}, u32[]{:S(2)}) %collective-permute-start) | collective-permute-done | bytes 196640 | tf_op jit(solution)/shard_map/ppermute | solution.py:30
  29.6 9.5 %collective-permute-start.1 = (bf16[384,128]{1,0:T(8,128)(2,1)S(1)}, bf16[384,128]{1,0:T(8,128)(2,1)S(1)}, u32[]{:S(2)}, u32[]{:S(2)}) collective-permute-start(bf16[384,128]{1,0:T(8,128)(2,1)S(1)} %get-tuple-element.49), channel_id=1, source_target_pairs={{0,3},{1,0},{2,1},{3,2},{4,7},{5,4},{6,5},{7,6},{8,11},{9,8},{10,9... | collective-permute-start | bytes 294920 | tf_op jit(solution)/shard_map/ppermute | solution.py:30
  39.1 14.9 %collective-permute-start.9 = (bf16[384,128]{1,0:T(8,128)(2,1)S(1)}, bf16[384,128]{1,0:T(8,128)(2,1)S(1)}, u32[]{:S(2)}, u32[]{:S(2)}) collective-permute-start(bf16[384,128]{1,0:T(8,128)(2,1)S(1)} %get-tuple-element.48), channel_id=1, source_target_pairs={{0,4},{1,5},{2,6},{3,7},{4,8},{5,9},{6,10},{7,11},{8,12},{9,13},{1... | collective-permute-start | bytes 294920 | tf_op jit(solution)/shard_map/ppermute | solution.py:30
  54.0 1.2 collective-permute-start.3
  55.9 2.8 %collective-permute-start.8 = (bf16[384,128]{1,0:T(8,128)(2,1)S(1)}, bf16[384,128]{1,0:T(8,128)(2,1)S(1)}, u32[]{:S(2)}, u32[]{:S(2)}) collective-permute-start(bf16[384,128]{1,0:T(8,128)(2,1)S(1)} %get-tuple-element.48), channel_id=1, source_target_pairs={{0,12},{1,13},{2,14},{3,15},{4,0},{5,1},{6,2},{7,3},{8,4},{9,5},{1... | collective-permute-start | bytes 294920 | tf_op jit(solution)/shard_map/ppermute | solution.py:30
  59.1 3.9 %collective-permute-start.4 = (bf16[4,384,128]{2,1,0:T(8,128)(2,1)S(1)}, bf16[4,384,128]{2,1,0:T(8,128)(2,1)S(1)}, u32[]{:S(2)}, u32[]{:S(2)}) collective-permute-start(bf16[4,384,128]{2,1,0:T(8,128)(2,1)S(1)} %pad_maximum_fusion.refs_0_), channel_id=1, source_target_pairs={{0,12},{1,13},{2,14},{3,15},{4,0},{5,1},{6,2},{7,3},{8,4},{9,5},{1... | collective-permute-start | bytes 1179656 | tf_op jit(solution)/shard_map/ppermute | solution.py:30
  63.9 2.8 %collective-permute-start.11 = (bf16[4,384,128]{2,1,0:T(8,128)(2,1)S(1)}, bf16[4,384,128]{2,1,0:T(8,128)(2,1)S(1)}, u32[]{:S(2)}, u32[]{:S(2)}) collective-permute-start(bf16[4,384,128]{2,1,0:T(8,128)(2,1)S(1)} %pad_maximum_fusion.1.refs_5_), channel_id=1, source_target_pairs={{0,3},{1,0},{2,1},{3,2},{4,7},{5,4},{6,5},{7,6},{8,11},{9,8},{10,9... | collective-permute-start | bytes 1179656 | tf_op jit(solution)/shard_map/ppermute | solution.py:30
  68.1 3.3 %collective-permute-start.41 = (bf16[1536,128]{1,0:T(8,128)(2,1)}, bf16[1536,128]{1,0:T(8,128)(2,1)S(1)}, u32[]{:S(2)}, u32[]{:S(2)}) collective-permute-start(bf16[1536,128]{1,0:T(8,128)(2,1)} %constant_dynamic-update-slice_fusion.19), channel_id=1, source_target_pairs={{0,0},{1,17},{2,34},{3,51},{4,68},{5,85},{6,102},{7,119},{8,8},{9,... | collective-permute-start | bytes 1179656 | tf_op jit(solution)/shard_map/ppermute | solution.py:30
  71.5 1.2 collective-permute-done.5.refs_4_
  72.7 5.8 %collective-permute-start.6 = (bf16[2,384,128]{2,1,0:T(8,128)(2,1)S(1)}, bf16[2,384,128]{2,1,0:T(8,128)(2,1)}, u32[]{:S(2)}, u32[]{:S(2)}) collective-permute-start(bf16[2,384,128]{2,1,0:T(8,128)(2,1)S(1)} %slice.179), channel_id=1, source_target_pairs={{0,4},{1,5},{2,6},{3,7},{4,8},{5,9},{6,10},{7,11},{8,12},{9,13},{1... | collective-permute-start | bytes 589832 | tf_op jit(solution)/shard_map/ppermute | solution.py:30
  78.9 2.7 %collective-permute-start.14 = (bf16[2,384,128]{2,1,0:T(8,128)(2,1)S(1)}, bf16[2,384,128]{2,1,0:T(8,128)(2,1)}, u32[]{:S(2)}, u32[]{:S(2)}) collective-permute-start(bf16[2,384,128]{2,1,0:T(8,128)(2,1)S(1)} %slice.183), channel_id=1, source_target_pairs={{0,3},{1,0},{2,1},{3,2},{4,7},{5,4},{6,5},{7,6},{8,11},{9,8},{10,9... | collective-permute-start | bytes 589832 | tf_op jit(solution)/shard_map/ppermute | solution.py:30
  81.6 3.2 %collective-permute-done.41 = bf16[1536,128]{1,0:T(8,128)(2,1)S(1)} collective-permute-done((bf16[1536,128]{1,0:T(8,128)(2,1)}, bf16[1536,128]{1,0:T(8,128)(2,1)S(1)}, u32[]{:S(2)}, u32[]{:S(2)}) %collective-permute-start.41) | collective-permute-done | bytes 393248 | tf_op jit(solution)/shard_map/ppermute | solution.py:30
  84.9 1.8 collective-permute-done.6.refs_2_
  86.7 1.4 collective-permute-done.13.refs_7_
  88.1 1.7 collective-permute-done.14.refs_8_
  91.5 5.0 %collective-permute-start.15 = (s32[576,1]{1,0:T(8,128)S(1)}, s32[576,1]{1,0:T(8,128)S(1)}, u32[]{:S(2)}, u32[]{:S(2)}) collective-permute-start(s32[576,1]{1,0:T(8,128)S(1)} %broadcast_in_dim.6), channel_id=1, source_target_pairs={{0,128},{1,129},{2,130},{3,131},{4,132},{5,133},{6,134},{7,135},{8... | collective-permute-start | bytes 6920 | tf_op jit(solution)/shard_map/ppermute | solution.py:30
  97.8 0.9 slice.170.refs_13_
  99.4 5.0 %collective-permute-done.15 = s32[576,1]{1,0:T(8,128)S(1)} collective-permute-done((s32[576,1]{1,0:T(8,128)S(1)}, s32[576,1]{1,0:T(8,128)S(1)}, u32[]{:S(2)}, u32[]{:S(2)}) %collective-permute-start.15) | collective-permute-done | bytes 2336 | tf_op jit(solution)/shard_map/ppermute | solution.py:30
  105.8 7.1 %shard_map.85 = (bf16[768,384]{1,0:T(8,128)(2,1)}, bf16[192,384]{1,0:T(8,128)(2,1)}, bf16[192,384]{1,0:T(8,128)(2,1)}) custom-call(s32[16]{0:T(128)} %multiply_add_fusion.3.slot_one, s32[16]{0:T(128)} %get-tuple-element.31.slot_two, bf16[4,384,128]{2,1,0:T(8,128)(2,1)} %copy-done, bf16[4,384,128]{2,1,0:T(8,128)(2,1)} %copy-done.5, ...), custom_call_target="tpu_custom_call" | custom-call | tf_op jit(solution)/shard_map/pallas_call | solution.py:242
  113.0 4.2 %collective-permute-done.16 = bf16[192,384]{1,0:T(8,128)(2,1)S(1)} collective-permute-done((bf16[192,384]{1,0:T(8,128)(2,1)}, bf16[192,384]{1,0:T(8,128)(2,1)S(1)}, u32[]{:S(2)}, u32[]{:S(2)}) %collective-permute-start.16) | collective-permute-done | bytes 147488 | tf_op jit(solution)/shard_map/ppermute | solution.py:30
  117.1 1.0 add_convert_fusion
  118.2 3.1 %collective-permute-start.19 = (bf16[96,384]{1,0:T(8,128)(2,1)S(1)}, bf16[96,384]{1,0:T(8,128)(2,1)S(1)}, u32[]{:S(2)}, u32[]{:S(2)}) collective-permute-start(bf16[96,384]{1,0:T(8,128)(2,1)S(1)} %get-tuple-element.53), channel_id=1, source_target_pairs={{0,1},{1,2},{2,3},{3,0},{4,5},{5,6},{6,7},{7,4},{8,9},{9,10},{10,1... | collective-permute-start | bytes 221192 | tf_op jit(solution)/shard_map/ppermute | solution.py:30
  121.3 8.0 %collective-permute-start.18 = (bf16[96,384]{1,0:T(8,128)(2,1)S(1)}, bf16[96,384]{1,0:T(8,128)(2,1)S(1)}, u32[]{:S(2)}, u32[]{:S(2)}) collective-permute-start(bf16[96,384]{1,0:T(8,128)(2,1)S(1)} %get-tuple-element.53), channel_id=1, source_target_pairs={{0,3},{1,0},{2,1},{3,2},{4,7},{5,4},{6,5},{7,6},{8,11},{9,8},{10,9... | collective-permute-start | bytes 221192 | tf_op jit(solution)/shard_map/ppermute | solution.py:30
  129.3 2.7 %collective-permute-done.19 = bf16[96,384]{1,0:T(8,128)(2,1)S(1)} collective-permute-done((bf16[96,384]{1,0:T(8,128)(2,1)S(1)}, bf16[96,384]{1,0:T(8,128)(2,1)S(1)}, u32[]{:S(2)}, u32[]{:S(2)}) %collective-permute-start.19) | collective-permute-done | bytes 73760 | tf_op jit(solution)/shard_map/ppermute | solution.py:30
  131.9 1.9 collective-permute-start.25
  133.8 2.5 %collective-permute-done.20 = bf16[96,384]{1,0:T(8,128)(2,1)S(1)} collective-permute-done((bf16[96,384]{1,0:T(8,128)(2,1)S(1)}, bf16[96,384]{1,0:T(8,128)(2,1)S(1)}, u32[]{:S(2)}, u32[]{:S(2)}) %collective-permute-start.20) | collective-permute-done | bytes 73760 | tf_op jit(solution)/shard_map/ppermute | solution.py:30
  136.4 1.9 collective-permute-start.21
  139.0 2.2 collective-permute-start.28
  141.3 1.7 collective-permute-start.17
  143.6 1.6 collective-permute-done.22.refs_4_
  145.5 2.7 %collective-permute-start.24 = (bf16[2,96,384]{2,1,0:T(8,128)(2,1)S(1)}, bf16[2,96,384]{2,1,0:T(8,128)(2,1)S(1)}, u32[]{:S(2)}, u32[]{:S(2)}) collective-permute-start(bf16[2,96,384]{2,1,0:T(8,128)(2,1)S(1)} %slice.200), channel_id=1, source_target_pairs={{0,12},{1,13},{2,14},{3,15},{4,0},{5,1},{6,2},{7,3},{8,4},{9,5},{1... | collective-permute-start | bytes 442376 | tf_op jit(solution)/shard_map/ppermute | solution.py:30
  149.0 3.4 %collective-permute-start.31 = (bf16[2,96,384]{2,1,0:T(8,128)(2,1)S(1)}, bf16[2,96,384]{2,1,0:T(8,128)(2,1)S(1)}, u32[]{:S(2)}, u32[]{:S(2)}) collective-permute-start(bf16[2,96,384]{2,1,0:T(8,128)(2,1)S(1)} %slice.203), channel_id=1, source_target_pairs={{0,3},{1,0},{2,1},{3,2},{4,7},{5,4},{6,5},{7,6},{8,11},{9,8},{10,9... | collective-permute-start | bytes 442376 | tf_op jit(solution)/shard_map/ppermute | solution.py:30
  153.0 2.6 %collective-permute-done.23.refs_2_ = bf16[2,96,384]{2,1,0:T(8,128)(2,1)S(1)} collective-permute-done((bf16[2,96,384]{2,1,0:T(8,128)(2,1)S(1)}, bf16[2,96,384]{2,1,0:T(8,128)(2,1)S(1)}, u32[]{:S(2)}, u32[]{:S(2)}) %collective-permute-start.23) | collective-permute-done | bytes 147488 | tf_op jit(solution)/shard_map/ppermute | solution.py:30
  155.6 2.7 %collective-permute-done.30.refs_7_ = bf16[2,96,384]{2,1,0:T(8,128)(2,1)S(1)} collective-permute-done((bf16[2,96,384]{2,1,0:T(8,128)(2,1)S(1)}, bf16[2,96,384]{2,1,0:T(8,128)(2,1)S(1)}, u32[]{:S(2)}, u32[]{:S(2)}) %collective-permute-start.30) | collective-permute-done | bytes 147488 | tf_op jit(solution)/shard_map/ppermute | solution.py:30
  159.4 6.1 %shard_map.87 = (f32[768,128]{1,0:T(8,128)}, bf16[256,384]{1,0:T(8,128)(2,1)}) custom-call(s32[16]{0:T(128)} %multiply_add_fusion.1.slot_one, s32[16]{0:T(128)} %get-tuple-element.28.slot_two, bf16[4,96,384]{2,1,0:T(8,128)(2,1)} %copy-done.2, bf16[4,96,384]{2,1,0:T(8,128)(2,1)} %copy-done.10, bf16[2,96,384]{2,1,0:T(8,128)(2,1)} %copy-done.22, ...), custom_call_target="tpu_custom_call" | custom-call | tf_op jit(solution)/shard_map/pallas_call | solution.py:242
  165.5 4.8 %collective-permute-start.33 = (bf16[256,384]{1,0:T(8,128)(2,1)}, bf16[256,384]{1,0:T(8,128)(2,1)S(1)}, u32[]{:S(2)}, u32[]{:S(2)}) collective-permute-start(bf16[256,384]{1,0:T(8,128)(2,1)} %get-tuple-element.16.refs_0_), channel_id=1, source_target_pairs={{0,32},{1,33},{2,34},{3,35},{4,36},{5,37},{6,38},{7,39},{8,40},{9,... | collective-permute-start | bytes 589832 | tf_op jit(solution)/shard_map/ppermute | solution.py:30
  170.2 5.0 %collective-permute-done.33.refs_4_ = bf16[256,384]{1,0:T(8,128)(2,1)S(1)} collective-permute-done((bf16[256,384]{1,0:T(8,128)(2,1)}, bf16[256,384]{1,0:T(8,128)(2,1)S(1)}, u32[]{:S(2)}, u32[]{:S(2)}) %collective-permute-start.33) | collective-permute-done | bytes 196640 | tf_op jit(solution)/shard_map/ppermute | solution.py:30
  175.3 3.2 %collective-permute-start.34 = (bf16[128,384]{1,0:T(8,128)(2,1)S(1)}, bf16[128,384]{1,0:T(8,128)(2,1)S(1)}, u32[]{:S(2)}, u32[]{:S(2)}) collective-permute-start(bf16[128,384]{1,0:T(8,128)(2,1)S(1)} %slice.204), channel_id=1, source_target_pairs={{0,32},{1,33},{2,34},{3,35},{4,36},{5,37},{6,38},{7,39},{8,40},{9,... | collective-permute-start | bytes 294920 | tf_op jit(solution)/shard_map/ppermute | solution.py:30
  179.0 11.8 %collective-permute-start.36 = (bf16[256,384]{1,0:T(8,128)(2,1)}, bf16[256,384]{1,0:T(8,128)(2,1)S(1)}, u32[]{:S(2)}, u32[]{:S(2)}) collective-permute-start(bf16[256,384]{1,0:T(8,128)(2,1)} %get-tuple-element.16.refs_0_), channel_id=1, source_target_pairs={{0,16},{1,17},{2,18},{3,19},{4,20},{5,21},{6,22},{7,23},{8,24},{9,... | collective-permute-start | bytes 589832 | tf_op jit(solution)/shard_map/ppermute | solution.py:30
  191.3 2.0 collective-permute-start.38
  193.3 4.6 %collective-permute-start.39 = (bf16[128,384]{1,0:T(8,128)(2,1)S(1)}, bf16[128,384]{1,0:T(8,128)(2,1)S(1)}, u32[]{:S(2)}, u32[]{:S(2)}) collective-permute-start(bf16[128,384]{1,0:T(8,128)(2,1)S(1)} %collective-permute-done.35.refs_3_), channel_id=1, source_target_pairs={{0,16},{1,17},{2,18},{3,19},{4,20},{5,21},{6,22},{7,23},{8,24},{9,... | collective-permute-start | bytes 294920 | tf_op jit(solution)/shard_map/ppermute | solution.py:30
  198.5 2.4 %shard_map.86 = f32[2304,128]{1,0:T(8,128)} custom-call(bf16[768,384]{1,0:T(8,128)(2,1)} %get-tuple-element.14.mine_ref, bf16[768,384]{1,0:T(8,128)(2,1)} %copy-done.15), custom_call_target="tpu_custom_call" | custom-call | tf_op jit(solution)/shard_map/pallas_call | solution.py:242
  200.8 6.0 %shard_map.88.refs_10_ = f32[2,256,256]{2,1,0:T(8,128)} custom-call(s32[16]{0:T(128)} %copy-done.31, bf16[16,1536,128]{2,1,0:T(8,128)(2,1)} %bitcast.150, bf16[8,2304,128]{2,1,0:T(8,128)(2,1)} %bitcast.149), custom_call_target="tpu_custom_call" | custom-call | tf_op jit(solution)/shard_map/pallas_call | solution.py:242
  208.4 5.7 %shard_map.89 = f32[1024,128]{1,0:T(8,128)} custom-call(s32[16]{0:T(128)} %copy-done.31, s32[8]{0:T(128)} %fusion.part_slots, bf16[256,384]{1,0:T(8,128)(2,1)} %get-tuple-element.16.refs_0_, bf16[256,384]{1,0:T(8,128)(2,1)} %copy-done.17, bf16[128,384]{1,0:T(8,128)(2,1)} %copy-done.26, bf16[128,384]{1,0:T(8,128)(2,1)} %copy-done.27, ...), custom_call_target="tpu_custom_call" | custom-call | tf_op jit(solution)/shard_map/pallas_call | solution.py:242
  (206 shorter events, 22.3 us)
Async XLA Ops:
  7.2 98.6 %all-gather.5.cloned.1.call-start = ((), (), s32[]{:S(2)}) async-start(), calls=%async_computation | async-start | bytes 5308416 | tf_op jit(solution)/shard_map/all_gather | solution.py:275
  8.4 58.8 %copy-start.9 = (bf16[1,6,1,64,2,1,128]{6,4,5,3,2,1,0:T(2,128)(2,1)S(1)}, bf16[1,6,1,64,2,1,128]{6,4,5,3,2,1,0:T(2,128)(2,1)}, u32[]{:S(2)}) copy-start(bf16[1,6,1,64,2,1,128]{6,4,5,3,2,1,0:T(2,128)(2,1)} %param.10) | copy-start | bytes 589828
  12.3 77.5 %copy-start.30 = (s32[1,3072]{1,0:T(1,128)S(1)}, s32[1,3072]{1,0:T(1,128)}, u32[]{:S(2)}) copy-start(s32[1,3072]{1,0:T(1,128)} %param.11) | copy-start | bytes 36868
  13.4 187.4 %all-gather.7.cloned.1.call-start = ((), (), s32[]{:S(2)}) async-start(), calls=%async_computation.1 | async-start | bytes 6684672 | tf_op jit(solution)/shard_map/all_gather | solution.py:290
  13.6 15.1 %collective-permute-start = (bf16[768,128]{1,0:T(8,128)(2,1)S(1)}, bf16[768,128]{1,0:T(8,128)(2,1)S(1)}, u32[]{:S(2)}, u32[]{:S(2)}) collective-permute-start(bf16[768,128]{1,0:T(8,128)(2,1)S(1)} %constant_dynamic-update-slice_fusion), channel_id=1, source_target_pairs={{0,0},{1,17},{2,34},{3,51},{4,68},{5,85},{6,102},{7,119},{8,8},{9,... | collective-permute-start | bytes 589832 | tf_op jit(solution)/shard_map/ppermute | solution.py:30
  28.7 25.3 %collective-permute-start.2 = (bf16[384,128]{1,0:T(8,128)(2,1)S(1)}, bf16[384,128]{1,0:T(8,128)(2,1)S(1)}, u32[]{:S(2)}, u32[]{:S(2)}) collective-permute-start(bf16[384,128]{1,0:T(8,128)(2,1)S(1)} %get-tuple-element.49), channel_id=1, source_target_pairs={{0,1},{1,2},{2,3},{3,0},{4,5},{5,6},{6,7},{7,4},{8,9},{9,10},{10,1... | collective-permute-start | bytes 294920 | tf_op jit(solution)/shard_map/ppermute | solution.py:30
  29.6 29.2 %collective-permute-start.1 = (bf16[384,128]{1,0:T(8,128)(2,1)S(1)}, bf16[384,128]{1,0:T(8,128)(2,1)S(1)}, u32[]{:S(2)}, u32[]{:S(2)}) collective-permute-start(bf16[384,128]{1,0:T(8,128)(2,1)S(1)} %get-tuple-element.49), channel_id=1, source_target_pairs={{0,3},{1,0},{2,1},{3,2},{4,7},{5,4},{6,5},{7,6},{8,11},{9,8},{10,9... | collective-permute-start | bytes 294920 | tf_op jit(solution)/shard_map/ppermute | solution.py:30
  39.1 19.6 %collective-permute-start.9 = (bf16[384,128]{1,0:T(8,128)(2,1)S(1)}, bf16[384,128]{1,0:T(8,128)(2,1)S(1)}, u32[]{:S(2)}, u32[]{:S(2)}) collective-permute-start(bf16[384,128]{1,0:T(8,128)(2,1)S(1)} %get-tuple-element.48), channel_id=1, source_target_pairs={{0,4},{1,5},{2,6},{3,7},{4,8},{5,9},{6,10},{7,11},{8,12},{9,13},{1... | collective-permute-start | bytes 294920 | tf_op jit(solution)/shard_map/ppermute | solution.py:30
  54.0 5.1 %collective-permute-start.3 = (bf16[384,128]{1,0:T(8,128)(2,1)S(1)}, bf16[384,128]{1,0:T(8,128)(2,1)S(1)}, u32[]{:S(2)}, u32[]{:S(2)}) collective-permute-start(bf16[384,128]{1,0:T(8,128)(2,1)S(1)} %collective-permute-done.2), channel_id=1, source_target_pairs={{0,1},{1,2},{2,3},{3,0},{4,5},{5,6},{6,7},{7,4},{8,9},{9,10},{10,1... | collective-permute-start | bytes 294920 | tf_op jit(solution)/shard_map/ppermute | solution.py:30
  55.9 7.2 %collective-permute-start.8 = (bf16[384,128]{1,0:T(8,128)(2,1)S(1)}, bf16[384,128]{1,0:T(8,128)(2,1)S(1)}, u32[]{:S(2)}, u32[]{:S(2)}) collective-permute-start(bf16[384,128]{1,0:T(8,128)(2,1)S(1)} %get-tuple-element.48), channel_id=1, source_target_pairs={{0,12},{1,13},{2,14},{3,15},{4,0},{5,1},{6,2},{7,3},{8,4},{9,5},{1... | collective-permute-start | bytes 294920 | tf_op jit(solution)/shard_map/ppermute | solution.py:30
  58.7 5.1 %collective-permute-start.10 = (bf16[384,128]{1,0:T(8,128)(2,1)S(1)}, bf16[384,128]{1,0:T(8,128)(2,1)S(1)}, u32[]{:S(2)}, u32[]{:S(2)}) collective-permute-start(bf16[384,128]{1,0:T(8,128)(2,1)S(1)} %collective-permute-done.9), channel_id=1, source_target_pairs={{0,4},{1,5},{2,6},{3,7},{4,8},{5,9},{6,10},{7,11},{8,12},{9,13},{1... | collective-permute-start | bytes 294920 | tf_op jit(solution)/shard_map/ppermute | solution.py:30
  59.1 46.6 %copy-start = (bf16[4,384,128]{2,1,0:T(8,128)(2,1)}, bf16[4,384,128]{2,1,0:T(8,128)(2,1)S(1)}, u32[]{:S(2)}) copy-start(bf16[4,384,128]{2,1,0:T(8,128)(2,1)S(1)} %pad_maximum_fusion.refs_0_) | copy-start | bytes 1179652
  59.1 19.3 %collective-permute-start.4 = (bf16[4,384,128]{2,1,0:T(8,128)(2,1)S(1)}, bf16[4,384,128]{2,1,0:T(8,128)(2,1)S(1)}, u32[]{:S(2)}, u32[]{:S(2)}) collective-permute-start(bf16[4,384,128]{2,1,0:T(8,128)(2,1)S(1)} %pad_maximum_fusion.refs_0_), channel_id=1, source_target_pairs={{0,12},{1,13},{2,14},{3,15},{4,0},{5,1},{6,2},{7,3},{8,4},{9,5},{1... | collective-permute-start | bytes 1179656 | tf_op jit(solution)/shard_map/ppermute | solution.py:30
  63.1 9.6 %collective-permute-start.5 = (bf16[4,384,128]{2,1,0:T(8,128)(2,1)S(1)}, bf16[4,384,128]{2,1,0:T(8,128)(2,1)S(1)}, u32[]{:S(2)}, u32[]{:S(2)}) collective-permute-start(bf16[4,384,128]{2,1,0:T(8,128)(2,1)S(1)} %pad_maximum_fusion.refs_0_), channel_id=1, source_target_pairs={{0,4},{1,5},{2,6},{3,7},{4,8},{5,9},{6,10},{7,11},{8,12},{9,13},{1... | collective-permute-start | bytes 1179656 | tf_op jit(solution)/shard_map/ppermute | solution.py:30
  63.8 41.9 %copy-start.1 = (bf16[4,384,128]{2,1,0:T(8,128)(2,1)}, bf16[4,384,128]{2,1,0:T(8,128)(2,1)S(1)}, u32[]{:S(2)}) copy-start(bf16[4,384,128]{2,1,0:T(8,128)(2,1)S(1)} %pad_maximum_fusion.1.refs_5_) | copy-start | bytes 1179652
  63.9 15.0 %collective-permute-start.11 = (bf16[4,384,128]{2,1,0:T(8,128)(2,1)S(1)}, bf16[4,384,128]{2,1,0:T(8,128)(2,1)S(1)}, u32[]{:S(2)}, u32[]{:S(2)}) collective-permute-start(bf16[4,384,128]{2,1,0:T(8,128)(2,1)S(1)} %pad_maximum_fusion.1.refs_5_), channel_id=1, source_target_pairs={{0,3},{1,0},{2,1},{3,2},{4,7},{5,4},{6,5},{7,6},{8,11},{9,8},{10,9... | collective-permute-start | bytes 1179656 | tf_op jit(solution)/shard_map/ppermute | solution.py:30
  66.6 12.0 %collective-permute-start.12 = (bf16[4,384,128]{2,1,0:T(8,128)(2,1)S(1)}, bf16[4,384,128]{2,1,0:T(8,128)(2,1)S(1)}, u32[]{:S(2)}, u32[]{:S(2)}) collective-permute-start(bf16[4,384,128]{2,1,0:T(8,128)(2,1)S(1)} %pad_maximum_fusion.1.refs_5_), channel_id=1, source_target_pairs={{0,1},{1,2},{2,3},{3,0},{4,5},{5,6},{6,7},{7,4},{8,9},{9,10},{10,1... | collective-permute-start | bytes 1179656 | tf_op jit(solution)/shard_map/ppermute | solution.py:30
  68.1 16.7 %collective-permute-start.41 = (bf16[1536,128]{1,0:T(8,128)(2,1)}, bf16[1536,128]{1,0:T(8,128)(2,1)S(1)}, u32[]{:S(2)}, u32[]{:S(2)}) collective-permute-start(bf16[1536,128]{1,0:T(8,128)(2,1)} %constant_dynamic-update-slice_fusion.19), channel_id=1, source_target_pairs={{0,0},{1,17},{2,34},{3,51},{4,68},{5,85},{6,102},{7,119},{8,8},{9,... | collective-permute-start | bytes 1179656 | tf_op jit(solution)/shard_map/ppermute | solution.py:30
  72.7 14.0 %collective-permute-start.6 = (bf16[2,384,128]{2,1,0:T(8,128)(2,1)S(1)}, bf16[2,384,128]{2,1,0:T(8,128)(2,1)}, u32[]{:S(2)}, u32[]{:S(2)}) collective-permute-start(bf16[2,384,128]{2,1,0:T(8,128)(2,1)S(1)} %slice.179), channel_id=1, source_target_pairs={{0,4},{1,5},{2,6},{3,7},{4,8},{5,9},{6,10},{7,11},{8,12},{9,13},{1... | collective-permute-start | bytes 589832 | tf_op jit(solution)/shard_map/ppermute | solution.py:30
  78.5 8.2 %collective-permute-start.7 = (bf16[2,384,128]{2,1,0:T(8,128)(2,1)S(1)}, bf16[2,384,128]{2,1,0:T(8,128)(2,1)}, u32[]{:S(2)}, u32[]{:S(2)}) collective-permute-start(bf16[2,384,128]{2,1,0:T(8,128)(2,1)S(1)} %slice.180), channel_id=1, source_target_pairs={{0,12},{1,13},{2,14},{3,15},{4,0},{5,1},{6,2},{7,3},{8,4},{9,5},{1... | collective-permute-start | bytes 589832 | tf_op jit(solution)/shard_map/ppermute | solution.py:30
  78.6 9.5 %collective-permute-start.13 = (bf16[2,384,128]{2,1,0:T(8,128)(2,1)S(1)}, bf16[2,384,128]{2,1,0:T(8,128)(2,1)}, u32[]{:S(2)}, u32[]{:S(2)}) collective-permute-start(bf16[2,384,128]{2,1,0:T(8,128)(2,1)S(1)} %slice.182), channel_id=1, source_target_pairs={{0,1},{1,2},{2,3},{3,0},{4,5},{5,6},{6,7},{7,4},{8,9},{9,10},{10,1... | collective-permute-start | bytes 589832 | tf_op jit(solution)/shard_map/ppermute | solution.py:30
  78.9 10.9 %collective-permute-start.14 = (bf16[2,384,128]{2,1,0:T(8,128)(2,1)S(1)}, bf16[2,384,128]{2,1,0:T(8,128)(2,1)}, u32[]{:S(2)}, u32[]{:S(2)}) collective-permute-start(bf16[2,384,128]{2,1,0:T(8,128)(2,1)S(1)} %slice.183), channel_id=1, source_target_pairs={{0,3},{1,0},{2,1},{3,2},{4,7},{5,4},{6,5},{7,6},{8,11},{9,8},{10,9... | collective-permute-start | bytes 589832 | tf_op jit(solution)/shard_map/ppermute | solution.py:30
  91.5 12.9 %collective-permute-start.15 = (s32[576,1]{1,0:T(8,128)S(1)}, s32[576,1]{1,0:T(8,128)S(1)}, u32[]{:S(2)}, u32[]{:S(2)}) collective-permute-start(s32[576,1]{1,0:T(8,128)S(1)} %broadcast_in_dim.6), channel_id=1, source_target_pairs={{0,128},{1,129},{2,130},{3,131},{4,132},{5,133},{6,134},{7,135},{8... | collective-permute-start | bytes 6920 | tf_op jit(solution)/shard_map/ppermute | solution.py:30
  112.9 4.3 %collective-permute-start.16 = (bf16[192,384]{1,0:T(8,128)(2,1)}, bf16[192,384]{1,0:T(8,128)(2,1)S(1)}, u32[]{:S(2)}, u32[]{:S(2)}) collective-permute-start(bf16[192,384]{1,0:T(8,128)(2,1)} %get-tuple-element.13), channel_id=1, source_target_pairs={{0,128},{1,129},{2,130},{3,131},{4,132},{5,133},{6,134},{7,135},{8... | collective-permute-start | bytes 442376 | tf_op jit(solution)/shard_map/ppermute | solution.py:30
  118.2 13.8 %collective-permute-start.19 = (bf16[96,384]{1,0:T(8,128)(2,1)S(1)}, bf16[96,384]{1,0:T(8,128)(2,1)S(1)}, u32[]{:S(2)}, u32[]{:S(2)}) collective-permute-start(bf16[96,384]{1,0:T(8,128)(2,1)S(1)} %get-tuple-element.53), channel_id=1, source_target_pairs={{0,1},{1,2},{2,3},{3,0},{4,5},{5,6},{6,7},{7,4},{8,9},{9,10},{10,1... | collective-permute-start | bytes 221192 | tf_op jit(solution)/shard_map/ppermute | solution.py:30
  121.3 12.6 %collective-permute-start.26 = (bf16[96,384]{1,0:T(8,128)(2,1)S(1)}, bf16[96,384]{1,0:T(8,128)(2,1)S(1)}, u32[]{:S(2)}, u32[]{:S(2)}) collective-permute-start(bf16[96,384]{1,0:T(8,128)(2,1)S(1)} %get-tuple-element.52), channel_id=1, source_target_pairs={{0,4},{1,5},{2,6},{3,7},{4,8},{5,9},{6,10},{7,11},{8,12},{9,13},{1... | collective-permute-start | bytes 221192 | tf_op jit(solution)/shard_map/ppermute | solution.py:30
  121.3 12.6 %collective-permute-start.18 = (bf16[96,384]{1,0:T(8,128)(2,1)S(1)}, bf16[96,384]{1,0:T(8,128)(2,1)S(1)}, u32[]{:S(2)}, u32[]{:S(2)}) collective-permute-start(bf16[96,384]{1,0:T(8,128)(2,1)S(1)} %get-tuple-element.53), channel_id=1, source_target_pairs={{0,3},{1,0},{2,1},{3,2},{4,7},{5,4},{6,5},{7,6},{8,11},{9,8},{10,9... | collective-permute-start | bytes 221192 | tf_op jit(solution)/shard_map/ppermute | solution.py:30
  131.9 4.4 %collective-permute-start.20 = (bf16[96,384]{1,0:T(8,128)(2,1)S(1)}, bf16[96,384]{1,0:T(8,128)(2,1)S(1)}, u32[]{:S(2)}, u32[]{:S(2)}) collective-permute-start(bf16[96,384]{1,0:T(8,128)(2,1)S(1)} %collective-permute-done.19), channel_id=1, source_target_pairs={{0,1},{1,2},{2,3},{3,0},{4,5},{5,6},{6,7},{7,4},{8,9},{9,10},{10,1... | collective-permute-start | bytes 221192 | tf_op jit(solution)/shard_map/ppermute | solution.py:30
  131.9 6.4 %collective-permute-start.25 = (bf16[96,384]{1,0:T(8,128)(2,1)S(1)}, bf16[96,384]{1,0:T(8,128)(2,1)S(1)}, u32[]{:S(2)}, u32[]{:S(2)}) collective-permute-start(bf16[96,384]{1,0:T(8,128)(2,1)S(1)} %get-tuple-element.52), channel_id=1, source_target_pairs={{0,12},{1,13},{2,14},{3,15},{4,0},{5,1},{6,2},{7,3},{8,4},{9,5},{1... | collective-permute-start | bytes 221192 | tf_op jit(solution)/shard_map/ppermute | solution.py:30
  133.8 4.6 %collective-permute-start.27 = (bf16[96,384]{1,0:T(8,128)(2,1)S(1)}, bf16[96,384]{1,0:T(8,128)(2,1)S(1)}, u32[]{:S(2)}, u32[]{:S(2)}) collective-permute-start(bf16[96,384]{1,0:T(8,128)(2,1)S(1)} %collective-permute-done.26), channel_id=1, source_target_pairs={{0,4},{1,5},{2,6},{3,7},{4,8},{5,9},{6,10},{7,11},{8,12},{9,13},{1... | collective-permute-start | bytes 221192 | tf_op jit(solution)/shard_map/ppermute | solution.py:30
  136.4 9.1 %collective-permute-start.21 = (bf16[4,96,384]{2,1,0:T(8,128)(2,1)S(1)}, bf16[4,96,384]{2,1,0:T(8,128)(2,1)S(1)}, u32[]{:S(2)}, u32[]{:S(2)}) collective-permute-start(bf16[4,96,384]{2,1,0:T(8,128)(2,1)S(1)} %pad_maximum_fusion.2.refs_0_), channel_id=1, source_target_pairs={{0,12},{1,13},{2,14},{3,15},{4,0},{5,1},{6,2},{7,3},{8,4},{9,5},{1... | collective-permute-start | bytes 884744 | tf_op jit(solution)/shard_map/ppermute | solution.py:30
  138.4 6.8 %collective-permute-start.22 = (bf16[4,96,384]{2,1,0:T(8,128)(2,1)S(1)}, bf16[4,96,384]{2,1,0:T(8,128)(2,1)S(1)}, u32[]{:S(2)}, u32[]{:S(2)}) collective-permute-start(bf16[4,96,384]{2,1,0:T(8,128)(2,1)S(1)} %pad_maximum_fusion.2.refs_0_), channel_id=1, source_target_pairs={{0,4},{1,5},{2,6},{3,7},{4,8},{5,9},{6,10},{7,11},{8,12},{9,13},{1... | collective-permute-start | bytes 884744 | tf_op jit(solution)/shard_map/ppermute | solution.py:30
  138.4 9.8 %collective-permute-start.29 = (bf16[4,96,384]{2,1,0:T(8,128)(2,1)S(1)}, bf16[4,96,384]{2,1,0:T(8,128)(2,1)S(1)}, u32[]{:S(2)}, u32[]{:S(2)}) collective-permute-start(bf16[4,96,384]{2,1,0:T(8,128)(2,1)S(1)} %pad_maximum_fusion.3.refs_5_), channel_id=1, source_target_pairs={{0,1},{1,2},{2,3},{3,0},{4,5},{5,6},{6,7},{7,4},{8,9},{9,10},{10,1... | collective-permute-start | bytes 884744 | tf_op jit(solution)/shard_map/ppermute | solution.py:30
  139.0 9.9 %collective-permute-start.28 = (bf16[4,96,384]{2,1,0:T(8,128)(2,1)S(1)}, bf16[4,96,384]{2,1,0:T(8,128)(2,1)S(1)}, u32[]{:S(2)}, u32[]{:S(2)}) collective-permute-start(bf16[4,96,384]{2,1,0:T(8,128)(2,1)S(1)} %pad_maximum_fusion.3.refs_5_), channel_id=1, source_target_pairs={{0,3},{1,0},{2,1},{3,2},{4,7},{5,4},{6,5},{7,6},{8,11},{9,8},{10,9... | collective-permute-start | bytes 884744 | tf_op jit(solution)/shard_map/ppermute | solution.py:30
  141.3 49.5 %collective-permute-start.17 = (bf16[768,384]{1,0:T(8,128)(2,1)}, bf16[768,384]{1,0:T(8,128)(2,1)S(1)}, u32[]{:S(2)}, u32[]{:S(2)}) collective-permute-start(bf16[768,384]{1,0:T(8,128)(2,1)} %get-tuple-element.14.mine_ref), channel_id=1, source_target_pairs={{0,128},{1,129},{2,130},{3,131},{4,132},{5,133},{6,134},{7,135},{8... | collective-permute-start | bytes 1769480 | tf_op jit(solution)/shard_map/ppermute | solution.py:30
  145.2 10.4 %collective-permute-start.23 = (bf16[2,96,384]{2,1,0:T(8,128)(2,1)S(1)}, bf16[2,96,384]{2,1,0:T(8,128)(2,1)S(1)}, u32[]{:S(2)}, u32[]{:S(2)}) collective-permute-start(bf16[2,96,384]{2,1,0:T(8,128)(2,1)S(1)} %slice.199), channel_id=1, source_target_pairs={{0,4},{1,5},{2,6},{3,7},{4,8},{5,9},{6,10},{7,11},{8,12},{9,13},{1... | collective-permute-start | bytes 442376 | tf_op jit(solution)/shard_map/ppermute | solution.py:30
  145.5 10.0 %collective-permute-start.24 = (bf16[2,96,384]{2,1,0:T(8,128)(2,1)S(1)}, bf16[2,96,384]{2,1,0:T(8,128)(2,1)S(1)}, u32[]{:S(2)}, u32[]{:S(2)}) collective-permute-start(bf16[2,96,384]{2,1,0:T(8,128)(2,1)S(1)} %slice.200), channel_id=1, source_target_pairs={{0,12},{1,13},{2,14},{3,15},{4,0},{5,1},{6,2},{7,3},{8,4},{9,5},{1... | collective-permute-start | bytes 442376 | tf_op jit(solution)/shard_map/ppermute | solution.py:30
  148.3 10.0 %collective-permute-start.30 = (bf16[2,96,384]{2,1,0:T(8,128)(2,1)S(1)}, bf16[2,96,384]{2,1,0:T(8,128)(2,1)S(1)}, u32[]{:S(2)}, u32[]{:S(2)}) collective-permute-start(bf16[2,96,384]{2,1,0:T(8,128)(2,1)S(1)} %slice.202), channel_id=1, source_target_pairs={{0,1},{1,2},{2,3},{3,0},{4,5},{5,6},{6,7},{7,4},{8,9},{9,10},{10,1... | collective-permute-start | bytes 442376 | tf_op jit(solution)/shard_map/ppermute | solution.py:30
  149.0 9.7 %collective-permute-start.31 = (bf16[2,96,384]{2,1,0:T(8,128)(2,1)S(1)}, bf16[2,96,384]{2,1,0:T(8,128)(2,1)S(1)}, u32[]{:S(2)}, u32[]{:S(2)}) collective-permute-start(bf16[2,96,384]{2,1,0:T(8,128)(2,1)S(1)} %slice.203), channel_id=1, source_target_pairs={{0,3},{1,0},{2,1},{3,2},{4,7},{5,4},{6,5},{7,6},{8,11},{9,8},{10,9... | collective-permute-start | bytes 442376 | tf_op jit(solution)/shard_map/ppermute | solution.py:30
  165.5 9.8 %collective-permute-start.33 = (bf16[256,384]{1,0:T(8,128)(2,1)}, bf16[256,384]{1,0:T(8,128)(2,1)S(1)}, u32[]{:S(2)}, u32[]{:S(2)}) collective-permute-start(bf16[256,384]{1,0:T(8,128)(2,1)} %get-tuple-element.16.refs_0_), channel_id=1, source_target_pairs={{0,32},{1,33},{2,34},{3,35},{4,36},{5,37},{6,38},{7,39},{8,40},{9,... | collective-permute-start | bytes 589832 | tf_op jit(solution)/shard_map/ppermute | solution.py:30
  170.2 8.2 %collective-permute-start.32 = (bf16[256,384]{1,0:T(8,128)(2,1)}, bf16[256,384]{1,0:T(8,128)(2,1)S(1)}, u32[]{:S(2)}, u32[]{:S(2)}) collective-permute-start(bf16[256,384]{1,0:T(8,128)(2,1)} %get-tuple-element.16.refs_0_), channel_id=1, source_target_pairs={{0,96},{1,97},{2,98},{3,99},{4,100},{5,101},{6,102},{7,103},{8,104... | collective-permute-start | bytes 589832 | tf_op jit(solution)/shard_map/ppermute | solution.py:30
  175.3 16.0 %collective-permute-start.34 = (bf16[128,384]{1,0:T(8,128)(2,1)S(1)}, bf16[128,384]{1,0:T(8,128)(2,1)S(1)}, u32[]{:S(2)}, u32[]{:S(2)}) collective-permute-start(bf16[128,384]{1,0:T(8,128)(2,1)S(1)} %slice.204), channel_id=1, source_target_pairs={{0,32},{1,33},{2,34},{3,35},{4,36},{5,37},{6,38},{7,39},{8,40},{9,... | collective-permute-start | bytes 294920 | tf_op jit(solution)/shard_map/ppermute | solution.py:30
  178.5 14.8 %collective-permute-start.35 = (bf16[128,384]{1,0:T(8,128)(2,1)S(1)}, bf16[128,384]{1,0:T(8,128)(2,1)S(1)}, u32[]{:S(2)}, u32[]{:S(2)}) collective-permute-start(bf16[128,384]{1,0:T(8,128)(2,1)S(1)} %slice.205), channel_id=1, source_target_pairs={{0,96},{1,97},{2,98},{3,99},{4,100},{5,101},{6,102},{7,103},{8,104... | collective-permute-start | bytes 294920 | tf_op jit(solution)/shard_map/ppermute | solution.py:30
  179.0 27.8 %collective-permute-start.36 = (bf16[256,384]{1,0:T(8,128)(2,1)}, bf16[256,384]{1,0:T(8,128)(2,1)S(1)}, u32[]{:S(2)}, u32[]{:S(2)}) collective-permute-start(bf16[256,384]{1,0:T(8,128)(2,1)} %get-tuple-element.16.refs_0_), channel_id=1, source_target_pairs={{0,16},{1,17},{2,18},{3,19},{4,20},{5,21},{6,22},{7,23},{8,24},{9,... | collective-permute-start | bytes 589832 | tf_op jit(solution)/shard_map/ppermute | solution.py:30
  190.8 16.1 %collective-permute-start.37 = (bf16[256,384]{1,0:T(8,128)(2,1)S(1)}, bf16[256,384]{1,0:T(8,128)(2,1)S(1)}, u32[]{:S(2)}, u32[]{:S(2)}) collective-permute-start(bf16[256,384]{1,0:T(8,128)(2,1)S(1)} %collective-permute-done.32.refs_1_), channel_id=1, source_target_pairs={{0,16},{1,17},{2,18},{3,19},{4,20},{5,21},{6,22},{7,23},{8,24},{9,... | collective-permute-start | bytes 589832 | tf_op jit(solution)/shard_map/ppermute | solution.py:30
  190.8 16.1 %collective-permute-start.40 = (bf16[256,384]{1,0:T(8,128)(2,1)S(1)}, bf16[256,384]{1,0:T(8,128)(2,1)S(1)}, u32[]{:S(2)}, u32[]{:S(2)}) collective-permute-start(bf16[256,384]{1,0:T(8,128)(2,1)S(1)} %collective-permute-done.33.refs_4_), channel_id=1, source_target_pairs={{0,16},{1,17},{2,18},{3,19},{4,20},{5,21},{6,22},{7,23},{8,24},{9,... | collective-permute-start | bytes 589832 | tf_op jit(solution)/shard_map/ppermute | solution.py:30
  191.3 15.6 %collective-permute-start.38 = (bf16[128,384]{1,0:T(8,128)(2,1)S(1)}, bf16[128,384]{1,0:T(8,128)(2,1)S(1)}, u32[]{:S(2)}, u32[]{:S(2)}) collective-permute-start(bf16[128,384]{1,0:T(8,128)(2,1)S(1)} %collective-permute-done.34.refs_2_), channel_id=1, source_target_pairs={{0,16},{1,17},{2,18},{3,19},{4,20},{5,21},{6,22},{7,23},{8,24},{9,... | collective-permute-start | bytes 294920 | tf_op jit(solution)/shard_map/ppermute | solution.py:30
  193.3 13.6 %collective-permute-start.39 = (bf16[128,384]{1,0:T(8,128)(2,1)S(1)}, bf16[128,384]{1,0:T(8,128)(2,1)S(1)}, u32[]{:S(2)}, u32[]{:S(2)}) collective-permute-start(bf16[128,384]{1,0:T(8,128)(2,1)S(1)} %collective-permute-done.35.refs_3_), channel_id=1, source_target_pairs={{0,16},{1,17},{2,18},{3,19},{4,20},{5,21},{6,22},{7,23},{8,24},{9,... | collective-permute-start | bytes 294920 | tf_op jit(solution)/shard_map/ppermute | solution.py:30
  (28 other events, 351.1 us)
Sparse Core Ops, SparseCore 0:
  13.5 62.2 all-gather.4
  89.9 88.4 all-gather.6
